TPU v7x, 256 devices: a whole 4x4x8 slice. The times are simulated.
256 devices in a mesh: grp: 2 (over x_lo), tile: 32 (over y, z), mem: 4 (over x_hi, core).
Axes of the slice: x: 4 (x_hi: 2, x_lo: 2; x = x_hi * 2 + x_lo), y: 4, z: 8, core: 2. Of those that a mesh axis runs over, the one named last changes fastest.
Arguments:
- current_state: float32 [512, 2, 65536], P(('grp', 'mem'), None, 'tile'), may hold values from -6 to 6
- lagged_states: float32 [3, 32, 8, 512, 512], P(None, 'tile', ('grp', 'mem')), may hold values from -6 to 6
- water_depth: float32 [65536], P('tile'), may hold values from 0.4 to 1
- obs_cells: int32 [32768], replicated, may hold values from 0 to 65535, as said below
- obs_values: float32 [32768], replicated, may hold values from -6 to 6
- obs_errors: float32 [32768], replicated, may hold values from 0.5 to 2
- tile_obs: int32 [32, 8, 1024], P('tile', ('grp', 'mem')), may hold values from -1 to 32767, as said below
Outputs:
- analysis_state: float32 [512, 2, 65536], P(('grp', 'mem'), None, 'tile')
- smoothed_lags: float32 [3, 32, 8, 512, 512], P(None, 'tile', ('grp', 'mem'))
Inputs may be any that keep to these rules, and one draw needn't show every extreme that they name: `obs_cells`: observation o lies in grid tile o // 1024, that is at a cell from (o // 1024) * 2048 to that plus 2048 - 1. `tile_obs`: each list holds distinct indices of observations in its own grid tile or the two beside it (periodically), used slots first and -1 after them; at least 256 slots are used in every list, all 1024 in some list.
All inputs are finite; a program needn't handle non-finite values. Where the computation divides by a largest or mean magnitude, that divisor is 1e-20 or more.
Results may differ from a plain program's by a relative error of at most 0.0003.
Values sent between devices are 32-bit elements; how exact they have to be, the bound alone decides.
No kernel may reach another device: no remote copies, remote signals or barrier semaphores. Data moves between devices by JAX's collectives and lax.ppermute only.
A program may use at most 64 MiB of HBM per device.

v0:
```python
import math

import jax
import jax.numpy as jnp
from jax import lax
from jax.sharding import PartitionSpec as P

OBS_DEV = 1024
ITERS = 6
MODEL_STEPS = 2
LOC = 512


flux_scale = 0.9
wave_scale = 0.9
highest = lax.Precision.HIGHEST


def shifted(array, axis, by):
    peers = lax.axis_size(axis)
    return lax.ppermute(array, axis, [(i, (i + by) % peers) for i in range(peers)])


def with_halo(block, sides, width):
    for axis, dim in sides:
        count = lax.axis_size(axis)
        forward = [(i, i + 1) for i in range(count - 1)]
        forward.append((count - 1, 0))
        backward = [(target, source) for source, target in forward]
        low = lax.ppermute(
            lax.slice_in_dim(block, block.shape[dim] - width, None, axis=dim), axis, forward
        )
        high = lax.ppermute(lax.slice_in_dim(block, 0, width, axis=dim), axis, backward)
        block = jnp.concatenate([low, block, high], axis=dim)
    return block


def copy_for_each(array, axis):
    copies = jnp.broadcast_to(array, (lax.axis_size(axis), *array.shape))
    return lax.all_to_all(copies, axis, split_axis=0, concat_axis=0, tiled=True)


def laid_out(tiles, dim):
    shape = list(tiles.shape[1:])
    shape[dim] *= tiles.shape[0]
    return jnp.moveaxis(tiles, 0, dim).reshape(shape)


def gather_directly(array, axis, dim):
    tiles = copy_for_each(array, axis)
    return laid_out(tiles, dim)


def advance(free_elevation, fluid_speed, water_depth):
    for repeat in range(MODEL_STEPS):
        velocity_left = shifted(fluid_speed[:, -1], "tile", 1)
        previous = jnp.concatenate([velocity_left[:, None], fluid_speed[:, :-1]], axis=1)
        free_elevation = free_elevation - flux_scale * water_depth * (fluid_speed - previous)
        height_right = shifted(free_elevation[:, 0], "tile", -1)
        following = jnp.concatenate([free_elevation[:, 1:], height_right[:, None]], axis=1)
        fluid_speed = fluid_speed - wave_scale * (following - free_elevation)
    return (free_elevation, fluid_speed)


def inverse_root(matrix, members):
    row_bound = jnp.max(jnp.sum(jnp.abs(matrix), axis=1))
    identity = jnp.eye(members, dtype=jnp.float32)

    def newton_step(repeat, carry):
        approx, root_inv = carry
        middle = 1.5 * identity - 0.5 * jnp.dot(root_inv, approx, precision=highest)
        return (
            jnp.dot(approx, middle, precision=highest),
            jnp.dot(middle, root_inv, precision=highest),
        )

    approx, root_inv = lax.fori_loop(0, ITERS, newton_step, (matrix / row_bound, identity))
    return root_inv / jnp.sqrt(row_bound)


def apply_transform(transform, states):
    state_mean = jnp.mean(states, axis=-2, keepdims=True)
    moved = jnp.einsum("ij,...iv->...jv", transform, states - state_mean, precision=highest)
    return state_mean + moved


def analyse_rows(
    patch_field_slab,
    lag_block,
    predicted_rows,
    obs_level,
    obs_spread,
    obs_sites,
    usable,
    center,
    cell_total,
):
    members = predicted_rows.shape[1]
    mean_obs = jnp.mean(predicted_rows, axis=1)
    spread_rows = predicted_rows - mean_obs[:, None]
    departure = obs_level - mean_obs
    distance = jnp.abs(obs_sites - center)
    distance = jnp.minimum(distance, cell_total - distance).astype(jnp.float32)
    weight = jnp.exp(-0.5 * (distance / LOC) ** 2) / (obs_spread * obs_spread)
    weight = jnp.where(usable, weight, jnp.zeros_like(weight))
    identity = jnp.eye(members, dtype=jnp.float32)
    weighted_rows = spread_rows * weight[:, None]
    product = lax.dot_general(
        weighted_rows, spread_rows, (((0,), (0,)), ((), ())), precision=highest
    )
    precision_matrix = (members - 1) * identity + product
    root_cover = inverse_root(precision_matrix, members)
    covariance = jnp.dot(root_cover, root_cover, precision=highest)
    innovation = jnp.dot(weight * departure, spread_rows, precision=highest)
    mean_weight = jnp.dot(covariance, innovation, precision=highest)
    transform = math.sqrt(members - 1) * root_cover + mean_weight[:, None]
    return (apply_transform(transform, patch_field_slab), apply_transform(transform, lag_block))


def per_device(
    current_state, lagged_states, water_depth, obs_cells, obs_values, obs_errors, tile_obs
):
    trial_slab_lines = current_state.shape[0]
    cells_dev = current_state.shape[2]
    group_size = lax.axis_size("grp")
    member_size = lax.axis_size("mem")
    trial_bundles = group_size * member_size
    tile_count = lax.axis_size("tile")
    tile_index = lax.axis_index("tile")
    part_index = lax.axis_index("grp") * member_size + lax.axis_index("mem")
    cell_total = cells_dev * tile_count
    obs_total = obs_values.shape[0]
    patch_point_number = cells_dev // trial_bundles
    members = trial_slab_lines * trial_bundles
    free_elevation, fluid_speed = advance(current_state[:, 0], current_state[:, 1], water_depth)
    prior_fields = jnp.stack([free_elevation, fluid_speed], axis=1)
    local_cells = (
        lax.dynamic_slice_in_dim(obs_cells, tile_index * OBS_DEV, OBS_DEV) - tile_index * cells_dev
    )
    obs_block = jnp.take(free_elevation.T, local_cells, axis=0, mode="clip")
    regrouped = lax.all_to_all(
        prior_fields.reshape(1, trial_slab_lines, 2, trial_bundles, patch_point_number),
        ("grp", "mem"),
        split_axis=3,
        concat_axis=0,
        tiled=True,
    )
    patch_field_slab = regrouped.reshape(members, 2 * patch_point_number)
    rows_here = tile_obs[0, 0]
    nearby = with_halo(obs_block, (("tile", 0),), OBS_DEV)
    row_lists = gather_directly(tile_obs, ("grp", "mem"), 1)[0]
    relative = (jnp.maximum(row_lists, 0) - (tile_index - 1) * OBS_DEV) % obs_total
    relative = jnp.where(row_lists >= 0, relative, 0)
    picked = jnp.take(nearby, relative.reshape(-1), axis=0, mode="clip")
    picked = picked.reshape(trial_bundles, rows_here.shape[0], trial_slab_lines)
    arrived = lax.all_to_all(picked, ("grp", "mem"), split_axis=0, concat_axis=2, tiled=True)
    predicted_rows = arrived.reshape(rows_here.shape[0], members)
    usable = rows_here >= 0
    clamped = jnp.maximum(rows_here, 0)
    center = tile_index * cells_dev + part_index * patch_point_number + patch_point_number // 2
    analysis, older = analyse_rows(
        patch_field_slab,
        lagged_states[:, 0, 0],
        predicted_rows,
        obs_values[clamped],
        obs_errors[clamped],
        obs_cells[clamped],
        usable,
        center,
        cell_total,
    )
    returned = lax.all_to_all(
        analysis.reshape(trial_bundles, trial_slab_lines, 2, 1, patch_point_number),
        ("grp", "mem"),
        split_axis=0,
        concat_axis=3,
        tiled=True,
    )
    analysis_state = returned.reshape(trial_slab_lines, 2, cells_dev)
    older_out = older[:, None, None]
    return (analysis_state, older_out)


def solution(mesh):
    placed = (
        P(("grp", "mem"), None, "tile"),
        P(None, "tile", ("grp", "mem"), None, None),
        P("tile"),
        P(),
        P(),
        P(),
        P("tile", ("grp", "mem"), None),
    )
    return jax.shard_map(
        per_device,
        mesh=mesh,
        in_specs=placed,
        out_specs=(P(("grp", "mem"), None, "tile"), P(None, "tile", ("grp", "mem"), None, None)),
        check_vma=False,
    )
```

profile of v0, /device:TPU:1, one launch (start us, length us, event | category | flops | bytes accessed | tf_op | source)
XLA Modules:
  0.0 191.5 jit_solution(4187576779033363363)
XLA Ops:
  0.7 3.4 %fusion.59 = (f32[64,1,2048]{2,1,0:T(1,128)}, f32[64,1,2048]{2,1,0:T(1,128)S(1)}) fusion(f32[64,2,2048]{2,1,0:T(2,128)} %param.9), kind=kLoop, calls=%fused_computation.112 | loop fusion | bytes 2097152 | tf_op jit(solution)/shard_map/slice | solution.py:135
  4.6 2.5 %collective-permute-start = (f32[64]{0:T(128)S(1)}, f32[64]{0:T(128)S(1)}, u32[]{:S(2)}, u32[]{:S(2)}) collective-permute-start(f32[64]{0:T(128)S(1)} %slice_bitcast_fusion.4), channel_id=1, source_target_pairs={{0,4},{4,8},{8,12},{12,16},{16,20},{20,24},{24,28},{28,32},{32,36}... | collective-permute-start | bytes 776 | tf_op jit(solution)/shard_map/ppermute | solution.py:21
  7.1 0.6 broadcast_in_dim.43
  7.8 5.3 %all-to-all-start.1 = ((s32[8,1,1,1024]{3,2,1,0:T(1,128)}), s32[8,1,1,1024]{3,2,1,0:T(1,128)S(1)}, u32[]{:S(2)}, u32[]{:S(2)}) async-start(s32[8,1,1,1024]{3,2,1,0:T(1,128)} %broadcast_in_dim.43), calls=%async_computation.1 | async-start | bytes 65536 | tf_op jit(solution)/shard_map/all_to_all | solution.py:40
  13.0 1.1 slice_bitcast_fusion.7
  14.2 1.4 copy.49
  15.9 6.2 %collective-permute-start.1 = (f32[64]{0:T(128)S(1)}, f32[64]{0:T(128)S(1)}, u32[]{:S(2)}, u32[]{:S(2)}) collective-permute-start(f32[64]{0:T(128)S(1)} %slice_bitcast_fusion.3), channel_id=1, source_target_pairs={{0,124},{4,0},{8,4},{12,8},{16,12},{20,16},{24,20},{28,24},{32,28}... | collective-permute-start | bytes 776 | tf_op jit(solution)/shard_map/ppermute | solution.py:21
  22.1 1.1 slice_bitcast_fusion.6
  23.6 1.1 slice_bitcast_fusion.5
  24.7 4.6 %collective-permute-done.2 = f32[64]{0:T(128)S(1)} collective-permute-done((f32[64]{0:T(128)S(1)}, f32[64]{0:T(128)S(1)}, u32[]{:S(2)}, u32[]{:S(2)}) %collective-permute-start.2) | collective-permute-done | bytes 288 | tf_op jit(solution)/shard_map/ppermute | solution.py:21
  29.7 1.4 collective-permute-start.3
  31.0 1.1 slice_bitcast_fusion
  32.1 4.0 %gather_fusion = f32[1024,64]{1,0:T(8,128)} fusion(f32[2048,64]{1,0:T(8,128)S(1)} %bitcast.115, s32[1024]{0:T(1024)S(1)} %subtract_clamp_fusion), kind=kCustom, calls=%fused_computation | custom fusion | bytes 528384 | tf_op jit(solution)/shard_map/jit(_take)/gather | solution.py:140
  36.3 1.3 collective-permute-start.4
  37.6 3.8 %fusion.18 = (f32[64,1,2048]{0,2,1:T(8,128)}, f32[64,1,2048]{0,2,1:T(8,128)S(1)}) fusion(f32[64,1,1]{0,2,1:T(1,128)S(1)} %bitcast.145, f32[64,1,2047]{0,2,1:T(8,128)} %slice_bitcast_fusion, f32[64,1,2048]{0,2,1:T(8,128)S(1)} %copy.50, f32[64,1,1]{0,2,1:T(1,128)S(1)} %bitcast.141, f32[64,1,2047]{0,2,1:T(8,128)} %get-tuple-element.69, ...), kind=kLoop, calls=%fused_computation.41 | loop fusion | flops 2097152 | bytes 4202496 | tf_op jit(solution)/shard_map/sub | solution.py:61
  41.4 1.5 copy.38
  43.4 1.9 pad_maximum_fusion.1
  45.3 7.9 %all-to-all-start = ((f32[1,64,2,8,256]{4,2,1,0,3:T(2,128)}), f32[1,64,2,8,256]{4,2,1,0,3:T(2,128)S(1)}, u32[]{:S(2)}, u32[]{:S(2)}) async-start(f32[1,64,2,8,256]{4,2,1,0,3:T(2,128)} %pad_maximum_fusion.1), calls=%async_computation | async-start | bytes 2097152 | tf_op jit(solution)/shard_map/all_to_all | solution.py:141
  53.6 1.3 pad_maximum_fusion
  54.9 27.9 %gather_fusion.1 = f32[8192,64]{1,0:T(8,128)} fusion(f32[3072,64]{1,0:T(8,128)S(1)} %pad_maximum_fusion, s32[8192]{0:T(1024)S(1)} %broadcast_clamp_fusion), kind=kCustom, calls=%fused_computation.1 | custom fusion | bytes 4227072 | tf_op jit(solution)/shard_map/jit(_take)/gather | solution.py:154
  82.7 3.8 %copy.39 = f32[8,1024,64]{1,2,0:T(8,128)} copy(f32[8,1024,64]{2,1,0:T(8,128)} %bitcast.120) | data formatting | bytes 4194304 | tf_op jit(solution)/shard_map/reshape | solution.py:155
  86.5 5.2 %all-to-all-start.2 = ((f32[8,1024,64]{1,2,0:T(8,128)}), f32[8,1024,64]{1,2,0:T(8,128)}, u32[]{:S(2)}, u32[]{:S(2)}) async-start(f32[8,1024,64]{1,2,0:T(8,128)} %copy.39), calls=%async_computation.2 | async-start | bytes 4194304 | tf_op jit(solution)/shard_map/all_to_all | solution.py:156
  91.7 6.2 %gather_fusion.2 = s32[1024]{0:T(1024)S(1)} fusion(s32[32768]{0:T(1024)S(1)} %copy-done.1, s32[1024]{0:T(1024)S(1)} %broadcast_clamp_fusion.1), kind=kCustom, calls=%fused_computation.2 | custom fusion | bytes 12288 | tf_op jit(solution)/shard_map/gather | solution.py:167
  97.9 6.2 %gather_fusion.3 = f32[1024]{0:T(1024)S(1)} fusion(f32[32768]{0:T(1024)S(1)} %copy-done, s32[1024]{0:T(1024)S(1)} %broadcast_clamp_fusion.1), kind=kCustom, calls=%fused_computation.3 | custom fusion | bytes 12288 | tf_op jit(solution)/shard_map/gather | solution.py:166
  104.1 6.2 %gather_fusion.4 = f32[1024]{0:T(1024)S(1)} fusion(f32[32768]{0:T(1024)S(1)} %copy-done.2, s32[1024]{0:T(1024)S(1)} %broadcast_clamp_fusion.1), kind=kCustom, calls=%fused_computation.4 | custom fusion | bytes 12288 | tf_op jit(solution)/shard_map/gather | solution.py:165
  110.2 1.1 fusion.21
  111.3 1.6 copy.40
  112.9 1.0 copy.52
  114.5 2.1 %all-to-all-done.2 = f32[8,1024,64]{1,2,0:T(8,128)} async-done(((f32[8,1024,64]{1,2,0:T(8,128)}), f32[8,1024,64]{1,2,0:T(8,128)}, u32[]{:S(2)}, u32[]{:S(2)}) %all-to-all-start.2) | async-done | bytes 2097184 | tf_op jit(solution)/shard_map/all_to_all | solution.py:156
  116.6 1.7 reduce_sum.37
  118.4 2.1 %bitcast_multiply_fusion = (f32[1,1024,8,64]{1,3,2,0:T(8,128)S(1)}, f32[8,1,1024,64]{2,3,0,1:T(8,128)S(1)}) fusion(f32[1024]{0:T(1024)S(1)} %get-tuple-element.61, f32[1024]{0:T(1024)S(1)} %get-tuple-element.75, f32[8,1024,64]{1,2,0:T(8,128)} %all-to-all-done.2), kind=kLoop, calls=%fused_computation.13 | loop fusion | flops 1048576 | bytes 6299648 | tf_op jit(solution)/shard_map/mul | solution.py:107
  120.5 3.6 %abs_reduce_fusion = (f32[512]{0:T(512)S(1)}, f32[512,512]{0,1:T(8,128)S(1)}) fusion(f32[1024,512]{0,1:T(8,128)S(1)} %bitcast.122, f32[1024,512]{0,1:T(8,128)S(1)} %bitcast.118), kind=kOutput, calls=%fused_computation.47 | convolution fusion | flops 3222535680 | bytes 5244928 | tf_op jit(solution)/shard_map/dot_general | solution.py:108
  124.1 0.7 reduce_max.9
  125.5 0.8 broadcast_divide_fusion.1
  126.3 34.7 %while.13 = (s32[]{:T(128)}, f32[512,512]{0,1:T(8,128)S(1)}, f32[512,512]{1,0:T(8,128)S(1)}, s32[]{:T(128)}) while((s32[]{:T(128)}, f32[512,512]{0,1:T(8,128)S(1)}, f32[512,512]{1,0:T(8,128)S(1)}, s32[]{:T(128)}) %tuple.43), condition=%wide.region_5.6_spmd.clone, body=%wide.region_4.5_spmd.clone.sunk | while | flops 4832886784 | bytes 13631541 | solution.py:77
  126.5 1.9 fusion.87
  128.4 1.8 convolution_bitcast_fusion.3
  130.2 1.8 fusion.88
  132.3 1.9 fusion.87
  134.1 1.8 convolution_bitcast_fusion.3
  136.0 1.8 fusion.88
  138.0 1.9 fusion.87
  139.9 1.8 convolution_bitcast_fusion.3
  141.7 1.8 fusion.88
  143.8 1.9 fusion.87
  145.6 1.8 convolution_bitcast_fusion.3
  147.5 1.8 fusion.88
  149.5 1.9 fusion.87
  151.4 1.9 convolution_bitcast_fusion.3
  153.2 1.8 fusion.88
  155.3 1.9 fusion.87
  157.1 1.8 convolution_bitcast_fusion.3
  159.0 1.8 fusion.88
  161.1 1.9 fusion.57
  163.0 1.8 convolution_bitcast_fusion.1
  164.8 1.0 fusion.61
  165.8 2.0 %convolution_add_fusion = f32[512,512]{1,0:T(8,128)S(1)} fusion(f32[512,512]{1,0:T(8,128)S(1)} %bitcast.126, f32[512]{0:T(512)S(1)} %bitcast.136, f32[512]{0:T(512)S(1)} %bitcast.144, f32[512,512]{1,0:T(8,128)S(1)} %get-tuple-element.24, f32[]{:T(128)S(6)} %sqrt.3), kind=kOutput, calls=%fused_computation.17 | convolution fusion | flops 1611923456 | bytes 3149828 | tf_op jit(solution)/shard_map/ij,...iv->...jv/dot_general | solution.py:83
  167.9 1.6 reshape.278
  169.5 5.5 %all-to-all-start.3 = ((f32[8,64,2,1,256]{4,2,1,3,0:T(2,128)}), f32[8,64,2,1,256]{4,2,1,3,0:T(2,128)S(1)}, u32[]{:S(2)}, u32[]{:S(2)}) async-start(f32[8,64,2,1,256]{4,2,1,3,0:T(2,128)} %bitcast.42), calls=%async_computation.3 | async-start | bytes 2097152 | tf_op jit(solution)/shard_map/all_to_all | solution.py:172
  175.1 2.1 %reduce_sum.39 = f32[3,512]{1,0:T(4,128)S(1)} reduce(f32[3,1,1,512,512]{4,3,2,1,0:T(8,128)} %param.10, f32[]{:T(128)} %constant.20.clone.1), dimensions={1,2,3}, to_apply=%region_6.7 | reduce | flops 784896 | bytes 3151876 | tf_op jit(solution)/shard_map/reduce_sum | solution.py:82
  177.2 8.6 %add_bitcast_fusion = f32[3,1,1,512,512]{3,4,0,2,1:T(8,128)} fusion(f32[3,1,1,512,512]{4,3,2,1,0:T(8,128)} %param.10, f32[3,512]{1,0:T(4,128)S(1)} %broadcast_multiply_fusion, f32[512]{0:T(512)S(1)} %bitcast.137, f32[512,512]{1,0:T(8,128)S(1)} %get-tuple-element.24, f32[]{:T(128)S(6)} %sqrt.3), kind=kOutput, calls=%fused_computation.12 | convolution fusion | flops 4834197504 | bytes 7348228 | tf_op jit(solution)/shard_map/ij,...iv->...jv/dot_general | solution.py:83
  185.7 3.5 %copy.45 = f32[3,1,1,512,512]{4,3,2,1,0:T(8,128)} copy(f32[3,1,1,512,512]{3,4,0,2,1:T(8,128)} %add_bitcast_fusion) | data formatting | bytes 6291456
  189.3 0.6 copy.47
  189.9 1.6 reshape.329
  (63 shorter events, 3.9 us)
Async XLA Ops:
  0.6 97.2 %copy-start = (f32[32768]{0:T(1024)S(1)}, f32[32768]{0:T(1024)}, u32[]{:S(2)}) copy-start(f32[32768]{0:T(1024)} %param.14) | copy-start | bytes 393220
  0.6 6.5 %copy-start.7 = (s32[1,1,1024]{2,1,0:T(1,128)S(1)}, s32[1,1,1024]{2,1,0:T(1,128)}, u32[]{:S(2)}) copy-start(s32[1,1,1024]{2,1,0:T(1,128)} %param.15) | copy-start | bytes 12292
  4.1 10.0 %copy-start.8 = (f32[2048]{0:T(1024)S(1)}, f32[2048]{0:T(1024)}, u32[]{:S(2)}) copy-start(f32[2048]{0:T(1024)} %param.11) | copy-start | bytes 24580
  4.1 10.0 %copy-start.1 = (s32[32768]{0:T(1024)S(1)}, s32[32768]{0:T(1024)}, u32[]{:S(2)}) copy-start(s32[32768]{0:T(1024)} %param.12) | copy-start | bytes 393220
  4.6 11.0 %collective-permute-start = (f32[64]{0:T(128)S(1)}, f32[64]{0:T(128)S(1)}, u32[]{:S(2)}, u32[]{:S(2)}) collective-permute-start(f32[64]{0:T(128)S(1)} %slice_bitcast_fusion.4), channel_id=1, source_target_pairs={{0,4},{4,8},{8,12},{12,16},{16,20},{20,24},{24,28},{28,32},{32,36}... | collective-permute-start | bytes 776 | tf_op jit(solution)/shard_map/ppermute | solution.py:21
  7.8 37.6 %all-to-all-start.1 = ((s32[8,1,1,1024]{3,2,1,0:T(1,128)}), s32[8,1,1,1024]{3,2,1,0:T(1,128)S(1)}, u32[]{:S(2)}, u32[]{:S(2)}) async-start(s32[8,1,1,1024]{3,2,1,0:T(1,128)} %broadcast_in_dim.43), calls=%async_computation.1 | async-start | bytes 65536 | tf_op jit(solution)/shard_map/all_to_all | solution.py:40
  15.9 7.3 %collective-permute-start.1 = (f32[64]{0:T(128)S(1)}, f32[64]{0:T(128)S(1)}, u32[]{:S(2)}, u32[]{:S(2)}) collective-permute-start(f32[64]{0:T(128)S(1)} %slice_bitcast_fusion.3), channel_id=1, source_target_pairs={{0,124},{4,0},{8,4},{12,8},{16,12},{20,16},{24,20},{28,24},{32,28}... | collective-permute-start | bytes 776 | tf_op jit(solution)/shard_map/ppermute | solution.py:21
  23.5 5.8 %collective-permute-start.2 = (f32[64]{0:T(128)S(1)}, f32[64]{0:T(128)S(1)}, u32[]{:S(2)}, u32[]{:S(2)}) collective-permute-start(f32[64]{0:T(128)S(1)} %slice_bitcast_fusion.2), channel_id=1, source_target_pairs={{0,4},{4,8},{8,12},{12,16},{16,20},{20,24},{24,28},{28,32},{32,36}... | collective-permute-start | bytes 776 | tf_op jit(solution)/shard_map/ppermute | solution.py:21
  29.7 7.9 %collective-permute-start.3 = (f32[64]{0:T(128)S(1)}, f32[64]{0:T(128)S(1)}, u32[]{:S(2)}, u32[]{:S(2)}) collective-permute-start(f32[64]{0:T(128)S(1)} %slice_bitcast_fusion.1), channel_id=1, source_target_pairs={{0,124},{4,0},{8,4},{12,8},{16,12},{20,16},{24,20},{28,24},{32,28}... | collective-permute-start | bytes 776 | tf_op jit(solution)/shard_map/ppermute | solution.py:21
  36.1 17.4 %collective-permute-start.5 = (f32[1024,64]{1,0:T(8,128)}, f32[1024,64]{1,0:T(8,128)}, u32[]{:S(2)}, u32[]{:S(2)}) collective-permute-start(f32[1024,64]{1,0:T(8,128)} %gather_fusion), channel_id=1, source_target_pairs={{4,0},{8,4},{12,8},{16,12},{20,16},{24,20},{28,24},{32,28},{36,32}... | collective-permute-start | bytes 786440 | tf_op jit(solution)/shard_map/ppermute | solution.py:33
  36.3 17.2 %collective-permute-start.4 = (f32[1024,64]{1,0:T(8,128)}, f32[1024,64]{1,0:T(8,128)}, u32[]{:S(2)}, u32[]{:S(2)}) collective-permute-start(f32[1024,64]{1,0:T(8,128)} %gather_fusion), channel_id=1, source_target_pairs={{0,4},{4,8},{8,12},{12,16},{16,20},{20,24},{24,28},{28,32},{32,36}... | collective-permute-start | bytes 786440 | tf_op jit(solution)/shard_map/ppermute | solution.py:30
  43.4 10.1 %copy-start.5 = (f32[1024,64]{1,0:T(8,128)S(1)}, f32[1024,64]{1,0:T(8,128)}, u32[]{:S(2)}) copy-start(f32[1024,64]{1,0:T(8,128)} %gather_fusion) | copy-start | bytes 786436
  45.3 41.2 %all-to-all-start = ((f32[1,64,2,8,256]{4,2,1,0,3:T(2,128)}), f32[1,64,2,8,256]{4,2,1,0,3:T(2,128)S(1)}, u32[]{:S(2)}, u32[]{:S(2)}) async-start(f32[1,64,2,8,256]{4,2,1,0,3:T(2,128)} %pad_maximum_fusion.1), calls=%async_computation | async-start | bytes 2097152 | tf_op jit(solution)/shard_map/all_to_all | solution.py:141
  86.5 30.1 %all-to-all-start.2 = ((f32[8,1024,64]{1,2,0:T(8,128)}), f32[8,1024,64]{1,2,0:T(8,128)}, u32[]{:S(2)}, u32[]{:S(2)}) async-start(f32[8,1024,64]{1,2,0:T(8,128)} %copy.39), calls=%async_computation.2 | async-start | bytes 4194304 | tf_op jit(solution)/shard_map/all_to_all | solution.py:156
  97.9 6.2 %copy-start.2 = (f32[32768]{0:T(1024)S(1)}, f32[32768]{0:T(1024)}, u32[]{:S(2)}) copy-start(f32[32768]{0:T(1024)} %param.13) | copy-start | bytes 393220
  120.5 3.6 %copy-start.3 = (f32[8,1,1024,64]{2,3,0,1:T(8,128)}, f32[8,1,1024,64]{2,3,0,1:T(8,128)S(1)}, u32[]{:S(2)}) copy-start(f32[8,1,1024,64]{2,3,0,1:T(8,128)S(1)} %get-tuple-element.60) | copy-start | bytes 6291460
  161.1 1.9 %copy-start.4 = (f32[8,1,1024,64]{2,3,0,1:T(8,128)S(1)}, f32[8,1,1024,64]{2,3,0,1:T(8,128)}, u32[]{:S(2)}) copy-start(f32[8,1,1024,64]{2,3,0,1:T(8,128)} %copy-done.3) | copy-start | bytes 6291460
  163.0 2.9 %copy-start.6 = (f32[64,8,2,256]{3,1,2,0:T(8,128)S(1)}, f32[64,8,2,256]{3,1,2,0:T(8,128)}, u32[]{:S(2)}) copy-start(f32[64,8,2,256]{3,1,2,0:T(8,128)} %copy.52) | copy-start | bytes 3145732
  169.5 19.8 %all-to-all-start.3 = ((f32[8,64,2,1,256]{4,2,1,3,0:T(2,128)}), f32[8,64,2,1,256]{4,2,1,3,0:T(2,128)S(1)}, u32[]{:S(2)}, u32[]{:S(2)}) async-start(f32[8,64,2,1,256]{4,2,1,3,0:T(2,128)} %bitcast.42), calls=%async_computation.3 | async-start | bytes 2097152 | tf_op jit(solution)/shard_map/all_to_all | solution.py:172
where the time goes:
time: 192 us
  local copies, waits for them, and re-layouts  77.4 us (40%)
  matrix products  52.3 us (27%)
  starting transfers between devices  35.6 us (19%)
  other arithmetic  17.3 us (9%)
  waiting for transfers between devices  6.71 us (3%)
    gather x1, local copies, waits for them, and re-layouts, per_device(): picked = jnp.take(nearby, relative.reshape(-1), axis=0, mode='clip')  27.9 us
    dot_general x6, matrix products, newton_step(): middle = 1.5 * identity - 0.5 * jnp.dot(root_inv, approx, precision=highest)  11.2 us
    dot_general x6, matrix products, newton_step(): jnp.dot(approx, middle, precision=highest)  11.1 us
    dot_general x6, matrix products, newton_step(): jnp.dot(middle, root_inv, precision=highest)  11.1 us
    dot_general x2, matrix products, apply_transform(): jnp.einsum('ij,...iv->...jv', transform, states - state_mean, precision=h...  10.6 us
    unnamed x26, local copies, waits for them, and re-layouts  10.3 us
    ppermute x4, starting transfers between devices, shifted(): lax.ppermute(array, axis, [(i, (i + by) % peers) for i in range(peers)])  10.2 us
    all_to_all x1, starting transfers between devices, per_device(): lax.all_to_all(prior_fields.reshape(1, trial_slab_lines, 2, trial_bundles...  7.94 us
  transfers between devices with their start and end apart: 10, of which 2 were waited for; matrix products, arithmetic and copies ran while one was open for 47% of the time, Pallas kernels for 0%

commit v1 on v0

v1 whole, which is shorter than its diff:
```python
import functools
import math

import jax
import jax.numpy as jnp
from jax import lax
from jax.experimental import pallas as pl
from jax.experimental.pallas import tpu as pltpu
from jax.sharding import PartitionSpec as P

GROUP = ("grp", "mem")
PARTS = 8
ROWS = 64
MEMBERS = 512
CELLS = 2048
CHUNKS = 16
CELLS_TILE = 256
STATE = 512
OBS = 1024
SLOTS = 1024
NOBS = 32768
NCELLS = 65536
TILES = 32
LOC = 512
LAGS = 3
f32 = jnp.float32
bf16 = jnp.bfloat16
VMEM = pl.BlockSpec(memory_space=pltpu.VMEM)
SMEM = pl.BlockSpec(memory_space=pltpu.SMEM)


def params(mib):
    return pltpu.CompilerParams(vmem_limit_bytes=mib * 1024 * 1024)


def halves(x):
    hi = x.astype(bf16)
    return hi, (x - hi.astype(f32)).astype(bf16)


def dot(a, b):
    return jnp.dot(a, b, preferred_element_type=f32)


def dot_nt(a, b):
    return lax.dot_general(a, b, (((1,), (1,)), ((), ())), preferred_element_type=f32)


def product(a, b):
    (ah, al), (bh, bl) = a, b
    return dot(ah, bh) + (dot(ah, bl) + dot(al, bh))


def forecast_kernel(cur, depth, left, right, cells, fields, own, packed, hbuf, ubuf, table):
    lane = lax.broadcasted_iota(jnp.int32, (ROWS, 128), 1)
    first, last = lane == 0, lane == 127

    def old(c, v):
        if c < 0:
            return left[pl.ds(v, ROWS, stride=2), :]
        if c == CHUNKS:
            return right[pl.ds(v, ROWS, stride=2), :]
        return cur[pl.ds(2 * c + v, ROWS, stride=2 * CHUNKS), :]

    def scaled_depth(c):
        if c < 0:
            row = left[128:129, :]
        elif c == CHUNKS:
            row = right[128:129, :]
        else:
            row = depth[c : c + 1, :]
        return 0.9 * row

    def height_step(h_of, u_of, put, low):
        before = None
        for c in range(low, CHUNKS + 1):
            u = u_of(c)
            turned = pltpu.roll(u, 1, 1)
            previous = turned if before is None else jnp.where(first, before, turned)
            before = turned
            put(c, h_of(c) - scaled_depth(c) * (u - previous))

    def speed_step(h_of, u_of, put, low, high):
        turned = pltpu.roll(h_of(low), 127, 1)
        for c in range(low, high):
            after = pltpu.roll(h_of(c + 1), 127, 1) if c < CHUNKS else turned
            following = jnp.where(last, after, turned)
            turned = after
            put(c, u_of(c) - 0.9 * (following - h_of(c)))

    def put_h(c, x):
        hbuf[c + 1] = x

    def put_u(c, x):
        ubuf[c + 1] = x

    def h_new(c):
        return hbuf[c + 1]

    def u_new(c):
        return ubuf[c + 1]

    height_step(lambda c: old(c, 0), lambda c: old(c, 1), put_h, -1)
    speed_step(h_new, lambda c: old(c, 1), put_u, -1, CHUNKS + 1)
    height_step(h_new, u_new, put_h, -1)

    def put_fields(v, c, x):
        fields[c // 2, :, v * CELLS_TILE + (c % 2) * 128 : v * CELLS_TILE + (c % 2 + 1) * 128] = x

    speed_step(h_new, u_new, functools.partial(put_fields, 1), 0, CHUNKS)
    for c in range(CHUNKS):
        h = h_new(c)
        put_fields(0, c, h)
        table[c * 128 : (c + 1) * 128, :] = jnp.concatenate([h, h], axis=0).T

    def pick(i, carry):
        for j in range(32):
            o = i * 32 + j
            own[pl.ds(o, 1), :] = table[pl.ds(cells[o], 1), :]
        return carry

    lax.fori_loop(0, OBS // 32, pick, 0)
    low_half = lax.broadcasted_iota(jnp.int32, (OBS // 2, 128), 1) < ROWS
    packed[...] = jnp.where(low_half, own[: OBS // 2, :], own[OBS // 2 :, :])


def forecast(cur, depth, left, right, cells):
    return pl.pallas_call(
        forecast_kernel,
        out_shape=(
            jax.ShapeDtypeStruct((PARTS, ROWS, STATE), f32),
            jax.ShapeDtypeStruct((OBS, 128), f32),
            jax.ShapeDtypeStruct((OBS // 2, 128), f32),
        ),
        in_specs=[VMEM, VMEM, VMEM, VMEM, SMEM],
        out_specs=(VMEM, VMEM, VMEM),
        scratch_shapes=[
            pltpu.VMEM((CHUNKS + 2, ROWS, 128), f32),
            pltpu.VMEM((CHUNKS + 2, ROWS, 128), f32),
            pltpu.VMEM((CELLS, 128), f32),
        ],
        compiler_params=params(24),
        name="forecast",
    )(cur, depth, left, right, cells)


def pick_kernel(lists, below, own, above, out, table, stage):
    low_half = lax.broadcasted_iota(jnp.int32, (OBS // 2, 128), 1) < ROWS
    for place, packed in ((0, below), (2, above)):
        x = packed[...]
        turned = pltpu.roll(x, ROWS, 1)
        table[place * OBS : place * OBS + OBS // 2, :] = jnp.where(low_half, x, turned)
        table[place * OBS + OBS // 2 : (place + 1) * OBS, :] = jnp.where(low_half, turned, x)
    table[OBS : 2 * OBS, :] = own[...]
    low_row = lax.broadcasted_iota(jnp.int32, (1, 128), 1) < ROWS

    def block(i, carry):
        k = i // 4
        q = i % 4
        for j in range(128):
            a = lists[k, q * 128 + j]
            b = lists[k, SLOTS // 2 + q * 128 + j]
            stage[j : j + 1, :] = jnp.where(low_row, table[pl.ds(a, 1), :], table[pl.ds(b, 1), :])
        turned = stage[...].T
        out[k, :, pl.ds(pl.multiple_of(q * 128, 128), 128)] = turned[:ROWS]
        out[k, :, pl.ds(pl.multiple_of(SLOTS // 2 + q * 128, 128), 128)] = turned[ROWS:]
        return carry

    lax.fori_loop(0, PARTS * 4, block, 0)


def pick(lists, below, own, above):
    return pl.pallas_call(
        pick_kernel,
        out_shape=jax.ShapeDtypeStruct((PARTS, ROWS, SLOTS), f32),
        in_specs=[SMEM, VMEM, VMEM, VMEM],
        out_specs=VMEM,
        scratch_shapes=[pltpu.VMEM((3 * OBS, 128), f32), pltpu.VMEM((128, 128), f32)],
        compiler_params=params(24),
        name="pick",
    )(lists, below, own, above)


def slots_kernel(where_ref, rel, values, errors, cells, out, rows):
    tile = where_ref[0]
    center = where_ref[1]
    for n in range(3):
        t = lax.rem(tile + (TILES - 1 + n), TILES)
        for j in range(8):
            at = n * OBS + j * 128
            rows[0:1, at : at + 128] = values[t, j : j + 1, :]
            rows[1:2, at : at + 128] = errors[t, j : j + 1, :]
            rows[2:3, at : at + 128] = cells[t, j : j + 1, :].astype(f32)
    listed = rel[...]
    total = jnp.zeros((9, SLOTS), f32)
    for n in range(12):
        x = rows[0:3, n * 256 : (n + 1) * 256]
        a, rest = x.astype(bf16), None
        rest = x - a.astype(f32)
        b = rest.astype(bf16)
        c = (rest - b.astype(f32)).astype(bf16)
        parts = jnp.concatenate([a.astype(f32), b.astype(f32), c.astype(f32)], axis=0).astype(bf16)
        here = lax.broadcasted_iota(jnp.int32, (256, SLOTS), 0) + n * 256
        chosen = jnp.where(here == listed, 1.0, 0.0).astype(bf16)
        total = total + dot(parts, chosen)
    found = total[0:3] + total[3:6] + total[6:9]
    value, error, cell = found[0:1], found[1:2], found[2:3].astype(jnp.int32)
    distance = jnp.abs(cell - center)
    distance = jnp.minimum(distance, NCELLS - distance).astype(f32)
    used = listed >= 0
    weight = jnp.exp(-0.5 * (distance / LOC) ** 2) / (error * error)
    out[0:1, :] = jnp.where(used, weight, 0.0)
    out[1:2, :] = jnp.where(used, value, 0.0)


def slots(where_arr, rel, values, errors, cells):
    return pl.pallas_call(
        slots_kernel,
        out_shape=jax.ShapeDtypeStruct((8, SLOTS), f32),
        in_specs=[SMEM, VMEM, VMEM, VMEM, VMEM],
        out_specs=VMEM,
        scratch_shapes=[pltpu.VMEM((8, 3 * OBS), f32)],
        compiler_params=params(24),
        name="slots",
    )(where_arr, rel, values, errors, cells)


def analyse_kernel(predicted, slot_rows, state, gain_hi, gain_lo, analysis):
    y = predicted[...]
    weight = slot_rows[0:1, :]
    mean = jnp.sum(y, axis=0, keepdims=True) * (1.0 / MEMBERS)
    root_weight = jnp.sqrt(weight)
    spread = (y - mean) * root_weight
    departure = (slot_rows[1:2, :] - mean) * root_weight
    sh, sl = halves(spread)
    dh, dl = halves(jnp.broadcast_to(departure, (16, SLOTS)))
    rows_i = lax.broadcasted_iota(jnp.int32, (MEMBERS, MEMBERS), 0)
    cols_i = lax.broadcasted_iota(jnp.int32, (MEMBERS, MEMBERS), 1)
    eye = jnp.where(rows_i == cols_i, 1.0, 0.0)
    a = dot_nt(sh, sh) + (dot_nt(sh, sl) + dot_nt(sl, sh)) + (MEMBERS - 1.0) * eye
    innovation = (dot_nt(dh, sh) + (dot_nt(dh, sl) + dot_nt(dl, sh)))[0:1, :]
    bound = jnp.max(jnp.sum(jnp.abs(a), axis=0, keepdims=True), axis=1, keepdims=True)
    approx = a / bound

    def two_steps(m):
        mp = halves(m)
        m2 = product(mp, mp)
        q = 1.6875 * eye - 0.5625 * m + 0.0625 * m2
        return 2.25 * eye - 2.4375 * m + product(halves(m2), halves(q))

    r = halves(two_steps(approx))
    z = r
    w = halves(product(halves(approx), r))
    r = halves(two_steps(product(z, w)))
    z, w = halves(product(r, z)), halves(product(w, r))
    r = halves(two_steps(product(z, w)))
    root = product(r, z) * lax.rsqrt(bound)
    once = jnp.sum(root * innovation, axis=1, keepdims=True)
    mean_weight = jnp.sum(root * once, axis=0, keepdims=True)
    moved = math.sqrt(MEMBERS - 1) * root + mean_weight
    gain = moved + (1.0 - jnp.sum(moved, axis=1, keepdims=True)) * (1.0 / MEMBERS)
    gh, gl = halves(gain)
    gain_hi[...] = gh
    gain_lo[...] = gl
    analysis[...] = product((gh, gl), halves(state[...]))


def analyse(predicted, slot_rows, state):
    return pl.pallas_call(
        analyse_kernel,
        out_shape=(
            jax.ShapeDtypeStruct((MEMBERS, MEMBERS), bf16),
            jax.ShapeDtypeStruct((MEMBERS, MEMBERS), bf16),
            jax.ShapeDtypeStruct((MEMBERS, STATE), f32),
        ),
        in_specs=[VMEM, VMEM, VMEM],
        out_specs=(VMEM, VMEM, VMEM),
        compiler_params=params(40),
        name="analyse",
    )(predicted, slot_rows, state)


def smooth_kernel(gain_hi, gain_lo, state, out):
    out[0] = product((gain_hi[...], gain_lo[...]), halves(state[0]))


def smooth(gain_hi, gain_lo, states):
    whole = pl.BlockSpec((MEMBERS, MEMBERS), lambda i: (0, 0))
    one = pl.BlockSpec((1, MEMBERS, STATE), lambda i: (i, 0, 0))
    return pl.pallas_call(
        smooth_kernel,
        out_shape=jax.ShapeDtypeStruct((LAGS, MEMBERS, STATE), f32),
        grid=(LAGS,),
        in_specs=[whole, whole, one],
        out_specs=one,
        compiler_params=params(24),
        cost_estimate=pl.CostEstimate(
            flops=2 * 3 * LAGS * MEMBERS**2 * STATE, bytes_accessed=8 * LAGS * MEMBERS * STATE, transcendentals=0
        ),
        name="smooth",
    )(gain_hi, gain_lo, states)


def assemble_kernel(parts, out):
    for k in range(PARTS):
        for v in range(2):
            for b in range(2):
                at = v * CELLS_TILE + b * 128
                out[pl.ds(2 * (2 * k + b) + v, ROWS, stride=2 * CHUNKS), :] = parts[k, :, at : at + 128]


def assemble(parts):
    return pl.pallas_call(
        assemble_kernel,
        out_shape=jax.ShapeDtypeStruct((ROWS * 2 * CHUNKS, 128), f32),
        in_specs=[VMEM],
        out_specs=VMEM,
        compiler_params=params(24),
        name="assemble",
    )(parts)


def along_tiles(x, by):
    return lax.ppermute(x, "tile", [(i, (i + by) % TILES) for i in range(TILES)])


def exchange(x):
    return lax.all_to_all(x, GROUP, split_axis=0, concat_axis=0, tiled=True)


def per_device(
    current_state, lagged_states, water_depth, obs_cells, obs_values, obs_errors, tile_obs
):
    tile = lax.axis_index("tile")
    part = lax.axis_index("grp") * lax.axis_size("mem") + lax.axis_index("mem")
    by_chunk = current_state.reshape(ROWS, 2, CHUNKS, 128).transpose(0, 2, 1, 3)
    depth = water_depth.reshape(CHUNKS, 128)

    def edge(c):
        return jnp.concatenate(
            [by_chunk[:, c].reshape(2 * ROWS, 128), jnp.broadcast_to(depth[c], (8, 128))], axis=0
        )

    left = along_tiles(edge(CHUNKS - 1), 1)
    right = along_tiles(edge(0), -1)
    listed = tile_obs[0, 0]
    rel = jnp.where(listed >= 0, (listed - (tile - 1) * OBS) & (NOBS - 1), -1)
    lists = lax.all_gather(jnp.maximum(rel, 0), GROUP, axis=0)
    local_cells = lax.dynamic_slice_in_dim(obs_cells, tile * OBS, OBS) - tile * CELLS
    fields, own, packed = forecast(
        by_chunk.reshape(ROWS * 2 * CHUNKS, 128), depth, left, right, local_cells
    )
    below = along_tiles(packed, 1)
    above = along_tiles(packed, -1)
    state = exchange(fields).reshape(MEMBERS, STATE)
    picked = pick(lists, below, own, above)
    predicted = exchange(picked).reshape(MEMBERS, SLOTS)
    center = tile * CELLS + part * CELLS_TILE + CELLS_TILE // 2
    slot_rows = slots(
        jnp.stack([tile, center]),
        rel.reshape(1, SLOTS),
        obs_values.reshape(TILES, 8, 128),
        obs_errors.reshape(TILES, 8, 128),
        obs_cells.reshape(TILES, 8, 128),
    )
    gain_hi, gain_lo, analysis = analyse(predicted, slot_rows, state)
    returned = exchange(analysis.reshape(PARTS, ROWS, STATE))
    older = smooth(gain_hi, gain_lo, lagged_states.reshape(LAGS, MEMBERS, STATE))
    analysed = assemble(returned).reshape(ROWS, CHUNKS, 2, 128).transpose(0, 2, 1, 3)
    return (
        analysed.reshape(ROWS, 2, CELLS),
        older.reshape(LAGS, 1, 1, MEMBERS, STATE),
    )


def solution(mesh):
    placed = (
        P(GROUP, None, "tile"),
        P(None, "tile", GROUP, None, None),
        P("tile"),
        P(),
        P(),
        P(),
        P("tile", GROUP, None),
    )
    return jax.shard_map(
        per_device,
        mesh=mesh,
        in_specs=placed,
        out_specs=(P(GROUP, None, "tile"), P(None, "tile", GROUP, None, None)),
        check_vma=False,
    )
```

time: 192 us -> 140 us (0.73)
  local copies, waits for them, and re-layouts: 77.4 us -> 10.7 us
  matrix products: 52.3 us -> 0 us
  Pallas kernels: 0 us -> 50.8 us
  waiting for transfers between devices: 6.71 us -> 28.9 us
  blocking collectives: 0 us -> 18.2 us
  other arithmetic: 17.3 us -> 0.79 us
  starting transfers between devices: 35.6 us -> 29.4 us
    dot_general x24 -> x0, matrix products: 52.3 us -> none  [the longest x6 11.2 us: newton_step(): middle = 1.5 * identity - 0.5 * jnp.dot(root_inv, approx, precision=highest)]
    pallas_call x0 -> x6, Pallas kernels: none -> 50.8 us  [the longest x1 24.3 us: pick(): pl.pallas_call(pick_kernel, out_shape=jax.ShapeDtypeStruct((PARTS, ROWS,...]
    gather x5 -> x0, local copies, waits for them, and re-layouts: 50.4 us -> none  [the longest x1 27.9 us: per_device(): picked = jnp.take(nearby, relative.reshape(-1), axis=0, mode='clip')]
    all_to_all x4 -> x3, waiting for transfers between devices: 2.12 us -> 28 us  [exchange(): return lax.all_to_all(x, GROUP, split_axis=0, concat_axis=0, tiled=True)]
    all_gather x0 -> x1, blocking collectives: none -> 18.2 us  [per_device(): lists = lax.all_gather(jnp.maximum(rel, 0), GROUP, axis=0)]
    all_to_all x4 -> x3, starting transfers between devices: 23.9 us -> 15.1 us  [exchange(): return lax.all_to_all(x, GROUP, split_axis=0, concat_axis=0, tiled=True)]
    reshape x2 -> x0, local copies, waits for them, and re-layouts: 5.4 us -> none  [the longest x1 3.78 us: per_device(): picked = picked.reshape(trial_bundles, rows_here.shape[0], trial_slab_lines)]
    reduce_sum x3 -> x0, other arithmetic: 4.41 us -> none  [the longest x2 2.67 us: apply_transform(): state_mean = jnp.mean(states, axis=-2, keepdims=True)]
  transfers between devices with their start and end apart: 10 -> 7, of which waited for: 2 -> 3; matrix products, arithmetic and copies ran while one was open for 47% -> 1% of each run, Pallas kernels for 0% -> 21%
where the time goes in v1:
time: 140 us
  Pallas kernels  50.8 us (36%)
  starting transfers between devices  29.4 us (21%)
  waiting for transfers between devices  28.9 us (21%)
  blocking collectives  18.2 us (13%)
  local copies, waits for them, and re-layouts  10.7 us (8%)
    all_to_all x3, waiting for transfers between devices, exchange(): return lax.all_to_all(x, GROUP, split_axis=0, concat_axis=0, tiled=True)  28 us
    pallas_call x1, Pallas kernels, pick(): pl.pallas_call(pick_kernel, out_shape=jax.ShapeDtypeStruct((PARTS, ROWS,...  24.3 us
    all_gather x1, blocking collectives, per_device(): lists = lax.all_gather(jnp.maximum(rel, 0), GROUP, axis=0)  18.2 us
    all_to_all x3, starting transfers between devices, exchange(): return lax.all_to_all(x, GROUP, split_axis=0, concat_axis=0, tiled=True)  15.1 us
    pallas_call x1, Pallas kernels, analyse(): pl.pallas_call(analyse_kernel, out_shape=(jax.ShapeDtypeStruct((MEMBERS,...  14.6 us
    ppermute x4, starting transfers between devices, along_tiles(): lax.ppermute(x, 'tile', [(i, (i + by) % TILES) for i in range(TILES)])  14.2 us
    unnamed x25, local copies, waits for them, and re-layouts  8.16 us
    pallas_call x1, Pallas kernels, forecast(): pl.pallas_call(forecast_kernel, out_shape=(jax.ShapeDtypeStruct((PARTS, R...  4.43 us
  transfers between devices with their start and end apart: 7, of which 3 were waited for; matrix products, arithmetic and copies ran while one was open for 1% of the time, Pallas kernels for 21%

profile of v1, /device:TPU:1, one launch (start us, length us, event | category | flops | bytes accessed | tf_op | source)
XLA Modules:
  0.0 139.6 jit_solution(2418885832673962809)
XLA Ops:
  0.6 0.0 copy-start
  0.6 0.0 copy-start.11
  0.6 1.8 %bitcast_bitcast_fusion = f32[64,16,2,128]{3,2,0,1:T(2,128)S(1)} fusion(f32[64,2,2048]{2,1,0:T(2,128)} %param.7), kind=kLoop, calls=%fused_computation | loop fusion | bytes 2097152 | tf_op jit(solution)/shard_map/transpose | solution.py:336
  2.5 0.7 fusion.3
  3.2 2.5 %collective-permute-start = (f32[136,128]{1,0:T(8,128)S(1)}, f32[136,128]{1,0:T(8,128)S(1)}, u32[]{:S(2)}, u32[]{:S(2)}) collective-permute-start(f32[136,128]{1,0:T(8,128)S(1)} %pad_maximum_fusion), channel_id=1, source_target_pairs={{0,4},{4,8},{8,12},{12,16},{16,20},{20,24},{24,28},{28,32},{32,36}... | collective-permute-start | bytes 208904 | tf_op jit(solution)/shard_map/ppermute | solution.py:324
  5.8 6.5 %collective-permute-start.1 = (f32[136,128]{1,0:T(8,128)S(1)}, f32[136,128]{1,0:T(8,128)S(1)}, u32[]{:S(2)}, u32[]{:S(2)}) collective-permute-start(f32[136,128]{1,0:T(8,128)S(1)} %pad_maximum_fusion.1), channel_id=1, source_target_pairs={{0,124},{4,0},{8,4},{12,8},{16,12},{20,16},{24,20},{28,24},{32,28}... | collective-permute-start | bytes 208904 | tf_op jit(solution)/shard_map/ppermute | solution.py:324
  12.3 0.7 dynamic-slice_subtract_fusion.cells
  13.0 0.9 collective-permute-done.left
  13.9 0.0 collective-permute-done.1.right
  13.9 0.0 copy-done
  13.9 0.0 copy-start.5
  13.9 0.7 copy-done.5
  14.6 4.4 %forecast.1 = (f32[8,64,512]{2,1,0:T(8,128)}, f32[1024,128]{1,0:T(8,128)S(1)}, f32[512,128]{1,0:T(8,128)S(1)}) custom-call(f32[2048,128]{1,0:T(8,128)S(1)} %bitcast.42, f32[16,128]{1,0:T(8,128)S(1)} %bitcast.48, f32[136,128]{1,0:T(8,128)S(1)} %collective-permute-done.left, f32[136,128]{1,0:T(8,128)S(1)} %collective-permute-done.1.right, ...), custom_call_target="tpu_custom_call" | custom-call | tf_op jit(solution)/shard_map/forecast/pallas_call | solution.py:128
  19.0 5.8 %all-to-all-start.1 = ((f32[8,64,512]{2,1,0:T(8,128)}), f32[8,64,512]{2,1,0:T(8,128)S(1)}, u32[]{:S(2)}, u32[]{:S(2)}) async-start(f32[8,64,512]{2,1,0:T(8,128)} %get-tuple-element.10), calls=%async_computation.1 | async-start | bytes 2097152 | tf_op jit(solution)/shard_map/all_to_all | solution.py:328
  24.8 0.0 collective-permute-start.2
  24.9 5.2 %collective-permute-start.3 = (f32[512,128]{1,0:T(8,128)S(1)}, f32[512,128]{1,0:T(8,128)S(1)}, u32[]{:S(2)}, u32[]{:S(2)}) collective-permute-start(f32[512,128]{1,0:T(8,128)S(1)} %get-tuple-element.8), channel_id=1, source_target_pairs={{0,124},{4,0},{8,4},{12,8},{16,12},{20,16},{24,20},{28,24},{32,28}... | collective-permute-start | bytes 786440 | tf_op jit(solution)/shard_map/ppermute | solution.py:324
  30.0 0.0 copy-done.11
  30.1 18.2 %all-gather = s32[8,1,1024]{2,1,0:T(1,128)S(1)} all-gather(s32[1,1,1024]{2,1,0:T(1,128)S(1)} %get-tuple-element.18), channel_id=1, replica_groups=mesh['grp'=2,'tile'=32,'mem'=4] {'grp','mem'}, dimensions={0}, use_global_device_ids=true | all-gather | bytes 36864 | tf_op jit(solution)/shard_map/all_gather | solution.py:348
  48.3 0.0 collective-permute-done.2.below
  48.3 0.0 collective-permute-done.3.above
  48.3 0.0 copy-start.2
  48.3 0.0 copy-start.3
  48.4 24.3 %pick.1 = f32[8,64,1024]{2,1,0:T(8,128)} custom-call(s32[8,1024]{1,0:T(8,128)S(1)} %bitcast.45, f32[512,128]{1,0:T(8,128)S(1)} %collective-permute-done.2.below, f32[1024,128]{1,0:T(8,128)S(1)} %get-tuple-element.9.own, f32[512,128]{1,0:T(8,128)S(1)} %collective-permute-done.3.above), custom_call_target="tpu_custom_call" | custom-call | tf_op jit(solution)/shard_map/pick/pallas_call | solution.py:173
  72.7 0.0 all-to-all-done.1
  72.7 3.7 %all-to-all-start = ((f32[8,64,1024]{2,1,0:T(8,128)}), f32[8,64,1024]{2,1,0:T(8,128)S(1)}, u32[]{:S(2)}, u32[]{:S(2)}) async-start(f32[8,64,1024]{2,1,0:T(8,128)} %pick.1), calls=%async_computation | async-start | bytes 4194304 | tf_op jit(solution)/shard_map/all_to_all | solution.py:328
  76.4 0.1 pad_add_fusion.where_ref
  76.5 0.0 copy-done.2
  76.5 0.0 copy-done.3
  76.5 0.0 copy-start.4
  76.5 0.9 copy-done.4
  77.4 1.5 %slots.1.slot_rows = f32[8,1024]{1,0:T(8,128)S(1)} custom-call(s32[2]{0:T(128)S(1)} %pad_add_fusion.where_ref, s32[1,1024]{1,0:T(1,128)S(1)} %get-tuple-element.19.rel, f32[32,8,128]{2,1,0:T(8,128)S(1)} %bitcast.46, f32[32,8,128]{2,1,0:T(8,128)S(1)} %bitcast.47, s32[32,8,128]{2,1,0:T(8,128)S(1)} %bitcast.44), custom_call_target="tpu_custom_call" | custom-call | tf_op jit(solution)/shard_map/slots/pallas_call | solution.py:217
  79.0 22.3 %all-to-all-done = f32[8,64,1024]{2,1,0:T(8,128)S(1)} async-done(((f32[8,64,1024]{2,1,0:T(8,128)}), f32[8,64,1024]{2,1,0:T(8,128)S(1)}, u32[]{:S(2)}, u32[]{:S(2)}) %all-to-all-start) | async-done | bytes 2097184 | tf_op jit(solution)/shard_map/all_to_all | solution.py:328
  101.2 14.6 %analyse.1 = (bf16[512,512]{1,0:T(8,128)(2,1)S(1)}, bf16[512,512]{1,0:T(8,128)(2,1)S(1)}, f32[512,512]{1,0:T(8,128)S(1)}) custom-call(f32[512,1024]{1,0:T(8,128)S(1)} %bitcast.40, f32[8,1024]{1,0:T(8,128)S(1)} %slots.1.slot_rows, f32[512,512]{1,0:T(8,128)S(1)} %bitcast.41), custom_call_target="tpu_custom_call" | custom-call | tf_op jit(solution)/shard_map/analyse/pallas_call | solution.py:269
  115.8 0.0 copy-start.1
  115.9 1.0 copy-done.1
  116.8 0.0 copy-start.7
  116.8 0.8 copy-done.7
  117.6 0.0 copy-start.9
  117.6 0.8 copy-done.9
  118.4 5.6 %all-to-all-start.2 = ((f32[8,64,512]{2,1,0:T(8,128)}), f32[8,64,512]{2,1,0:T(8,128)S(1)}, u32[]{:S(2)}, u32[]{:S(2)}) async-start(f32[8,64,512]{2,1,0:T(8,128)} %bitcast.43), calls=%async_computation.2 | async-start | bytes 2097152 | tf_op jit(solution)/shard_map/all_to_all | solution.py:328
  124.0 0.0 copy-start.6
  124.0 1.9 %copy-done.6 = f32[3,1,1,512,512]{4,3,2,1,0:T(8,128)S(1)} copy-done((f32[3,1,1,512,512]{4,3,2,1,0:T(8,128)S(1)}, f32[3,1,1,512,512]{4,3,2,1,0:T(8,128)}, u32[]{:S(2)}) %copy-start.6) | copy-done | bytes 3145752
  125.9 0.0 copy-start.8
  125.9 1.0 copy-done.8
  126.9 0.0 copy-start.10
  126.9 1.0 copy-done.10
  127.9 3.9 %smooth.1 = f32[3,512,512]{2,1,0:T(8,128)} custom-call(bf16[512,512]{1,0:T(8,128)(2,1)S(1)} %copy-done.8, bf16[512,512]{1,0:T(8,128)(2,1)S(1)} %copy-done.10, f32[3,512,512]{2,1,0:T(8,128)S(1)} %bitcast.49), custom_call_target="tpu_custom_call" | custom-call | flops 2415919104 | bytes 6291456 | tf_op jit(solution)/shard_map/smooth/pallas_call | solution.py:290
  131.9 5.7 %all-to-all-done.2.parts = f32[8,64,512]{2,1,0:T(8,128)S(1)} async-done(((f32[8,64,512]{2,1,0:T(8,128)}), f32[8,64,512]{2,1,0:T(8,128)S(1)}, u32[]{:S(2)}, u32[]{:S(2)}) %all-to-all-start.2) | async-done | bytes 1048608 | tf_op jit(solution)/shard_map/all_to_all | solution.py:328
  137.6 2.0 %assemble.1 = f32[2048,128]{1,0:T(8,128)} custom-call(f32[8,64,512]{2,1,0:T(8,128)S(1)} %all-to-all-done.2.parts), custom_call_target="tpu_custom_call" | custom-call | tf_op jit(solution)/shard_map/assemble/pallas_call | solution.py:313
  (7 shorter events, 0.1 us)
Async XLA Ops:
  0.6 13.2 %copy-start = (f32[64,2,2048]{2,1,0:T(2,128)S(1)}, f32[64,2,2048]{2,1,0:T(2,128)}, u32[]{:S(2)}) copy-start(f32[64,2,2048]{2,1,0:T(2,128)} %param.7) | copy-start | bytes 3145732
  0.6 29.4 %copy-start.11 = (s32[1,1,1024]{2,1,0:T(1,128)S(1)}, s32[1,1,1024]{2,1,0:T(1,128)}, u32[]{:S(2)}) copy-start(s32[1,1,1024]{2,1,0:T(1,128)} %param.13) | copy-start | bytes 12292
  3.2 10.6 %collective-permute-start = (f32[136,128]{1,0:T(8,128)S(1)}, f32[136,128]{1,0:T(8,128)S(1)}, u32[]{:S(2)}, u32[]{:S(2)}) collective-permute-start(f32[136,128]{1,0:T(8,128)S(1)} %pad_maximum_fusion), channel_id=1, source_target_pairs={{0,4},{4,8},{8,12},{12,16},{16,20},{20,24},{24,28},{28,32},{32,36}... | collective-permute-start | bytes 208904 | tf_op jit(solution)/shard_map/ppermute | solution.py:324
  5.8 8.1 %collective-permute-start.1 = (f32[136,128]{1,0:T(8,128)S(1)}, f32[136,128]{1,0:T(8,128)S(1)}, u32[]{:S(2)}, u32[]{:S(2)}) collective-permute-start(f32[136,128]{1,0:T(8,128)S(1)} %pad_maximum_fusion.1), channel_id=1, source_target_pairs={{0,124},{4,0},{8,4},{12,8},{16,12},{20,16},{24,20},{28,24},{32,28}... | collective-permute-start | bytes 208904 | tf_op jit(solution)/shard_map/ppermute | solution.py:324
  13.9 0.7 copy-start.5
  19.0 53.7 %all-to-all-start.1 = ((f32[8,64,512]{2,1,0:T(8,128)}), f32[8,64,512]{2,1,0:T(8,128)S(1)}, u32[]{:S(2)}, u32[]{:S(2)}) async-start(f32[8,64,512]{2,1,0:T(8,128)} %get-tuple-element.10), calls=%async_computation.1 | async-start | bytes 2097152 | tf_op jit(solution)/shard_map/all_to_all | solution.py:328
  24.8 23.5 %collective-permute-start.2 = (f32[512,128]{1,0:T(8,128)S(1)}, f32[512,128]{1,0:T(8,128)S(1)}, u32[]{:S(2)}, u32[]{:S(2)}) collective-permute-start(f32[512,128]{1,0:T(8,128)S(1)} %get-tuple-element.8), channel_id=1, source_target_pairs={{0,4},{4,8},{8,12},{12,16},{16,20},{20,24},{24,28},{28,32},{32,36}... | collective-permute-start | bytes 786440 | tf_op jit(solution)/shard_map/ppermute | solution.py:324
  24.9 23.5 %collective-permute-start.3 = (f32[512,128]{1,0:T(8,128)S(1)}, f32[512,128]{1,0:T(8,128)S(1)}, u32[]{:S(2)}, u32[]{:S(2)}) collective-permute-start(f32[512,128]{1,0:T(8,128)S(1)} %get-tuple-element.8), channel_id=1, source_target_pairs={{0,124},{4,0},{8,4},{12,8},{16,12},{20,16},{24,20},{28,24},{32,28}... | collective-permute-start | bytes 786440 | tf_op jit(solution)/shard_map/ppermute | solution.py:324
  48.3 28.2 %copy-start.2 = (s32[32768]{0:T(1024)S(1)}, s32[32768]{0:T(1024)}, u32[]{:S(2)}) copy-start(s32[32768]{0:T(1024)} %param.10) | copy-start | bytes 393220
  48.3 28.2 %copy-start.3 = (f32[32768]{0:T(1024)S(1)}, f32[32768]{0:T(1024)}, u32[]{:S(2)}) copy-start(f32[32768]{0:T(1024)} %param.11) | copy-start | bytes 393220
  72.7 28.6 %all-to-all-start = ((f32[8,64,1024]{2,1,0:T(8,128)}), f32[8,64,1024]{2,1,0:T(8,128)S(1)}, u32[]{:S(2)}, u32[]{:S(2)}) async-start(f32[8,64,1024]{2,1,0:T(8,128)} %pick.1), calls=%async_computation | async-start | bytes 4194304 | tf_op jit(solution)/shard_map/all_to_all | solution.py:328
  76.5 0.9 copy-start.4
  115.8 1.0 copy-start.1
  116.8 0.8 copy-start.7
  117.6 0.8 copy-start.9
  118.4 19.2 %all-to-all-start.2 = ((f32[8,64,512]{2,1,0:T(8,128)}), f32[8,64,512]{2,1,0:T(8,128)S(1)}, u32[]{:S(2)}, u32[]{:S(2)}) async-start(f32[8,64,512]{2,1,0:T(8,128)} %bitcast.43), calls=%async_computation.2 | async-start | bytes 2097152 | tf_op jit(solution)/shard_map/all_to_all | solution.py:328
  124.0 1.9 %copy-start.6 = (f32[3,1,1,512,512]{4,3,2,1,0:T(8,128)S(1)}, f32[3,1,1,512,512]{4,3,2,1,0:T(8,128)}, u32[]{:S(2)}) copy-start(f32[3,1,1,512,512]{4,3,2,1,0:T(8,128)} %param.8) | copy-start | bytes 9437188
  125.9 1.0 copy-start.8
  126.9 1.0 copy-start.10

commit v2 on v1

v2 whole, which is shorter than its diff:
```python
import functools
import math

import jax
import jax.numpy as jnp
from jax import lax
from jax.experimental import pallas as pl
from jax.experimental.pallas import tpu as pltpu
from jax.sharding import PartitionSpec as P

GROUP = ("grp", "mem")
PARTS = 8
ROWS = 64
MEMBERS = 512
CELLS = 2048
CHUNKS = 16
CELLS_TILE = 256
STATE = 512
OBS = 1024
SLOTS = 1024
NOBS = 32768
NCELLS = 65536
TILES = 32
LOC = 512
LAGS = 3
f32 = jnp.float32
bf16 = jnp.bfloat16
VMEM = pl.BlockSpec(memory_space=pltpu.VMEM)
HBM = pl.BlockSpec(memory_space=pltpu.HBM)
SMEM = pl.BlockSpec(memory_space=pltpu.SMEM)


def params(mib):
    return pltpu.CompilerParams(vmem_limit_bytes=mib * 1024 * 1024)


def cost(flops):
    return pl.CostEstimate(flops=flops, bytes_accessed=2**20, transcendentals=0)


def halves(x):
    hi = x.astype(bf16)
    return hi, (x - hi.astype(f32)).astype(bf16)


def dot(a, b):
    return jnp.dot(a, b, preferred_element_type=f32)


def dot_nt(a, b):
    return lax.dot_general(a, b, (((1,), (1,)), ((), ())), preferred_element_type=f32)


def product(a, b):
    (ah, al), (bh, bl) = a, b
    return dot(ah, bh) + (dot(ah, bl) + dot(al, bh))


def edges_kernel(cur, depth, to_right, to_left, ends, sems):
    copies = [
        pltpu.make_async_copy(cur.at[:, pl.ds(at, 8), :], ends.at[n], sems.at[n])
        for n, at in enumerate((0, 2 * CHUNKS - 8))
    ]
    for copy in copies:
        copy.start()
    low_half = lax.broadcasted_iota(jnp.int32, (ROWS, 128), 1) < ROWS
    end = CHUNKS - 1
    to_right[ROWS:, :] = jnp.broadcast_to(depth[end : end + 1, :], (8, 128))
    to_left[ROWS:, :] = jnp.broadcast_to(depth[0:1, :], (8, 128))
    copies[1].wait()
    h, u = ends[1, :, 6, :], ends[1, :, 7, :]
    to_right[:ROWS, :] = jnp.where(low_half, pltpu.roll(h, ROWS, 1), u)
    copies[0].wait()
    h, u = ends[0, :, 0, :], ends[0, :, 1, :]
    to_left[:ROWS, :] = jnp.where(low_half, h, pltpu.roll(u, ROWS, 1))


def edges(cur, depth):
    message = jax.ShapeDtypeStruct((ROWS + 8, 128), f32)
    return pl.pallas_call(
        edges_kernel,
        out_shape=(message, message),
        in_specs=[HBM, VMEM],
        out_specs=(VMEM, VMEM),
        scratch_shapes=[pltpu.VMEM((2, ROWS, 8, 128), f32), pltpu.SemaphoreType.DMA((2,))],
        compiler_params=params(8),
        name="edges",
    )(cur, depth)


def order_kernel(where_ref, tile_list, ordered, copies, row_list, row_place):
    listed = tile_list[...]
    rel = jnp.where(listed >= 0, (listed - (where_ref[0] - 1) * OBS) & (NOBS - 1), -1)
    count = jnp.sum(jnp.where(rel >= 0, 1.0, 0.0))
    top = jnp.max(rel)
    for j in range(8):
        row_list[0:1, j * 128 : (j + 1) * 128] = rel[j : j + 1, :]
    row = row_list[0:1, :]
    chunks = 3 * OBS // 128

    def iota(shape, dim):
        return lax.broadcasted_iota(jnp.int32, shape, dim)

    def flags(x):
        return jnp.where(x, 1.0, 0.0).astype(bf16)

    in_chunk = flags((row >> 7) == iota((32, SLOTS), 0))
    in_lane = flags((row & 127) == iota((128, SLOTS), 0))
    present = dot_nt(in_chunk, in_lane).astype(bf16)
    before = dot(present, flags(iota((128, 128), 0) < iota((128, 128), 1)))
    totals = dot(present, jnp.ones((128, 128), bf16)).astype(bf16)
    place = before + dot(flags(iota((32, 32), 1) < iota((32, 32), 0)), totals)
    place = jnp.where(present.astype(f32) > 0.5, place, -1.0).astype(jnp.int32)
    for c in range(chunks):
        row_place[0:1, c * 128 : (c + 1) * 128] = place[c : c + 1, :]
    row = row_place[0:1, :]
    wide = 3 * OBS
    to_row = (row >> 7) == iota((8, wide), 0)
    number = iota((8, wide), 1)
    parts = jnp.concatenate(
        [jnp.where(to_row, number >> 7, 0), jnp.where(to_row, number & 127, 0)], axis=0
    )
    found = dot_nt(parts.astype(f32).astype(bf16), flags((row & 127) == iota((128, wide), 0)))
    found = (found[:8] * 128.0 + found[8:]).astype(jnp.int32)
    used = (iota((8, 128), 0) * 128 + iota((8, 128), 1)).astype(f32) < count
    ordered[...] = jnp.where(used, found, -1)
    filled = jnp.where(used, found, jnp.maximum(top, 0))
    for k in range(PARTS):
        copies[k] = filled


def order(where_arr, tile_list):
    return pl.pallas_call(
        order_kernel,
        out_shape=(
            jax.ShapeDtypeStruct((8, 128), jnp.int32),
            jax.ShapeDtypeStruct((PARTS, 8, 128), jnp.int32),
        ),
        in_specs=[SMEM, VMEM],
        out_specs=(VMEM, VMEM),
        scratch_shapes=[pltpu.VMEM((8, SLOTS), jnp.int32), pltpu.VMEM((8, 3 * OBS), jnp.int32)],
        cost_estimate=pl.CostEstimate(flops=0, bytes_accessed=100 * 2**20, transcendentals=0),
        compiler_params=params(12),
        name="order",
    )(where_arr, tile_list)


def take_lanes(chunk_of, chunks, index):
    at = jnp.broadcast_to(index, (8, 128))
    lane = at & 127
    chunk = at >> 7
    out = []
    for g in range(ROWS // 8):
        found = jnp.take_along_axis(chunk_of(g, 0), lane, axis=1)
        out.append(found)
    for c in range(1, chunks):
        here = chunk == c
        for g in range(ROWS // 8):
            out[g] = jnp.where(here, jnp.take_along_axis(chunk_of(g, c), lane, axis=1), out[g])
    return out


def heights_kernel(cur, depth, left, right, cells, hbuf, ubuf, own):
    lane = lax.broadcasted_iota(jnp.int32, (ROWS, 128), 1)
    first, last = lane == 0, lane == 127

    def old(c, v):
        if c < 0:
            x = left[:ROWS, :]
            return x if v else pltpu.roll(x, ROWS, 1)
        if c == CHUNKS:
            x = right[:ROWS, :]
            return pltpu.roll(x, ROWS, 1) if v else x
        return cur[pl.ds(2 * c + v, ROWS, stride=2 * CHUNKS), :]

    def scaled_depth(c):
        if c < 0:
            row = left[ROWS : ROWS + 1, :]
        elif c == CHUNKS:
            row = right[ROWS : ROWS + 1, :]
        else:
            row = depth[c : c + 1, :]
        return 0.9 * row

    def height_step(h_of, u_of):
        before = None
        for c in range(-1, CHUNKS + 1):
            u = u_of(c)
            turned = pltpu.roll(u, 1, 1)
            previous = turned if before is None else jnp.where(first, before, turned)
            before = turned
            hbuf[c + 1] = h_of(c) - scaled_depth(c) * (u - previous)

    height_step(lambda c: old(c, 0), lambda c: old(c, 1))
    turned = pltpu.roll(hbuf[0], 127, 1)
    for c in range(-1, CHUNKS + 1):
        after = pltpu.roll(hbuf[c + 2], 127, 1) if c < CHUNKS else turned
        following = jnp.where(last, after, turned)
        turned = after
        ubuf[c + 1] = old(c, 1) - 0.9 * (following - hbuf[c + 1])
    height_step(lambda c: hbuf[c + 1], lambda c: ubuf[c + 1])

    for j in range(OBS // 128):
        rows = take_lanes(lambda g, c: hbuf[c + 1, g * 8 : g * 8 + 8, :], CHUNKS, cells[j : j + 1, :])
        for g in range(ROWS // 8):
            own[g * 8 : g * 8 + 8, j * 128 : (j + 1) * 128] = rows[g]


def heights(cur, depth, left, right, cells):
    buffer = jax.ShapeDtypeStruct((CHUNKS + 2, ROWS, 128), f32)
    return pl.pallas_call(
        heights_kernel,
        out_shape=(buffer, buffer, jax.ShapeDtypeStruct((ROWS, OBS), f32)),
        in_specs=[VMEM] * 5,
        out_specs=(VMEM,) * 3,
        compiler_params=params(12),
        cost_estimate=cost(10**12),
        name="heights",
    )(cur, depth, left, right, cells)


def fields_kernel(hbuf, ubuf, fields):
    last = lax.broadcasted_iota(jnp.int32, (ROWS, 128), 1) == 127
    turned = pltpu.roll(hbuf[1], 127, 1)
    for c in range(CHUNKS):
        h = hbuf[c + 1]
        after = pltpu.roll(hbuf[c + 2], 127, 1)
        following = jnp.where(last, after, turned)
        turned = after
        at = (c % 2) * 128
        fields[c // 2, :, at : at + 128] = h
        at += CELLS_TILE
        fields[c // 2, :, at : at + 128] = ubuf[c + 1] - 0.9 * (following - h)


def fields_by_tile(hbuf, ubuf):
    return pl.pallas_call(
        fields_kernel,
        out_shape=jax.ShapeDtypeStruct((PARTS, ROWS, STATE), f32),
        in_specs=[VMEM] * 2,
        out_specs=VMEM,
        compiler_params=params(8),
        cost_estimate=cost(1000),
        name="fields",
    )(hbuf, ubuf)


def pick_kernel(bounds, lists, below, own, above, out, source):
    for n, part in enumerate((below, own, above)):
        for c in range(8):
            source[n * 8 + c] = part[:, c * 128 : (c + 1) * 128]

    def block(i, carry):
        k = i // 8
        j = i % 8
        at = jnp.broadcast_to(lists[k, pl.ds(j, 1), :], (8, 128))
        lane = at & 127
        chunk = at >> 7

        def rows(c):
            return [
                jnp.take_along_axis(source[c, g * 8 : g * 8 + 8, :], lane, axis=1)
                for g in range(ROWS // 8)
            ]

        def more(c, found):
            here = chunk == c
            return tuple(jnp.where(here, new, old) for new, old in zip(rows(c), found))

        low = bounds[k, j, 0] >> 7
        high = bounds[k, j, 127] >> 7
        found = lax.fori_loop(low + 1, high + 1, more, tuple(rows(low)))
        to = pl.ds(pl.multiple_of(j * 128, 128), 128)
        for g in range(ROWS // 8):
            out[k, g * 8 : g * 8 + 8, to] = found[g]
        return carry

    lax.fori_loop(0, PARTS * 8, block, 0)


def pick(lists, below, own, above):
    return pl.pallas_call(
        pick_kernel,
        out_shape=jax.ShapeDtypeStruct((PARTS, ROWS, SLOTS), f32),
        in_specs=[SMEM] + [VMEM] * 4,
        out_specs=VMEM,
        scratch_shapes=[pltpu.VMEM((24, ROWS, 128), f32)],
        compiler_params=params(16),
        cost_estimate=cost(10**12),
        name="pick",
    )(lists, lists, below, own, above)


def slots_kernel(where_ref, rel, values, errors, cells, out):
    tile = where_ref[0]
    center = where_ref[1]
    listed = rel[...]
    at = jnp.maximum(listed, 0)
    lane = at & 127
    chunk = at >> 7
    value = jnp.zeros((8, 128), f32)
    error = jnp.ones((8, 128), f32)
    cell = jnp.zeros((8, 128), jnp.int32)
    for n in range(3):
        t = lax.rem(tile + (TILES - 1 + n), TILES)
        for j in range(8):
            here = chunk == n * 8 + j

            def found(ref):
                row = jnp.broadcast_to(ref[t, j : j + 1, :], (8, 128))
                return jnp.take_along_axis(row, lane, axis=1)

            value = jnp.where(here, found(values), value)
            error = jnp.where(here, found(errors), error)
            cell = jnp.where(here, found(cells), cell)
    distance = jnp.abs(cell - center)
    distance = jnp.minimum(distance, NCELLS - distance).astype(f32)
    weight = jnp.exp(-0.5 * (distance / LOC) ** 2) / (error * error)
    weight = jnp.where(listed >= 0, weight, 0.0)
    for j in range(8):
        out[0:1, j * 128 : (j + 1) * 128] = weight[j : j + 1, :]
        out[1:2, j * 128 : (j + 1) * 128] = value[j : j + 1, :]


def slots(where_arr, rel, values, errors, cells):
    return pl.pallas_call(
        slots_kernel,
        out_shape=jax.ShapeDtypeStruct((8, SLOTS), f32),
        in_specs=[SMEM, VMEM, VMEM, VMEM, VMEM],
        out_specs=VMEM,
        compiler_params=params(8),
        name="slots",
    )(where_arr, rel, values, errors, cells)


def analyse_kernel(predicted, slot_rows, state, gain_hi, gain_lo, analysis, held, result, sems):
    y = predicted[...]
    weight = slot_rows[0:1, :]
    mean = jnp.sum(y, axis=0, keepdims=True) * (1.0 / MEMBERS)
    root_weight = jnp.sqrt(weight)
    spread = (y - mean) * root_weight
    departure = (slot_rows[1:2, :] - mean) * root_weight
    sh, sl = halves(spread)
    dh, dl = halves(jnp.broadcast_to(departure, (16, SLOTS)))
    rows_i = lax.broadcasted_iota(jnp.int32, (MEMBERS, MEMBERS), 0)
    cols_i = lax.broadcasted_iota(jnp.int32, (MEMBERS, MEMBERS), 1)
    eye = jnp.where(rows_i == cols_i, 1.0, 0.0)
    a = dot_nt(sh, sh) + (dot_nt(sh, sl) + dot_nt(sl, sh)) + (MEMBERS - 1.0) * eye
    innovation = (dot_nt(dh, sh) + (dot_nt(dh, sl) + dot_nt(dl, sh)))[0:1, :]
    bound = jnp.max(jnp.sum(jnp.abs(a), axis=0, keepdims=True), axis=1, keepdims=True)
    approx = a / bound

    def two_steps(m):
        mp = halves(m)
        m2 = product(mp, mp)
        q = 1.6875 * eye - 0.5625 * m + 0.0625 * m2
        return 2.25 * eye - 2.4375 * m + product(halves(m2), halves(q))

    r = halves(two_steps(approx))
    z = r
    w = halves(product(halves(approx), r))
    r = halves(two_steps(product(z, w)))
    z, w = halves(product(r, z)), halves(product(w, r))
    r = halves(two_steps(product(z, w)))
    root = product(r, z) * lax.rsqrt(bound)
    once = jnp.sum(root * innovation, axis=1, keepdims=True)
    mean_weight = jnp.sum(root * once, axis=0, keepdims=True)
    moved = math.sqrt(MEMBERS - 1) * root + mean_weight
    gain = moved + (1.0 - jnp.sum(moved, axis=1, keepdims=True)) * (1.0 / MEMBERS)
    gain = halves(gain)
    held[0], held[1] = gain
    copies = [
        pltpu.make_async_copy(held.at[0], gain_hi, sems.at[0]),
        pltpu.make_async_copy(held.at[1], gain_lo, sems.at[1]),
        pltpu.make_async_copy(result, analysis, sems.at[2]),
    ]
    copies[0].start()
    copies[1].start()
    result[...] = product(gain, halves(state[...]))
    copies[2].start()
    for copy in copies:
        copy.wait()


def analyse(predicted, slot_rows, state):
    return pl.pallas_call(
        analyse_kernel,
        out_shape=(
            pltpu.HBM((MEMBERS, MEMBERS), bf16),
            pltpu.HBM((MEMBERS, MEMBERS), bf16),
            pltpu.HBM((MEMBERS, STATE), f32),
        ),
        in_specs=[VMEM, VMEM, VMEM],
        out_specs=(HBM, HBM, HBM),
        scratch_shapes=[
            pltpu.VMEM((2, MEMBERS, MEMBERS), bf16),
            pltpu.VMEM((MEMBERS, STATE), f32),
            pltpu.SemaphoreType.DMA((3,)),
        ],
        compiler_params=params(32),
        name="analyse",
    )(predicted, slot_rows, state)


def smooth_kernel(gain_hi, gain_lo, state, out):
    out[0] = product((gain_hi[...], gain_lo[...]), halves(state[0]))


def smooth(gain_hi, gain_lo, states):
    whole = pl.BlockSpec((MEMBERS, MEMBERS), lambda i: (0, 0))
    one = pl.BlockSpec((1, MEMBERS, STATE), lambda i: (i, 0, 0))
    return pl.pallas_call(
        smooth_kernel,
        out_shape=jax.ShapeDtypeStruct((LAGS, MEMBERS, STATE), f32),
        grid=(LAGS,),
        in_specs=[whole, whole, one],
        out_specs=one,
        compiler_params=params(24),
        cost_estimate=pl.CostEstimate(
            flops=2 * 3 * LAGS * MEMBERS**2 * STATE, bytes_accessed=8 * LAGS * MEMBERS * STATE, transcendentals=0
        ),
        name="smooth",
    )(gain_hi, gain_lo, states)


def assemble_kernel(parts, out):
    for k in range(PARTS):
        for v in range(2):
            for b in range(2):
                at = v * CELLS_TILE + b * 128
                out[pl.ds(2 * (2 * k + b) + v, ROWS, stride=2 * CHUNKS), :] = parts[k, :, at : at + 128]


def assemble(parts):
    return pl.pallas_call(
        assemble_kernel,
        out_shape=jax.ShapeDtypeStruct((ROWS * 2 * CHUNKS, 128), f32),
        in_specs=[VMEM],
        out_specs=VMEM,
        compiler_params=params(24),
        name="assemble",
    )(parts)


def along_tiles(x, by):
    return lax.ppermute(x, "tile", [(i, (i + by) % TILES) for i in range(TILES)])


def exchange(x):
    return lax.all_to_all(x, GROUP, split_axis=0, concat_axis=0, tiled=True)


def per_device(
    current_state, lagged_states, water_depth, obs_cells, obs_values, obs_errors, tile_obs
):
    tile = lax.axis_index("tile")
    part = lax.axis_index("grp") * lax.axis_size("mem") + lax.axis_index("mem")
    where_arr = jnp.stack([tile, tile * CELLS + part * CELLS_TILE + CELLS_TILE // 2])
    cur = current_state.reshape(ROWS, 2, CHUNKS, 128).transpose(0, 2, 1, 3)
    depth = water_depth.reshape(CHUNKS, 128)
    whole = pltpu.with_memory_space_constraint(cur.reshape(ROWS, 2 * CHUNKS, 128), pltpu.HBM)
    to_right, to_left = edges(whole, depth)
    cur = cur.reshape(ROWS * 2 * CHUNKS, 128)
    left = along_tiles(to_right, 1)
    right = along_tiles(to_left, -1)
    to_left, where_arr = lax.optimization_barrier((to_left, where_arr))
    ordered, copies = order(where_arr, tile_obs[0, 0].reshape(8, 128))
    lists = exchange(copies)
    left, right, copies = lax.optimization_barrier((left, right, copies))
    local_cells = lax.dynamic_slice_in_dim(obs_cells, tile * OBS, OBS) - tile * CELLS
    hbuf, ubuf, own = heights(cur, depth, left, right, local_cells.reshape(8, 128))
    own, lists = lax.optimization_barrier((own, lists))
    below = along_tiles(own, 1)
    above = along_tiles(own, -1)
    state = exchange(fields_by_tile(hbuf, ubuf)).reshape(MEMBERS, STATE)
    picked = pick(lists, below, own, above)
    predicted = exchange(picked).reshape(MEMBERS, SLOTS)
    slot_rows = slots(
        where_arr,
        ordered,
        obs_values.reshape(TILES, 8, 128),
        obs_errors.reshape(TILES, 8, 128),
        obs_cells.reshape(TILES, 8, 128),
    )
    gain_hi, gain_lo, analysis = analyse(predicted, slot_rows, state)
    returned = exchange(analysis.reshape(PARTS, ROWS, STATE))
    older = smooth(gain_hi, gain_lo, lagged_states.reshape(LAGS, MEMBERS, STATE))
    analysed = assemble(returned).reshape(ROWS, CHUNKS, 2, 128).transpose(0, 2, 1, 3)
    return (
        analysed.reshape(ROWS, 2, CELLS),
        older.reshape(LAGS, 1, 1, MEMBERS, STATE),
    )


def solution(mesh):
    placed = (
        P(GROUP, None, "tile"),
        P(None, "tile", GROUP, None, None),
        P("tile"),
        P(),
        P(),
        P(),
        P("tile", GROUP, None),
    )
    return jax.shard_map(
        per_device,
        mesh=mesh,
        in_specs=placed,
        out_specs=(P(GROUP, None, "tile"), P(None, "tile", GROUP, None, None)),
        check_vma=False,
    )
```

time: 140 us -> 121 us (0.86)
  blocking collectives: 18.2 us -> 0 us
  Pallas kernels: 50.8 us -> 44.3 us
  starting transfers between devices: 29.4 us -> 35.4 us
  local copies, waits for them, and re-layouts: 10.7 us -> 8.61 us
    all_gather x1 -> x0, blocking collectives: 18.2 us -> none  [per_device(): lists = lax.all_gather(jnp.maximum(rel, 0), GROUP, axis=0)]
    pallas_call x1, Pallas kernels: 24.3 us -> 13.8 us  [pick(): pl.pallas_call(pick_kernel, out_shape=jax.ShapeDtypeStruct((PARTS, ROWS,...]
    all_to_all x3 -> x4, starting transfers between devices: 15.1 us -> 21.2 us  [exchange(): return lax.all_to_all(x, GROUP, split_axis=0, concat_axis=0, tiled=True)]
    pallas_call x2 -> x5, Pallas kernels: 19 us -> 23.9 us  [the longest x1 16.9 us: analyse(): pl.pallas_call(analyse_kernel, out_shape=(pltpu.HBM((MEMBERS, MEMBERS), b...]
    transpose x1 -> x0, local copies, waits for them, and re-layouts: 1.84 us -> none  [per_device(): by_chunk = current_state.reshape(ROWS, 2, CHUNKS, 128).transpose(0, 2, 1, 3)]
    all_to_all x3 -> x4, waiting for transfers between devices: 28 us -> 29.8 us  [exchange(): return lax.all_to_all(x, GROUP, split_axis=0, concat_axis=0, tiled=True)]
    unnamed x25 -> x26, local copies, waits for them, and re-layouts: 8.16 us -> 8.61 us
  transfers between devices with their start and end apart: 7 -> 8, of which waited for: 3 -> 3; matrix products, arithmetic and copies ran while one was open for 1% -> 1% of each run, Pallas kernels for 21% -> 20%
where the time goes in v2:
time: 121 us; the launch traced here: 120 us
  Pallas kernels  44.3 us (37%)
  starting transfers between devices  35.4 us (29%)
  waiting for transfers between devices  30 us (25%)
  local copies, waits for them, and re-layouts  8.61 us (7%)
    all_to_all x4, waiting for transfers between devices, exchange(): return lax.all_to_all(x, GROUP, split_axis=0, concat_axis=0, tiled=True)  29.8 us
    all_to_all x4, starting transfers between devices, exchange(): return lax.all_to_all(x, GROUP, split_axis=0, concat_axis=0, tiled=True)  21.2 us
    pallas_call x1, Pallas kernels, analyse(): pl.pallas_call(analyse_kernel, out_shape=(pltpu.HBM((MEMBERS, MEMBERS), b...  16.9 us
    ppermute x4, starting transfers between devices, along_tiles(): lax.ppermute(x, 'tile', [(i, (i + by) % TILES) for i in range(TILES)])  14.2 us
    pallas_call x1, Pallas kernels, pick(): pl.pallas_call(pick_kernel, out_shape=jax.ShapeDtypeStruct((PARTS, ROWS,...  13.8 us
    unnamed x26, local copies, waits for them, and re-layouts  8.61 us
    pallas_call x1, Pallas kernels, smooth(): pl.pallas_call(smooth_kernel, out_shape=jax.ShapeDtypeStruct((LAGS, MEMBE...  3.93 us
    pallas_call x1, Pallas kernels, heights(): pl.pallas_call(heights_kernel, out_shape=(buffer, buffer, jax.ShapeDtypeS...  2.53 us
  transfers between devices with their start and end apart: 8, of which 3 were waited for; matrix products, arithmetic and copies ran while one was open for 1% of the time, Pallas kernels for 20%

profile of v2, /device:TPU:1, one launch (start us, length us, event | category | flops | bytes accessed | tf_op | source)
XLA Modules:
  0.0 119.7 jit_solution(6437698763107888798)
XLA Ops:
  0.6 0.0 copy-start.5
  0.6 0.7 copy-done.5
  1.3 1.2 %edges.1 = (f32[72,128]{1,0:T(8,128)S(1)}, f32[72,128]{1,0:T(8,128)S(1)}) custom-call(f32[64,32,128]{2,1,0:T(8,128)} %bitcast.29, f32[16,128]{1,0:T(8,128)S(1)} %bitcast.34), custom_call_target="tpu_custom_call" | custom-call | tf_op jit(solution)/shard_map/edges/pallas_call | solution.py:80
  2.6 8.9 %collective-permute-start.1 = (f32[72,128]{1,0:T(8,128)S(1)}, f32[72,128]{1,0:T(8,128)S(1)}, u32[]{:S(2)}, u32[]{:S(2)}) collective-permute-start(f32[72,128]{1,0:T(8,128)S(1)} %get-tuple-element.18), channel_id=1, source_target_pairs={{0,124},{4,0},{8,4},{12,8},{16,12},{20,16},{24,20},{28,24},{32,28}... | collective-permute-start | bytes 110600 | tf_op jit(solution)/shard_map/ppermute | solution.py:446
  11.5 0.0 collective-permute-start
  11.5 0.1 pad_add_fusion.where_ref
  11.6 0.0 copy-start.8
  11.6 0.0 copy-start.7
  11.6 0.7 copy-done.7
  12.3 2.1 %order.1 = (s32[8,128]{1,0:T(8,128)S(1)}, s32[8,8,128]{2,1,0:T(8,128)}) custom-call(s32[2]{0:T(128)S(1)} %pad_add_fusion.where_ref, s32[8,128]{1,0:T(8,128)S(1)} %bitcast.36), custom_call_target="tpu_custom_call" | custom-call | bytes 104857600 | tf_op jit(solution)/shard_map/order/pallas_call | solution.py:133
  14.3 0.0 copy-done.8
  14.3 5.3 %all-to-all-start = ((s32[8,8,128]{2,1,0:T(8,128)}), s32[8,8,128]{2,1,0:T(8,128)}, u32[]{:S(2)}, u32[]{:S(2)}) async-start(s32[8,8,128]{2,1,0:T(8,128)} %get-tuple-element.20), calls=%async_computation | async-start | bytes 65536 | tf_op jit(solution)/shard_map/all_to_all | solution.py:450
  19.6 0.7 subtract_bitcast_fusion.cells
  20.3 0.0 collective-permute-done.1.right
  20.3 0.0 collective-permute-done.left
  20.3 0.0 copy-start.1
  20.3 1.2 %copy-done.1 = f32[64,2,2048]{2,1,0:T(2,128)S(1)} copy-done((f32[64,2,2048]{2,1,0:T(2,128)S(1)}, f32[64,2,2048]{2,1,0:T(2,128)}, u32[]{:S(2)}) %copy-start.1) | copy-done | bytes 1048600
  21.5 0.0 copy-start.6
  21.5 0.7 copy-done.6
  22.2 2.5 %heights.1 = (f32[18,64,128]{2,1,0:T(8,128)S(1)}, f32[18,64,128]{2,1,0:T(8,128)S(1)}, f32[64,1024]{1,0:T(8,128)S(1)}) custom-call(f32[2048,128]{1,0:T(8,128)S(1)} %bitcast.30, f32[16,128]{1,0:T(8,128)S(1)} %bitcast.35, f32[72,128]{1,0:T(8,128)S(1)} %collective-permute-done.left, f32[72,128]{1,0:T(8,128)S(1)} %collective-permute-done.1.right, ...), custom_call_target="tpu_custom_call" | custom-call | flops 999999995904 | bytes 1048576 | tf_op jit(solution)/shard_map/heights/pallas_call | solution.py:211
  24.7 0.0 all-to-all-done.bounds.lists
  24.8 0.1 collective-permute-start.2
  24.8 5.1 %collective-permute-start.3 = (f32[64,1024]{1,0:T(8,128)S(1)}, f32[64,1024]{1,0:T(8,128)S(1)}, u32[]{:S(2)}, u32[]{:S(2)}) collective-permute-start(f32[64,1024]{1,0:T(8,128)S(1)} %get-tuple-element.25.own), channel_id=1, source_target_pairs={{0,124},{4,0},{8,4},{12,8},{16,12},{20,16},{24,20},{28,24},{32,28}... | collective-permute-start | bytes 786440 | tf_op jit(solution)/shard_map/ppermute | solution.py:446
  30.0 1.2 fields.1
  31.2 5.1 %all-to-all-start.2 = ((f32[8,64,512]{2,1,0:T(8,128)}), f32[8,64,512]{2,1,0:T(8,128)}, u32[]{:S(2)}, u32[]{:S(2)}) async-start(f32[8,64,512]{2,1,0:T(8,128)} %fields.1), calls=%async_computation.2 | async-start | bytes 2097152 | tf_op jit(solution)/shard_map/all_to_all | solution.py:450
  36.3 0.2 collective-permute-done.2.below
  36.4 0.0 collective-permute-done.3.above
  36.4 13.8 %pick.1 = f32[8,64,1024]{2,1,0:T(8,128)S(1)} custom-call(s32[8,8,128]{2,1,0:T(8,128)} %all-to-all-done.bounds.lists, s32[8,8,128]{2,1,0:T(8,128)} %all-to-all-done.bounds.lists, f32[64,1024]{1,0:T(8,128)S(1)} %collective-permute-done.2.below, f32[64,1024]{1,0:T(8,128)S(1)} %get-tuple-element.25.own, f32[64,1024]{1,0:T(8,128)S(1)} %collective-permute-done.3.above), custom_call_target="tpu_custom_call" | custom-call | flops 999999995904 | bytes 1048576 | tf_op jit(solution)/shard_map/pick/pallas_call | solution.py:282
  50.2 0.0 copy-start
  50.2 1.3 %copy-done = f32[8,64,1024]{2,1,0:T(8,128)} copy-done((f32[8,64,1024]{2,1,0:T(8,128)}, f32[8,64,1024]{2,1,0:T(8,128)S(1)}, u32[]{:S(2)}) %copy-start) | copy-done | bytes 2097176
  51.5 0.0 copy-start.2
  51.5 0.0 copy-start.3
  51.5 0.0 copy-start.4
  51.5 0.0 copy-start.9
  51.6 0.0 all-to-all-done.2
  51.6 5.3 %all-to-all-start.1 = ((f32[8,64,1024]{2,1,0:T(8,128)}), f32[8,64,1024]{2,1,0:T(8,128)S(1)}, u32[]{:S(2)}, u32[]{:S(2)}) async-start(f32[8,64,1024]{2,1,0:T(8,128)} %copy-done), calls=%async_computation.1 | async-start | bytes 4194304 | tf_op jit(solution)/shard_map/all_to_all | solution.py:450
  56.9 0.0 copy-done.2
  56.9 0.0 copy-done.3
  56.9 0.0 copy-done.4
  56.9 0.0 copy-done.9
  56.9 0.7 slots.1.slot_rows
  57.6 24.1 %all-to-all-done.1 = f32[8,64,1024]{2,1,0:T(8,128)S(1)} async-done(((f32[8,64,1024]{2,1,0:T(8,128)}), f32[8,64,1024]{2,1,0:T(8,128)S(1)}, u32[]{:S(2)}, u32[]{:S(2)}) %all-to-all-start.1) | async-done | bytes 2097184 | tf_op jit(solution)/shard_map/all_to_all | solution.py:450
  81.7 16.9 %analyse.1 = (bf16[512,512]{1,0:T(8,128)(2,1)}, bf16[512,512]{1,0:T(8,128)(2,1)}, f32[512,512]{1,0:T(8,128)}) custom-call(f32[512,1024]{1,0:T(8,128)S(1)} %bitcast.28, f32[8,1024]{1,0:T(8,128)S(1)} %slots.1.slot_rows, f32[512,512]{1,0:T(8,128)} %bitcast.14.state), custom_call_target="tpu_custom_call" | custom-call | tf_op jit(solution)/shard_map/analyse/pallas_call | solution.py:386
  98.6 5.6 %all-to-all-start.3 = ((f32[8,64,512]{2,1,0:T(8,128)}), f32[8,64,512]{2,1,0:T(8,128)S(1)}, u32[]{:S(2)}, u32[]{:S(2)}) async-start(f32[8,64,512]{2,1,0:T(8,128)} %bitcast.38), calls=%async_computation.3 | async-start | bytes 2097152 | tf_op jit(solution)/shard_map/all_to_all | solution.py:450
  104.1 0.0 copy-start.10
  104.1 1.9 %copy-done.10 = f32[3,1,1,512,512]{4,3,2,1,0:T(8,128)S(1)} copy-done((f32[3,1,1,512,512]{4,3,2,1,0:T(8,128)S(1)}, f32[3,1,1,512,512]{4,3,2,1,0:T(8,128)}, u32[]{:S(2)}) %copy-start.10) | copy-done | bytes 3145752
  106.0 0.0 copy-start.11
  106.0 1.0 copy-done.11
  107.1 0.0 copy-start.12
  107.1 1.0 copy-done.12
  108.1 3.9 %smooth.1 = f32[3,512,512]{2,1,0:T(8,128)} custom-call(bf16[512,512]{1,0:T(8,128)(2,1)S(1)} %copy-done.11, bf16[512,512]{1,0:T(8,128)(2,1)S(1)} %copy-done.12, f32[3,512,512]{2,1,0:T(8,128)S(1)} %bitcast.37), custom_call_target="tpu_custom_call" | custom-call | flops 2415919104 | bytes 6291456 | tf_op jit(solution)/shard_map/smooth/pallas_call | solution.py:412
  112.0 5.7 %all-to-all-done.3.parts = f32[8,64,512]{2,1,0:T(8,128)S(1)} async-done(((f32[8,64,512]{2,1,0:T(8,128)}), f32[8,64,512]{2,1,0:T(8,128)S(1)}, u32[]{:S(2)}, u32[]{:S(2)}) %all-to-all-start.3) | async-done | bytes 1048608 | tf_op jit(solution)/shard_map/all_to_all | solution.py:450
  117.7 2.0 %assemble.1 = f32[2048,128]{1,0:T(8,128)} custom-call(f32[8,64,512]{2,1,0:T(8,128)S(1)} %all-to-all-done.3.parts), custom_call_target="tpu_custom_call" | custom-call | tf_op jit(solution)/shard_map/assemble/pallas_call | solution.py:435
Async XLA Ops:
  0.6 0.7 copy-start.5
  2.6 17.7 %collective-permute-start.1 = (f32[72,128]{1,0:T(8,128)S(1)}, f32[72,128]{1,0:T(8,128)S(1)}, u32[]{:S(2)}, u32[]{:S(2)}) collective-permute-start(f32[72,128]{1,0:T(8,128)S(1)} %get-tuple-element.18), channel_id=1, source_target_pairs={{0,124},{4,0},{8,4},{12,8},{16,12},{20,16},{24,20},{28,24},{32,28}... | collective-permute-start | bytes 110600 | tf_op jit(solution)/shard_map/ppermute | solution.py:446
  11.5 8.8 %collective-permute-start = (f32[72,128]{1,0:T(8,128)S(1)}, f32[72,128]{1,0:T(8,128)S(1)}, u32[]{:S(2)}, u32[]{:S(2)}) collective-permute-start(f32[72,128]{1,0:T(8,128)S(1)} %get-tuple-element.17), channel_id=1, source_target_pairs={{0,4},{4,8},{8,12},{12,16},{16,20},{20,24},{24,28},{28,32},{32,36}... | collective-permute-start | bytes 110600 | tf_op jit(solution)/shard_map/ppermute | solution.py:446
  11.6 2.8 %copy-start.8 = (s32[2]{0:T(128)}, s32[2]{0:T(128)S(1)}, u32[]{:S(2)}) copy-start(s32[2]{0:T(128)S(1)} %pad_add_fusion.where_ref) | copy-start | bytes 28
  11.6 0.7 copy-start.7
  14.3 10.4 %all-to-all-start = ((s32[8,8,128]{2,1,0:T(8,128)}), s32[8,8,128]{2,1,0:T(8,128)}, u32[]{:S(2)}, u32[]{:S(2)}) async-start(s32[8,8,128]{2,1,0:T(8,128)} %get-tuple-element.20), calls=%async_computation | async-start | bytes 65536 | tf_op jit(solution)/shard_map/all_to_all | solution.py:450
  20.3 1.2 %copy-start.1 = (f32[64,2,2048]{2,1,0:T(2,128)S(1)}, f32[64,2,2048]{2,1,0:T(2,128)}, u32[]{:S(2)}) copy-start(f32[64,2,2048]{2,1,0:T(2,128)} %param.7) | copy-start | bytes 3145732
  21.5 0.7 copy-start.6
  24.8 11.7 %collective-permute-start.2 = (f32[64,1024]{1,0:T(8,128)S(1)}, f32[64,1024]{1,0:T(8,128)S(1)}, u32[]{:S(2)}, u32[]{:S(2)}) collective-permute-start(f32[64,1024]{1,0:T(8,128)S(1)} %get-tuple-element.25.own), channel_id=1, source_target_pairs={{0,4},{4,8},{8,12},{12,16},{16,20},{20,24},{24,28},{28,32},{32,36}... | collective-permute-start | bytes 786440 | tf_op jit(solution)/shard_map/ppermute | solution.py:446
  24.8 11.6 %collective-permute-start.3 = (f32[64,1024]{1,0:T(8,128)S(1)}, f32[64,1024]{1,0:T(8,128)S(1)}, u32[]{:S(2)}, u32[]{:S(2)}) collective-permute-start(f32[64,1024]{1,0:T(8,128)S(1)} %get-tuple-element.25.own), channel_id=1, source_target_pairs={{0,124},{4,0},{8,4},{12,8},{16,12},{20,16},{24,20},{28,24},{32,28}... | collective-permute-start | bytes 786440 | tf_op jit(solution)/shard_map/ppermute | solution.py:446
  31.2 20.4 %all-to-all-start.2 = ((f32[8,64,512]{2,1,0:T(8,128)}), f32[8,64,512]{2,1,0:T(8,128)}, u32[]{:S(2)}, u32[]{:S(2)}) async-start(f32[8,64,512]{2,1,0:T(8,128)} %fields.1), calls=%async_computation.2 | async-start | bytes 2097152 | tf_op jit(solution)/shard_map/all_to_all | solution.py:450
  50.2 1.3 %copy-start = (f32[8,64,1024]{2,1,0:T(8,128)}, f32[8,64,1024]{2,1,0:T(8,128)S(1)}, u32[]{:S(2)}) copy-start(f32[8,64,1024]{2,1,0:T(8,128)S(1)} %pick.1) | copy-start | bytes 6291460
  51.5 5.3 %copy-start.2 = (s32[32768]{0:T(1024)S(1)}, s32[32768]{0:T(1024)}, u32[]{:S(2)}) copy-start(s32[32768]{0:T(1024)} %param.10) | copy-start | bytes 393220
  51.5 5.3 %copy-start.3 = (f32[32768]{0:T(1024)S(1)}, f32[32768]{0:T(1024)}, u32[]{:S(2)}) copy-start(f32[32768]{0:T(1024)} %param.11) | copy-start | bytes 393220
  51.5 5.3 %copy-start.4 = (f32[32768]{0:T(1024)S(1)}, f32[32768]{0:T(1024)}, u32[]{:S(2)}) copy-start(f32[32768]{0:T(1024)} %param.12) | copy-start | bytes 393220
  51.5 5.3 %copy-start.9 = (s32[2]{0:T(128)S(1)}, s32[2]{0:T(128)}, u32[]{:S(2)}) copy-start(s32[2]{0:T(128)} %copy-done.8) | copy-start | bytes 28
  51.6 30.1 %all-to-all-start.1 = ((f32[8,64,1024]{2,1,0:T(8,128)}), f32[8,64,1024]{2,1,0:T(8,128)S(1)}, u32[]{:S(2)}, u32[]{:S(2)}) async-start(f32[8,64,1024]{2,1,0:T(8,128)} %copy-done), calls=%async_computation.1 | async-start | bytes 4194304 | tf_op jit(solution)/shard_map/all_to_all | solution.py:450
  98.6 19.2 %all-to-all-start.3 = ((f32[8,64,512]{2,1,0:T(8,128)}), f32[8,64,512]{2,1,0:T(8,128)S(1)}, u32[]{:S(2)}, u32[]{:S(2)}) async-start(f32[8,64,512]{2,1,0:T(8,128)} %bitcast.38), calls=%async_computation.3 | async-start | bytes 2097152 | tf_op jit(solution)/shard_map/all_to_all | solution.py:450
  104.1 1.9 %copy-start.10 = (f32[3,1,1,512,512]{4,3,2,1,0:T(8,128)S(1)}, f32[3,1,1,512,512]{4,3,2,1,0:T(8,128)}, u32[]{:S(2)}) copy-start(f32[3,1,1,512,512]{4,3,2,1,0:T(8,128)} %param.8) | copy-start | bytes 9437188
  106.0 1.0 copy-start.11
  107.1 1.0 copy-start.12

commit v3 on v2

--- a/solution.py
+++ b/solution.py
@@ -23,6 +23,7 @@
 TILES = 32
 LOC = 512
 LAGS = 3
+DIRECT = 3
 f32 = jnp.float32
 bf16 = jnp.bfloat16
 VMEM = pl.BlockSpec(memory_space=pltpu.VMEM)
@@ -56,15 +57,17 @@
     return dot(ah, bh) + (dot(ah, bl) + dot(al, bh))
 
 
-def edges_kernel(cur, depth, to_right, to_left, ends, sems):
+def edges_kernel(cur, far_depth, to_right, to_left, ends, depth, sems):
     copies = [
         pltpu.make_async_copy(cur.at[:, pl.ds(at, 8), :], ends.at[n], sems.at[n])
         for n, at in enumerate((0, 2 * CHUNKS - 8))
     ]
+    copies.append(pltpu.make_async_copy(far_depth, depth, sems.at[2]))
     for copy in copies:
         copy.start()
     low_half = lax.broadcasted_iota(jnp.int32, (ROWS, 128), 1) < ROWS
     end = CHUNKS - 1
+    copies[2].wait()
     to_right[ROWS:, :] = jnp.broadcast_to(depth[end : end + 1, :], (8, 128))
     to_left[ROWS:, :] = jnp.broadcast_to(depth[0:1, :], (8, 128))
     copies[1].wait()
@@ -80,17 +83,34 @@
     return pl.pallas_call(
         edges_kernel,
         out_shape=(message, message),
-        in_specs=[HBM, VMEM],
+        in_specs=[HBM, HBM],
         out_specs=(VMEM, VMEM),
-        scratch_shapes=[pltpu.VMEM((2, ROWS, 8, 128), f32), pltpu.SemaphoreType.DMA((2,))],
+        scratch_shapes=[
+            pltpu.VMEM((2, ROWS, 8, 128), f32),
+            pltpu.VMEM((CHUNKS, 128), f32),
+            pltpu.SemaphoreType.DMA((3,)),
+        ],
         compiler_params=params(8),
         name="edges",
     )(cur, depth)
 
 
-def order_kernel(where_ref, tile_list, ordered, copies, row_list, row_place):
+def order_kernel(
+    far_list, far_cur, far_depth, far_cells,
+    ordered, copies, cur, depth, cells, tile_list, row_list, row_place, sems,
+):
+    tile = lax.axis_index("tile")
+    arrivals = [
+        pltpu.make_async_copy(source, target, sems.at[n])
+        for n, (source, target) in enumerate(
+            ((far_list, tile_list), (far_cells.at[tile], cells), (far_depth, depth), (far_cur, cur))
+        )
+    ]
+    for arrival in arrivals:
+        arrival.start()
+    arrivals[0].wait()
     listed = tile_list[...]
-    rel = jnp.where(listed >= 0, (listed - (where_ref[0] - 1) * OBS) & (NOBS - 1), -1)
+    rel = jnp.where(listed >= 0, (listed - (tile - 1) * OBS) & (NOBS - 1), -1)
     count = jnp.sum(jnp.where(rel >= 0, 1.0, 0.0))
     top = jnp.max(rel)
     for j in range(8):
@@ -127,22 +147,33 @@
     filled = jnp.where(used, found, jnp.maximum(top, 0))
     for k in range(PARTS):
         copies[k] = filled
-
-
-def order(where_arr, tile_list):
+    for arrival in arrivals[1:]:
+        arrival.wait()
+    cells[...] = cells[...] - tile * CELLS
+
+
+def order(tile_list, cur, depth, cells):
     return pl.pallas_call(
         order_kernel,
         out_shape=(
             jax.ShapeDtypeStruct((8, 128), jnp.int32),
             jax.ShapeDtypeStruct((PARTS, 8, 128), jnp.int32),
+            jax.ShapeDtypeStruct(cur.shape, f32),
+            jax.ShapeDtypeStruct(depth.shape, f32),
+            jax.ShapeDtypeStruct((8, 128), jnp.int32),
         ),
-        in_specs=[SMEM, VMEM],
-        out_specs=(VMEM, VMEM),
-        scratch_shapes=[pltpu.VMEM((8, SLOTS), jnp.int32), pltpu.VMEM((8, 3 * OBS), jnp.int32)],
+        in_specs=[HBM] * 4,
+        out_specs=(VMEM,) * 5,
+        scratch_shapes=[
+            pltpu.VMEM((8, 128), jnp.int32),
+            pltpu.VMEM((8, SLOTS), jnp.int32),
+            pltpu.VMEM((8, 3 * OBS), jnp.int32),
+            pltpu.SemaphoreType.DMA((4,)),
+        ],
         cost_estimate=pl.CostEstimate(flops=0, bytes_accessed=100 * 2**20, transcendentals=0),
         compiler_params=params(12),
         name="order",
-    )(where_arr, tile_list)
+    )(tile_list, cur, depth, cells)
 
 
 def take_lanes(chunk_of, chunks, index):
@@ -245,55 +276,69 @@
     )(hbuf, ubuf)
 
 
-def pick_kernel(bounds, lists, below, own, above, out, source):
+def pick_kernel(bounds, lists, below, own, above, out, source, held, sems):
     for n, part in enumerate((below, own, above)):
         for c in range(8):
             source[n * 8 + c] = part[:, c * 128 : (c + 1) * 128]
 
-    def block(i, carry):
-        k = i // 8
-        j = i % 8
-        at = jnp.broadcast_to(lists[k, pl.ds(j, 1), :], (8, 128))
-        lane = at & 127
-        chunk = at >> 7
-
-        def rows(c):
-            return [
-                jnp.take_along_axis(source[c, g * 8 : g * 8 + 8, :], lane, axis=1)
-                for g in range(ROWS // 8)
-            ]
-
-        def more(c, found):
-            here = chunk == c
-            return tuple(jnp.where(here, new, old) for new, old in zip(rows(c), found))
-
-        low = bounds[k, j, 0] >> 7
-        high = bounds[k, j, 127] >> 7
-        found = lax.fori_loop(low + 1, high + 1, more, tuple(rows(low)))
-        to = pl.ds(pl.multiple_of(j * 128, 128), 128)
-        for g in range(ROWS // 8):
-            out[k, g * 8 : g * 8 + 8, to] = found[g]
+    def send(k):
+        return pltpu.make_async_copy(held.at[k], out.at[k], sems.at[k])
+
+    def take(c, g, lane):
+        return jnp.take_along_axis(source[c, g * 8 : g * 8 + 8, :], lane, axis=1)
+
+    def one_list(k, carry):
+        blocks = []
+        for j in range(8):
+            at = jnp.broadcast_to(lists[k, j : j + 1, :], (8, 128))
+            lane, chunk = at & 127, at >> 7
+            low, high = bounds[k, j, 0] >> 7, bounds[k, j, 127] >> 7
+            blocks.append((j, lane, chunk, low, high))
+            found = [take(low, g, lane) for g in range(ROWS // 8)]
+            for d in range(1, DIRECT):
+                here = chunk == low + d
+                found = [jnp.where(here, take(low + d, g, lane), f) for g, f in enumerate(found)]
+            for g in range(ROWS // 8):
+                held[k, g * 8 : g * 8 + 8, j * 128 : (j + 1) * 128] = found[g]
+        for j, lane, chunk, low, high in blocks:
+
+            def more(c, carry):
+                here = chunk == c
+                for g in range(ROWS // 8):
+                    at = (k, slice(g * 8, g * 8 + 8), slice(j * 128, (j + 1) * 128))
+                    held[at] = jnp.where(here, take(c, g, lane), held[at])
+                return carry
+
+            lax.fori_loop(low + DIRECT, high + 1, more, 0)
+        send(k).start()
         return carry
 
-    lax.fori_loop(0, PARTS * 8, block, 0)
+    lax.fori_loop(0, PARTS, one_list, 0)
+    for k in range(PARTS):
+        send(k).wait()
 
 
 def pick(lists, below, own, above):
     return pl.pallas_call(
         pick_kernel,
-        out_shape=jax.ShapeDtypeStruct((PARTS, ROWS, SLOTS), f32),
+        out_shape=pltpu.HBM((PARTS, ROWS, SLOTS), f32),
         in_specs=[SMEM] + [VMEM] * 4,
-        out_specs=VMEM,
-        scratch_shapes=[pltpu.VMEM((24, ROWS, 128), f32)],
+        out_specs=HBM,
+        scratch_shapes=[
+            pltpu.VMEM((24 + DIRECT, ROWS, 128), f32),
+            pltpu.VMEM((PARTS, ROWS, SLOTS), f32),
+            pltpu.SemaphoreType.DMA((PARTS,)),
+        ],
         compiler_params=params(16),
         cost_estimate=cost(10**12),
         name="pick",
     )(lists, lists, below, own, above)
 
 
-def slots_kernel(where_ref, rel, values, errors, cells, out):
-    tile = where_ref[0]
-    center = where_ref[1]
+def slots_kernel(rel, values, errors, cells, out):
+    tile = lax.axis_index("tile")
+    part = lax.axis_index("grp") * lax.axis_size("mem") + lax.axis_index("mem")
+    center = tile * CELLS + part * CELLS_TILE + CELLS_TILE // 2
     listed = rel[...]
     at = jnp.maximum(listed, 0)
     lane = at & 127
@@ -322,15 +367,15 @@
         out[1:2, j * 128 : (j + 1) * 128] = value[j : j + 1, :]
 
 
-def slots(where_arr, rel, values, errors, cells):
+def slots(rel, values, errors, cells):
     return pl.pallas_call(
         slots_kernel,
         out_shape=jax.ShapeDtypeStruct((8, SLOTS), f32),
-        in_specs=[SMEM, VMEM, VMEM, VMEM, VMEM],
+        in_specs=[VMEM] * 4,
         out_specs=VMEM,
         compiler_params=params(8),
         name="slots",
-    )(where_arr, rel, values, errors, cells)
+    )(rel, values, errors, cells)
 
 
 def analyse_kernel(predicted, slot_rows, state, gain_hi, gain_lo, analysis, held, result, sems):
@@ -376,7 +421,10 @@
     ]
     copies[0].start()
     copies[1].start()
-    result[...] = product(gain, halves(state[...]))
+    analysed = product(gain, halves(state[...]))
+    for row in range(4):
+        at = (row % 2) * CELLS_TILE + (row // 2) * 128
+        result[pl.ds(row, MEMBERS, stride=4), :] = analysed[:, at : at + 128]
     copies[2].start()
     for copy in copies:
         copy.wait()
@@ -388,13 +436,13 @@
         out_shape=(
             pltpu.HBM((MEMBERS, MEMBERS), bf16),
             pltpu.HBM((MEMBERS, MEMBERS), bf16),
-            pltpu.HBM((MEMBERS, STATE), f32),
+            pltpu.HBM((MEMBERS * 4, 128), f32),
         ),
         in_specs=[VMEM, VMEM, VMEM],
         out_specs=(HBM, HBM, HBM),
         scratch_shapes=[
             pltpu.VMEM((2, MEMBERS, MEMBERS), bf16),
-            pltpu.VMEM((MEMBERS, STATE), f32),
+            pltpu.VMEM((MEMBERS * 4, 128), f32),
             pltpu.SemaphoreType.DMA((3,)),
         ],
         compiler_params=params(32),
@@ -423,27 +471,32 @@
     )(gain_hi, gain_lo, states)
 
 
-def assemble_kernel(parts, out):
-    for k in range(PARTS):
-        for v in range(2):
-            for b in range(2):
-                at = v * CELLS_TILE + b * 128
-                out[pl.ds(2 * (2 * k + b) + v, ROWS, stride=2 * CHUNKS), :] = parts[k, :, at : at + 128]
+def assemble_kernel(parts, out, sems):
+    copies = [pltpu.make_async_copy(parts.at[k], out.at[:, k], sems.at[k]) for k in range(PARTS)]
+    for copy in copies:
+        copy.start()
+    for copy in copies:
+        copy.wait()
 
 
 def assemble(parts):
     return pl.pallas_call(
         assemble_kernel,
-        out_shape=jax.ShapeDtypeStruct((ROWS * 2 * CHUNKS, 128), f32),
-        in_specs=[VMEM],
-        out_specs=VMEM,
-        compiler_params=params(24),
+        out_shape=pltpu.HBM((ROWS, PARTS, 4, 128), f32),
+        in_specs=[pl.BlockSpec(memory_space=pl.ANY)],
+        out_specs=HBM,
+        scratch_shapes=[pltpu.SemaphoreType.DMA((PARTS,))],
+        compiler_params=params(8),
         name="assemble",
     )(parts)
 
 
 def along_tiles(x, by):
     return lax.ppermute(x, "tile", [(i, (i + by) % TILES) for i in range(TILES)])
+
+
+def far(x):
+    return pltpu.with_memory_space_constraint(x, pltpu.HBM)
 
 
 def exchange(x):
@@ -453,22 +506,20 @@
 def per_device(
     current_state, lagged_states, water_depth, obs_cells, obs_values, obs_errors, tile_obs
 ):
-    tile = lax.axis_index("tile")
-    part = lax.axis_index("grp") * lax.axis_size("mem") + lax.axis_index("mem")
-    where_arr = jnp.stack([tile, tile * CELLS + part * CELLS_TILE + CELLS_TILE // 2])
     cur = current_state.reshape(ROWS, 2, CHUNKS, 128).transpose(0, 2, 1, 3)
     depth = water_depth.reshape(CHUNKS, 128)
-    whole = pltpu.with_memory_space_constraint(cur.reshape(ROWS, 2 * CHUNKS, 128), pltpu.HBM)
-    to_right, to_left = edges(whole, depth)
-    cur = cur.reshape(ROWS * 2 * CHUNKS, 128)
+    to_right, to_left = edges(far(cur.reshape(ROWS, 2 * CHUNKS, 128)), far(depth))
     left = along_tiles(to_right, 1)
     right = along_tiles(to_left, -1)
-    to_left, where_arr = lax.optimization_barrier((to_left, where_arr))
-    ordered, copies = order(where_arr, tile_obs[0, 0].reshape(8, 128))
+    to_left, listed = lax.optimization_barrier((to_left, tile_obs[0, 0].reshape(8, 128)))
+    ordered, copies, cur, depth, cells = order(
+        far(listed),
+        far(cur.reshape(ROWS * 2 * CHUNKS, 128)),
+        far(depth),
+        far(obs_cells.reshape(TILES, 8, 128)),
+    )
     lists = exchange(copies)
-    left, right, copies = lax.optimization_barrier((left, right, copies))
-    local_cells = lax.dynamic_slice_in_dim(obs_cells, tile * OBS, OBS) - tile * CELLS
-    hbuf, ubuf, own = heights(cur, depth, left, right, local_cells.reshape(8, 128))
+    hbuf, ubuf, own = heights(cur, depth, left, right, cells)
     own, lists = lax.optimization_barrier((own, lists))
     below = along_tiles(own, 1)
     above = along_tiles(own, -1)
@@ -476,16 +527,16 @@
     picked = pick(lists, below, own, above)
     predicted = exchange(picked).reshape(MEMBERS, SLOTS)
     slot_rows = slots(
-        where_arr,
         ordered,
         obs_values.reshape(TILES, 8, 128),
         obs_errors.reshape(TILES, 8, 128),
         obs_cells.reshape(TILES, 8, 128),
     )
     gain_hi, gain_lo, analysis = analyse(predicted, slot_rows, state)
-    returned = exchange(analysis.reshape(PARTS, ROWS, STATE))
+    returned = exchange(analysis.reshape(PARTS, ROWS * 4, 128))
     older = smooth(gain_hi, gain_lo, lagged_states.reshape(LAGS, MEMBERS, STATE))
-    analysed = assemble(returned).reshape(ROWS, CHUNKS, 2, 128).transpose(0, 2, 1, 3)
+    analysed = assemble(returned.reshape(PARTS, ROWS, 4, 128))
+    analysed = analysed.reshape(ROWS, CHUNKS, 2, 128).transpose(0, 2, 1, 3)
     return (
         analysed.reshape(ROWS, 2, CELLS),
         older.reshape(LAGS, 1, 1, MEMBERS, STATE),

time: 121 us -> 117 us (0.967)
  waiting for transfers between devices: 30 us -> 39.9 us
  Pallas kernels: 44.3 us -> 35.5 us
  local copies, waits for them, and re-layouts: 8.61 us -> 3.99 us
    all_to_all x4, waiting for transfers between devices: 29.8 us -> 39.9 us  [exchange(): return lax.all_to_all(x, GROUP, split_axis=0, concat_axis=0, tiled=True)]
    pallas_call x2, Pallas kernels: 15.8 us -> 7.27 us  [the longest x1 6.25 us: pick(): pl.pallas_call(pick_kernel, out_shape=pltpu.HBM((PARTS, ROWS, SLOTS), f32...]
    unnamed x26 -> x12, local copies, waits for them, and re-layouts: 8.61 us -> 3.99 us
  transfers between devices with their start and end apart: 8 -> 8, of which waited for: 3 -> 4; matrix products, arithmetic and copies ran while one was open for 1% -> 0% of each run, Pallas kernels for 20% -> 14%
where the time goes in v3:
time: 117 us; the launch traced here: 116 us
  waiting for transfers between devices  39.9 us (34%)
  starting transfers between devices  35.6 us (30%)
  Pallas kernels  35.5 us (30%)
  local copies, waits for them, and re-layouts  3.99 us (3%)
    all_to_all x4, waiting for transfers between devices, exchange(): return lax.all_to_all(x, GROUP, split_axis=0, concat_axis=0, tiled=True)  39.9 us
    all_to_all x4, starting transfers between devices, exchange(): return lax.all_to_all(x, GROUP, split_axis=0, concat_axis=0, tiled=True)  21.6 us
    pallas_call x1, Pallas kernels, analyse(): pl.pallas_call(analyse_kernel, out_shape=(pltpu.HBM((MEMBERS, MEMBERS), b...  16.9 us
    ppermute x4, starting transfers between devices, along_tiles(): lax.ppermute(x, 'tile', [(i, (i + by) % TILES) for i in range(TILES)])  14 us
    pallas_call x1, Pallas kernels, pick(): pl.pallas_call(pick_kernel, out_shape=pltpu.HBM((PARTS, ROWS, SLOTS), f32...  6.25 us
    pallas_call x1, Pallas kernels, smooth(): pl.pallas_call(smooth_kernel, out_shape=jax.ShapeDtypeStruct((LAGS, MEMBE...  4 us
    unnamed x12, local copies, waits for them, and re-layouts  3.99 us
    pallas_call x1, Pallas kernels, heights(): pl.pallas_call(heights_kernel, out_shape=(buffer, buffer, jax.ShapeDtypeS...  2.55 us
  transfers between devices with their start and end apart: 8, of which 4 were waited for; matrix products, arithmetic and copies ran while one was open for 0% of the time, Pallas kernels for 14%

profile of v3, /device:TPU:1, one launch (start us, length us, event | category | flops | bytes accessed | tf_op | source)
XLA Modules:
  0.0 115.9 jit_solution(16180773500751737676)
XLA Ops:
  0.6 1.2 %edges.1 = (f32[72,128]{1,0:T(8,128)S(1)}, f32[72,128]{1,0:T(8,128)S(1)}) custom-call(f32[64,32,128]{2,1,0:T(8,128)} %bitcast.32, f32[16,128]{1,0:T(8,128)} %bitcast.36), custom_call_target="tpu_custom_call" | custom-call | tf_op jit(solution)/shard_map/edges/pallas_call | solution.py:83
  1.9 8.9 %collective-permute-start.1 = (f32[72,128]{1,0:T(8,128)S(1)}, f32[72,128]{1,0:T(8,128)S(1)}, u32[]{:S(2)}, u32[]{:S(2)}) collective-permute-start(f32[72,128]{1,0:T(8,128)S(1)} %get-tuple-element.18), channel_id=1, source_target_pairs={{0,124},{4,0},{8,4},{12,8},{16,12},{20,16},{24,20},{28,24},{32,28}... | collective-permute-start | bytes 110600 | tf_op jit(solution)/shard_map/ppermute | solution.py:495
  10.8 0.0 collective-permute-start
  10.8 2.2 %order.1 = (s32[8,128]{1,0:T(8,128)S(1)}, s32[8,8,128]{2,1,0:T(8,128)}, f32[2048,128]{1,0:T(8,128)S(1)}, f32[16,128]{1,0:T(8,128)S(1)}, s32[8,128]{1,0:T(8,128)S(1)}) custom-call(s32[8,128]{1,0:T(8,128)} %bitcast.38, f32[2048,128]{1,0:T(8,128)} %bitcast.33, f32[16,128]{1,0:T(8,128)} %bitcast.37, s32[32,8,128]{2,1,0:T(8,128)} %bitcast.27), custom_call_target="tpu_custom_call" | custom-call | bytes 104857600 | tf_op jit(solution)/shard_map/order/pallas_call | solution.py:156
  13.1 5.3 %all-to-all-start = ((s32[8,8,128]{2,1,0:T(8,128)}), s32[8,8,128]{2,1,0:T(8,128)}, u32[]{:S(2)}, u32[]{:S(2)}) async-start(s32[8,8,128]{2,1,0:T(8,128)} %get-tuple-element.25), calls=%async_computation | async-start | bytes 65536 | tf_op jit(solution)/shard_map/all_to_all | solution.py:503
  18.3 0.0 collective-permute-done.1.right
  18.3 0.0 collective-permute-done.left
  18.3 2.5 %heights.1 = (f32[18,64,128]{2,1,0:T(8,128)S(1)}, f32[18,64,128]{2,1,0:T(8,128)S(1)}, f32[64,1024]{1,0:T(8,128)S(1)}) custom-call(f32[2048,128]{1,0:T(8,128)S(1)} %get-tuple-element.20.cur, f32[16,128]{1,0:T(8,128)S(1)} %get-tuple-element.21.depth, f32[72,128]{1,0:T(8,128)S(1)} %collective-permute-done.left, f32[72,128]{1,0:T(8,128)S(1)} %collective-permute-done.1.right, ...), custom_call_target="tpu_custom_call" | custom-call | flops 999999995904 | bytes 1048576 | tf_op jit(solution)/shard_map/heights/pallas_call | solution.py:242
  20.9 2.2 %all-to-all-done.bounds.lists = s32[8,8,128]{2,1,0:T(8,128)} async-done(((s32[8,8,128]{2,1,0:T(8,128)}), s32[8,8,128]{2,1,0:T(8,128)}, u32[]{:S(2)}, u32[]{:S(2)}) %all-to-all-start) | async-done | bytes 32800 | tf_op jit(solution)/shard_map/all_to_all | solution.py:503
  23.1 0.0 collective-permute-start.2
  23.1 5.1 %collective-permute-start.3 = (f32[64,1024]{1,0:T(8,128)S(1)}, f32[64,1024]{1,0:T(8,128)S(1)}, u32[]{:S(2)}, u32[]{:S(2)}) collective-permute-start(f32[64,1024]{1,0:T(8,128)S(1)} %get-tuple-element.27.own), channel_id=1, source_target_pairs={{0,124},{4,0},{8,4},{12,8},{16,12},{20,16},{24,20},{28,24},{32,28}... | collective-permute-start | bytes 786440 | tf_op jit(solution)/shard_map/ppermute | solution.py:495
  28.1 1.2 %fields.1 = f32[8,64,512]{2,1,0:T(8,128)} custom-call(f32[18,64,128]{2,1,0:T(8,128)S(1)} %get-tuple-element.29.hbuf, f32[18,64,128]{2,1,0:T(8,128)S(1)} %get-tuple-element.30.ubuf), custom_call_target="tpu_custom_call" | custom-call | flops 1000 | bytes 1048576 | tf_op jit(solution)/shard_map/fields/pallas_call | solution.py:268
  29.3 5.1 %all-to-all-start.2 = ((f32[8,64,512]{2,1,0:T(8,128)}), f32[8,64,512]{2,1,0:T(8,128)}, u32[]{:S(2)}, u32[]{:S(2)}) async-start(f32[8,64,512]{2,1,0:T(8,128)} %fields.1), calls=%async_computation.2 | async-start | bytes 2097152 | tf_op jit(solution)/shard_map/all_to_all | solution.py:503
  34.5 0.0 collective-permute-done.2.below
  34.5 0.0 collective-permute-done.3.above
  34.5 6.2 %pick.1 = f32[8,64,1024]{2,1,0:T(8,128)} custom-call(s32[8,8,128]{2,1,0:T(8,128)} %all-to-all-done.bounds.lists, s32[8,8,128]{2,1,0:T(8,128)} %all-to-all-done.bounds.lists, f32[64,1024]{1,0:T(8,128)S(1)} %collective-permute-done.2.below, f32[64,1024]{1,0:T(8,128)S(1)} %get-tuple-element.27.own, f32[64,1024]{1,0:T(8,128)S(1)} %collective-permute-done.3.above), custom_call_target="tpu_custom_call" | custom-call | flops 999999995904 | bytes 1048576 | tf_op jit(solution)/shard_map/pick/pallas_call | solution.py:322
  40.7 0.0 copy-start
  40.7 0.0 copy-start.1
  40.7 0.0 copy-start.2
  40.8 7.4 %all-to-all-done.2 = f32[8,64,512]{2,1,0:T(8,128)} async-done(((f32[8,64,512]{2,1,0:T(8,128)}), f32[8,64,512]{2,1,0:T(8,128)}, u32[]{:S(2)}, u32[]{:S(2)}) %all-to-all-start.2) | async-done | bytes 1048608 | tf_op jit(solution)/shard_map/all_to_all | solution.py:503
  48.2 5.6 %all-to-all-start.1 = ((f32[8,64,1024]{2,1,0:T(8,128)}), f32[8,64,1024]{2,1,0:T(8,128)S(1)}, u32[]{:S(2)}, u32[]{:S(2)}) async-start(f32[8,64,1024]{2,1,0:T(8,128)} %pick.1), calls=%async_computation.1 | async-start | bytes 4194304 | tf_op jit(solution)/shard_map/all_to_all | solution.py:503
  53.8 0.0 copy-done
  53.8 0.0 copy-done.1
  53.8 0.0 copy-done.2
  53.8 0.2 slots.1.slot_rows
  54.0 24.7 %all-to-all-done.1 = f32[8,64,1024]{2,1,0:T(8,128)S(1)} async-done(((f32[8,64,1024]{2,1,0:T(8,128)}), f32[8,64,1024]{2,1,0:T(8,128)S(1)}, u32[]{:S(2)}, u32[]{:S(2)}) %all-to-all-start.1) | async-done | bytes 2097184 | tf_op jit(solution)/shard_map/all_to_all | solution.py:503
  78.6 16.9 %analyse.1 = (bf16[512,512]{1,0:T(8,128)(2,1)}, bf16[512,512]{1,0:T(8,128)(2,1)}, f32[2048,128]{1,0:T(8,128)}) custom-call(f32[512,1024]{1,0:T(8,128)S(1)} %bitcast.25, f32[8,1024]{1,0:T(8,128)S(1)} %slots.1.slot_rows, f32[512,512]{1,0:T(8,128)} %bitcast.11.state), custom_call_target="tpu_custom_call" | custom-call | tf_op jit(solution)/shard_map/analyse/pallas_call | solution.py:434
  95.5 5.6 %all-to-all-start.3 = ((f32[8,256,128]{2,1,0:T(8,128)}), f32[8,256,128]{2,1,0:T(8,128)S(1)}, u32[]{:S(2)}, u32[]{:S(2)}) async-start(f32[8,256,128]{2,1,0:T(8,128)} %bitcast.34), calls=%async_computation.3 | async-start | bytes 2097152 | tf_op jit(solution)/shard_map/all_to_all | solution.py:503
  101.1 0.0 copy-start.3
  101.1 1.9 %copy-done.3 = f32[3,1,1,512,512]{4,3,2,1,0:T(8,128)S(1)} copy-done((f32[3,1,1,512,512]{4,3,2,1,0:T(8,128)S(1)}, f32[3,1,1,512,512]{4,3,2,1,0:T(8,128)}, u32[]{:S(2)}) %copy-start.3) | copy-done | bytes 3145752
  103.0 0.0 copy-start.4
  103.0 1.0 copy-done.4
  104.0 0.0 copy-start.5
  104.0 1.0 copy-done.5
  105.0 4.0 %smooth.1 = f32[3,512,512]{2,1,0:T(8,128)} custom-call(bf16[512,512]{1,0:T(8,128)(2,1)S(1)} %copy-done.4, bf16[512,512]{1,0:T(8,128)(2,1)S(1)} %copy-done.5, f32[3,512,512]{2,1,0:T(8,128)S(1)} %bitcast.31), custom_call_target="tpu_custom_call" | custom-call | flops 2415919104 | bytes 6291456 | tf_op jit(solution)/shard_map/smooth/pallas_call | solution.py:460
  109.0 5.6 %all-to-all-done.3 = f32[8,256,128]{2,1,0:T(8,128)S(1)} async-done(((f32[8,256,128]{2,1,0:T(8,128)}), f32[8,256,128]{2,1,0:T(8,128)S(1)}, u32[]{:S(2)}, u32[]{:S(2)}) %all-to-all-start.3) | async-done | bytes 1048608 | tf_op jit(solution)/shard_map/all_to_all | solution.py:503
  114.7 1.0 assemble.1
Async XLA Ops:
  1.9 16.5 %collective-permute-start.1 = (f32[72,128]{1,0:T(8,128)S(1)}, f32[72,128]{1,0:T(8,128)S(1)}, u32[]{:S(2)}, u32[]{:S(2)}) collective-permute-start(f32[72,128]{1,0:T(8,128)S(1)} %get-tuple-element.18), channel_id=1, source_target_pairs={{0,124},{4,0},{8,4},{12,8},{16,12},{20,16},{24,20},{28,24},{32,28}... | collective-permute-start | bytes 110600 | tf_op jit(solution)/shard_map/ppermute | solution.py:495
  10.8 7.5 %collective-permute-start = (f32[72,128]{1,0:T(8,128)S(1)}, f32[72,128]{1,0:T(8,128)S(1)}, u32[]{:S(2)}, u32[]{:S(2)}) collective-permute-start(f32[72,128]{1,0:T(8,128)S(1)} %get-tuple-element.22), channel_id=1, source_target_pairs={{0,4},{4,8},{8,12},{12,16},{16,20},{20,24},{24,28},{28,32},{32,36}... | collective-permute-start | bytes 110600 | tf_op jit(solution)/shard_map/ppermute | solution.py:495
  13.1 10.0 %all-to-all-start = ((s32[8,8,128]{2,1,0:T(8,128)}), s32[8,8,128]{2,1,0:T(8,128)}, u32[]{:S(2)}, u32[]{:S(2)}) async-start(s32[8,8,128]{2,1,0:T(8,128)} %get-tuple-element.25), calls=%async_computation | async-start | bytes 65536 | tf_op jit(solution)/shard_map/all_to_all | solution.py:503
  23.1 11.4 %collective-permute-start.2 = (f32[64,1024]{1,0:T(8,128)S(1)}, f32[64,1024]{1,0:T(8,128)S(1)}, u32[]{:S(2)}, u32[]{:S(2)}) collective-permute-start(f32[64,1024]{1,0:T(8,128)S(1)} %get-tuple-element.27.own), channel_id=1, source_target_pairs={{0,4},{4,8},{8,12},{12,16},{16,20},{20,24},{24,28},{28,32},{32,36}... | collective-permute-start | bytes 786440 | tf_op jit(solution)/shard_map/ppermute | solution.py:495
  23.1 11.4 %collective-permute-start.3 = (f32[64,1024]{1,0:T(8,128)S(1)}, f32[64,1024]{1,0:T(8,128)S(1)}, u32[]{:S(2)}, u32[]{:S(2)}) collective-permute-start(f32[64,1024]{1,0:T(8,128)S(1)} %get-tuple-element.27.own), channel_id=1, source_target_pairs={{0,124},{4,0},{8,4},{12,8},{16,12},{20,16},{24,20},{28,24},{32,28}... | collective-permute-start | bytes 786440 | tf_op jit(solution)/shard_map/ppermute | solution.py:495
  29.3 18.8 %all-to-all-start.2 = ((f32[8,64,512]{2,1,0:T(8,128)}), f32[8,64,512]{2,1,0:T(8,128)}, u32[]{:S(2)}, u32[]{:S(2)}) async-start(f32[8,64,512]{2,1,0:T(8,128)} %fields.1), calls=%async_computation.2 | async-start | bytes 2097152 | tf_op jit(solution)/shard_map/all_to_all | solution.py:503
  40.7 13.1 %copy-start = (s32[32768]{0:T(1024)S(1)}, s32[32768]{0:T(1024)}, u32[]{:S(2)}) copy-start(s32[32768]{0:T(1024)} %param.10) | copy-start | bytes 393220
  40.7 13.1 %copy-start.1 = (f32[32768]{0:T(1024)S(1)}, f32[32768]{0:T(1024)}, u32[]{:S(2)}) copy-start(f32[32768]{0:T(1024)} %param.11) | copy-start | bytes 393220
  40.7 13.0 %copy-start.2 = (f32[32768]{0:T(1024)S(1)}, f32[32768]{0:T(1024)}, u32[]{:S(2)}) copy-start(f32[32768]{0:T(1024)} %param.12) | copy-start | bytes 393220
  48.2 30.5 %all-to-all-start.1 = ((f32[8,64,1024]{2,1,0:T(8,128)}), f32[8,64,1024]{2,1,0:T(8,128)S(1)}, u32[]{:S(2)}, u32[]{:S(2)}) async-start(f32[8,64,1024]{2,1,0:T(8,128)} %pick.1), calls=%async_computation.1 | async-start | bytes 4194304 | tf_op jit(solution)/shard_map/all_to_all | solution.py:503
  95.5 19.2 %all-to-all-start.3 = ((f32[8,256,128]{2,1,0:T(8,128)}), f32[8,256,128]{2,1,0:T(8,128)S(1)}, u32[]{:S(2)}, u32[]{:S(2)}) async-start(f32[8,256,128]{2,1,0:T(8,128)} %bitcast.34), calls=%async_computation.3 | async-start | bytes 2097152 | tf_op jit(solution)/shard_map/all_to_all | solution.py:503
  101.1 1.9 %copy-start.3 = (f32[3,1,1,512,512]{4,3,2,1,0:T(8,128)S(1)}, f32[3,1,1,512,512]{4,3,2,1,0:T(8,128)}, u32[]{:S(2)}) copy-start(f32[3,1,1,512,512]{4,3,2,1,0:T(8,128)} %param.8) | copy-start | bytes 9437188
  103.0 1.0 copy-start.4
  104.0 1.0 copy-start.5

commit v4 on v3

--- a/solution.py
+++ b/solution.py
@@ -96,8 +96,8 @@
 
 
 def order_kernel(
-    far_list, far_cur, far_depth, far_cells,
-    ordered, copies, cur, depth, cells, tile_list, row_list, row_place, sems,
+    far_list, far_parts, far_cur, far_depth, far_cells,
+    ordered, payload, cur, depth, cells, tile_list, row_list, row_place, filled, sems, sent,
 ):
     tile = lax.axis_index("tile")
     arrivals = [
@@ -106,7 +106,11 @@
             ((far_list, tile_list), (far_cells.at[tile], cells), (far_depth, depth), (far_cur, cur))
         )
     ]
-    for arrival in arrivals:
+    raw = [
+        pltpu.make_async_copy(far_parts.at[:, k], payload.at[k, pl.ds(0, ROWS)], sent.at[k])
+        for k in range(PARTS)
+    ]
+    for arrival in arrivals + raw:
         arrival.start()
     arrivals[0].wait()
     listed = tile_list[...]
@@ -144,36 +148,85 @@
     found = (found[:8] * 128.0 + found[8:]).astype(jnp.int32)
     used = (iota((8, 128), 0) * 128 + iota((8, 128), 1)).astype(f32) < count
     ordered[...] = jnp.where(used, found, -1)
-    filled = jnp.where(used, found, jnp.maximum(top, 0))
-    for k in range(PARTS):
-        copies[k] = filled
-    for arrival in arrivals[1:]:
-        arrival.wait()
+    whole = jnp.where(used, found, jnp.maximum(top, 0)).astype(f32)
+    filled[0], filled[1] = whole[:4], whole[4:]
+    lists = [
+        pltpu.make_async_copy(filled, payload.at[k, pl.ds(ROWS, 2)], sent.at[PARTS + k])
+        for k in range(PARTS)
+    ]
+    for copy in lists:
+        copy.start()
+    for copy in arrivals[1:] + raw + lists:
+        copy.wait()
     cells[...] = cells[...] - tile * CELLS
 
 
-def order(tile_list, cur, depth, cells):
+def order(tile_list, parts, cur, depth, cells):
     return pl.pallas_call(
         order_kernel,
         out_shape=(
             jax.ShapeDtypeStruct((8, 128), jnp.int32),
-            jax.ShapeDtypeStruct((PARTS, 8, 128), jnp.int32),
-            jax.ShapeDtypeStruct(cur.shape, f32),
-            jax.ShapeDtypeStruct(depth.shape, f32),
+            pltpu.HBM((PARTS, ROWS + 4, 4, 128), f32),
+            jax.ShapeDtypeStruct((ROWS * 2 * CHUNKS, 128), f32),
+            jax.ShapeDtypeStruct((CHUNKS, 128), f32),
             jax.ShapeDtypeStruct((8, 128), jnp.int32),
         ),
-        in_specs=[HBM] * 4,
-        out_specs=(VMEM,) * 5,
+        in_specs=[HBM] * 5,
+        out_specs=(VMEM, HBM, VMEM, VMEM, VMEM),
         scratch_shapes=[
             pltpu.VMEM((8, 128), jnp.int32),
             pltpu.VMEM((8, SLOTS), jnp.int32),
             pltpu.VMEM((8, 3 * OBS), jnp.int32),
+            pltpu.VMEM((2, 4, 128), f32),
             pltpu.SemaphoreType.DMA((4,)),
+            pltpu.SemaphoreType.DMA((2 * PARTS,)),
         ],
         cost_estimate=pl.CostEstimate(flops=0, bytes_accessed=100 * 2**20, transcendentals=0),
         compiler_params=params(12),
         name="order",
-    )(tile_list, cur, depth, cells)
+    )(tile_list, parts, cur, depth, cells)
+
+
+def chunk_with_halo(cur, left, right, c, v):
+    if c < 0:
+        x = left[:ROWS, :]
+        return x if v else pltpu.roll(x, ROWS, 1)
+    if c == CHUNKS:
+        x = right[:ROWS, :]
+        return pltpu.roll(x, ROWS, 1) if v else x
+    return cur[pl.ds(2 * c + v, ROWS, stride=2 * CHUNKS), :]
+
+
+def beside_kernel(_, cur, left, right, payload, rows, sems):
+    def turned(c):
+        pair = [chunk_with_halo(cur, left, right, c, v) for v in range(2)]
+        return jnp.concatenate(pair, axis=0).T
+
+    upper = lax.broadcasted_iota(jnp.int32, (8, 128), 0) < 4
+    copies = []
+    for k in range(PARTS):
+        chosen = jnp.where(upper, turned(2 * k + 2)[:8], turned(2 * k - 1)[120:])
+        rows[k, 0], rows[k, 1] = chosen[:4], chosen[4:]
+        copies.append(
+            pltpu.make_async_copy(rows.at[k], payload.at[k, pl.ds(ROWS + 2, 2)], sems.at[k])
+        )
+        copies[k].start()
+    for copy in copies:
+        copy.wait()
+
+
+def with_beside(payload, cur, left, right):
+    return pl.pallas_call(
+        beside_kernel,
+        out_shape=pltpu.HBM(payload.shape, f32),
+        in_specs=[HBM, VMEM, VMEM, VMEM],
+        out_specs=HBM,
+        scratch_shapes=[pltpu.VMEM((PARTS, 2, 4, 128), f32), pltpu.SemaphoreType.DMA((PARTS,))],
+        input_output_aliases={0: 0},
+        compiler_params=params(8),
+        cost_estimate=cost(1000),
+        name="beside",
+    )(payload, cur, left, right)
 
 
 def take_lanes(chunk_of, chunks, index):
@@ -191,18 +244,12 @@
     return out
 
 
-def heights_kernel(cur, depth, left, right, cells, hbuf, ubuf, own):
+def heights_kernel(cur, depth, left, right, cells, own, hbuf, ubuf):
     lane = lax.broadcasted_iota(jnp.int32, (ROWS, 128), 1)
     first, last = lane == 0, lane == 127
 
     def old(c, v):
-        if c < 0:
-            x = left[:ROWS, :]
-            return x if v else pltpu.roll(x, ROWS, 1)
-        if c == CHUNKS:
-            x = right[:ROWS, :]
-            return pltpu.roll(x, ROWS, 1) if v else x
-        return cur[pl.ds(2 * c + v, ROWS, stride=2 * CHUNKS), :]
+        return chunk_with_halo(cur, left, right, c, v)
 
     def scaled_depth(c):
         if c < 0:
@@ -238,48 +285,94 @@
 
 
 def heights(cur, depth, left, right, cells):
-    buffer = jax.ShapeDtypeStruct((CHUNKS + 2, ROWS, 128), f32)
+    buffer = pltpu.VMEM((CHUNKS + 2, ROWS, 128), f32)
     return pl.pallas_call(
         heights_kernel,
-        out_shape=(buffer, buffer, jax.ShapeDtypeStruct((ROWS, OBS), f32)),
+        out_shape=jax.ShapeDtypeStruct((ROWS, OBS), f32),
         in_specs=[VMEM] * 5,
-        out_specs=(VMEM,) * 3,
+        out_specs=VMEM,
+        scratch_shapes=[buffer, buffer],
         compiler_params=params(12),
         cost_estimate=cost(10**12),
         name="heights",
     )(cur, depth, left, right, cells)
 
 
-def fields_kernel(hbuf, ubuf, fields):
-    last = lax.broadcasted_iota(jnp.int32, (ROWS, 128), 1) == 127
-    turned = pltpu.roll(hbuf[1], 127, 1)
-    for c in range(CHUNKS):
-        h = hbuf[c + 1]
-        after = pltpu.roll(hbuf[c + 2], 127, 1)
-        following = jnp.where(last, after, turned)
-        turned = after
-        at = (c % 2) * 128
-        fields[c // 2, :, at : at + 128] = h
-        at += CELLS_TILE
-        fields[c // 2, :, at : at + 128] = ubuf[c + 1] - 0.9 * (following - h)
-
-
-def fields_by_tile(hbuf, ubuf):
-    return pl.pallas_call(
-        fields_kernel,
-        out_shape=jax.ShapeDtypeStruct((PARTS, ROWS, STATE), f32),
-        in_specs=[VMEM] * 2,
+def forecast_kernel(received, depth, left, right, state, beside, depths):
+    part = lax.axis_index("grp") * lax.axis_size("mem") + lax.axis_index("mem")
+    depths[0:1, :] = left[ROWS : ROWS + 1, :]
+    depths[1 : CHUNKS + 1, :] = depth[...]
+    depths[CHUNKS + 1 : CHUNKS + 2, :] = right[ROWS : ROWS + 1, :]
+    scaled = [0.9 * depths[pl.ds(2 * part + i, 1), :] for i in range(4)]
+    lane = lax.broadcasted_iota(jnp.int32, (ROWS, 128), 1)
+    first, last = lane == 0, lane == 127
+    beside[...] = jnp.zeros((128, 128), f32)
+
+    def height_step(h, u, low):
+        turned = [pltpu.roll(x, 1, 1) for x in u]
+        out = list(h)
+        for i in range(low, 4):
+            previous = turned[i] if i == 0 else jnp.where(first, turned[i - 1], turned[i])
+            out[i] = h[i] - scaled[i] * (u[i] - previous)
+        return out
+
+    def speed_step(h, u, low, high):
+        turned = [pltpu.roll(x, 127, 1) for x in h]
+        out = list(u)
+        for i in range(low, high):
+            following = turned[i] if i == 3 else jnp.where(last, turned[i + 1], turned[i])
+            out[i] = u[i] - 0.9 * (following - h[i])
+        return out
+
+    for b in range(PARTS):
+        edge = received[b, 4 * ROWS + 8 : 4 * ROWS + 16, :]
+        beside[0:8, :] = edge
+        beside[120:128, :] = edge
+        turned = beside[...].T
+        own = [received[b, pl.ds(j, ROWS, stride=4), :] for j in range(4)]
+        h = [turned[:ROWS], own[0], own[2], turned[:ROWS]]
+        u = [turned[ROWS:], own[1], own[3], turned[ROWS:]]
+        h = height_step(h, u, 0)
+        u = speed_step(h, u, 0, 4)
+        h = height_step(h, u, 1)
+        u = speed_step(h, u, 1, 3)
+        for i, x in enumerate((h[1], h[2], u[1], u[2])):
+            state[b * ROWS : (b + 1) * ROWS, i * 128 : (i + 1) * 128] = x
+
+
+def forecast(received, depth, left, right):
+    return pl.pallas_call(
+        forecast_kernel,
+        out_shape=jax.ShapeDtypeStruct((MEMBERS, STATE), f32),
+        in_specs=[VMEM] * 4,
         out_specs=VMEM,
+        scratch_shapes=[pltpu.VMEM((128, 128), f32), pltpu.VMEM((24, 128), f32)],
         compiler_params=params(8),
-        cost_estimate=cost(1000),
-        name="fields",
-    )(hbuf, ubuf)
-
-
-def pick_kernel(bounds, lists, below, own, above, out, source, held, sems):
+        cost_estimate=cost(10**10),
+        name="forecast",
+    )(received, depth, left, right)
+
+
+def pick_kernel(
+    received, below, own, above, out, source, held, floats, lists, bounds, sems, list_sems
+):
+    arrivals = [
+        pltpu.make_async_copy(
+            received.at[k, pl.ds(4 * ROWS, 8), :], floats.at[k], list_sems.at[k]
+        )
+        for k in range(PARTS)
+    ]
+    for arrival in arrivals:
+        arrival.start()
+    for arrival in arrivals:
+        arrival.wait()
+    lists[...] = floats[...].astype(jnp.int32)
+    to_scalars = pltpu.make_async_copy(lists, bounds, list_sems.at[PARTS])
+    to_scalars.start()
     for n, part in enumerate((below, own, above)):
         for c in range(8):
             source[n * 8 + c] = part[:, c * 128 : (c + 1) * 128]
+    to_scalars.wait()
 
     def send(k):
         return pltpu.make_async_copy(held.at[k], out.at[k], sems.at[k])
@@ -318,21 +411,25 @@
         send(k).wait()
 
 
-def pick(lists, below, own, above):
+def pick(received, below, own, above):
     return pl.pallas_call(
         pick_kernel,
         out_shape=pltpu.HBM((PARTS, ROWS, SLOTS), f32),
-        in_specs=[SMEM] + [VMEM] * 4,
+        in_specs=[pl.BlockSpec(memory_space=pl.ANY)] + [VMEM] * 3,
         out_specs=HBM,
         scratch_shapes=[
             pltpu.VMEM((24 + DIRECT, ROWS, 128), f32),
             pltpu.VMEM((PARTS, ROWS, SLOTS), f32),
+            pltpu.VMEM((PARTS, 8, 128), f32),
+            pltpu.VMEM((PARTS, 8, 128), jnp.int32),
+            pltpu.SMEM((PARTS, 8, 128), jnp.int32),
             pltpu.SemaphoreType.DMA((PARTS,)),
+            pltpu.SemaphoreType.DMA((PARTS + 1,)),
         ],
         compiler_params=params(16),
         cost_estimate=cost(10**12),
         name="pick",
-    )(lists, lists, below, own, above)
+    )(received, below, own, above)
 
 
 def slots_kernel(rel, values, errors, cells, out):
@@ -512,20 +609,21 @@
     left = along_tiles(to_right, 1)
     right = along_tiles(to_left, -1)
     to_left, listed = lax.optimization_barrier((to_left, tile_obs[0, 0].reshape(8, 128)))
-    ordered, copies, cur, depth, cells = order(
+    ordered, payload, cur, depth, cells = order(
         far(listed),
+        far(cur.reshape(ROWS, PARTS, 4, 128)),
         far(cur.reshape(ROWS * 2 * CHUNKS, 128)),
         far(depth),
         far(obs_cells.reshape(TILES, 8, 128)),
     )
-    lists = exchange(copies)
-    hbuf, ubuf, own = heights(cur, depth, left, right, cells)
-    own, lists = lax.optimization_barrier((own, lists))
+    payload = with_beside(payload, cur, left, right)
+    received = exchange(payload.reshape(PARTS, ROWS * 4 + 16, 128))
+    own = heights(cur, depth, left, right, cells)
     below = along_tiles(own, 1)
     above = along_tiles(own, -1)
-    state = exchange(fields_by_tile(hbuf, ubuf)).reshape(MEMBERS, STATE)
-    picked = pick(lists, below, own, above)
+    picked = pick(received, below, own, above)
     predicted = exchange(picked).reshape(MEMBERS, SLOTS)
+    state = forecast(received, depth, left, right)
     slot_rows = slots(
         ordered,
         obs_values.reshape(TILES, 8, 128),

time: 117 us -> 140 us (1.20)
  Pallas kernels: 35.5 us -> 69.6 us
  starting transfers between devices: 35.6 us -> 27.4 us
  local copies, waits for them, and re-layouts: 3.99 us -> 1.94 us
    pallas_call x1, Pallas kernels: 2.25 us -> 33.1 us  [order(): pl.pallas_call(order_kernel, out_shape=(jax.ShapeDtypeStruct((8, 128), jn...]
    all_to_all x4 -> x3, waiting for transfers between devices: 39.9 us -> 28.9 us  [exchange(): return lax.all_to_all(x, GROUP, split_axis=0, concat_axis=0, tiled=True)]
    ppermute x4, waiting for transfers between devices: 0.01 us -> 10.9 us  [along_tiles(): lax.ppermute(x, 'tile', [(i, (i + by) % TILES) for i in range(TILES)])]
    all_to_all x4 -> x3, starting transfers between devices: 21.6 us -> 16.7 us  [exchange(): return lax.all_to_all(x, GROUP, split_axis=0, concat_axis=0, tiled=True)]
    pallas_call x2 -> x3, Pallas kernels: 3.74 us -> 7.25 us  [the longest x1 3.46 us: forecast(): pl.pallas_call(forecast_kernel, out_shape=jax.ShapeDtypeStruct((MEMBERS,...]
    ppermute x4, starting transfers between devices: 14 us -> 10.8 us  [along_tiles(): lax.ppermute(x, 'tile', [(i, (i + by) % TILES) for i in range(TILES)])]
    unnamed x12 -> x24, local copies, waits for them, and re-layouts: 3.99 us -> 1.94 us
  transfers between devices with their start and end apart: 8 -> 7, of which waited for: 4 -> 4; matrix products, arithmetic and copies ran while one was open for 0% -> 0% of each run, Pallas kernels for 14% -> 31%
where the time goes in v4:
time: 140 us
  Pallas kernels  69.6 us (50%)
  waiting for transfers between devices  39.9 us (28%)
  starting transfers between devices  27.4 us (20%)
  local copies, waits for them, and re-layouts  1.94 us (1%)
    pallas_call x1, Pallas kernels, order(): pl.pallas_call(order_kernel, out_shape=(jax.ShapeDtypeStruct((8, 128), jn...  33.1 us
    all_to_all x3, waiting for transfers between devices, exchange(): return lax.all_to_all(x, GROUP, split_axis=0, concat_axis=0, tiled=True)  28.9 us
    all_to_all x3, starting transfers between devices, exchange(): return lax.all_to_all(x, GROUP, split_axis=0, concat_axis=0, tiled=True)  16.7 us
    pallas_call x1, Pallas kernels, analyse(): pl.pallas_call(analyse_kernel, out_shape=(pltpu.HBM((MEMBERS, MEMBERS), b...  15.6 us
    ppermute x4, waiting for transfers between devices, along_tiles(): lax.ppermute(x, 'tile', [(i, (i + by) % TILES) for i in range(TILES)])  10.9 us
    ppermute x4, starting transfers between devices, along_tiles(): lax.ppermute(x, 'tile', [(i, (i + by) % TILES) for i in range(TILES)])  10.8 us
    pallas_call x1, Pallas kernels, pick(): pl.pallas_call(pick_kernel, out_shape=pltpu.HBM((PARTS, ROWS, SLOTS), f32...  7.3 us
    pallas_call x1, Pallas kernels, smooth(): pl.pallas_call(smooth_kernel, out_shape=jax.ShapeDtypeStruct((LAGS, MEMBE...  3.93 us
  transfers between devices with their start and end apart: 7, of which 4 were waited for; matrix products, arithmetic and copies ran while one was open for 0% of the time, Pallas kernels for 31%

profile of v4, /device:TPU:1, one launch (start us, length us, event | category | flops | bytes accessed | tf_op | source)
XLA Modules:
  0.0 139.8 jit_solution(17060162573945675725)
XLA Ops:
  0.6 1.2 edges.1
  1.9 2.5 %collective-permute-start = (f32[72,128]{1,0:T(8,128)S(1)}, f32[72,128]{1,0:T(8,128)S(1)}, u32[]{:S(2)}, u32[]{:S(2)}) collective-permute-start(f32[72,128]{1,0:T(8,128)S(1)} %get-tuple-element.17), channel_id=1, source_target_pairs={{0,4},{4,8},{8,12},{12,16},{16,20},{20,24},{24,28},{28,32},{32,36}... | collective-permute-start | bytes 110600 | tf_op jit(solution)/shard_map/ppermute | solution.py:592
  4.4 6.5 %collective-permute-start.1 = (f32[72,128]{1,0:T(8,128)S(1)}, f32[72,128]{1,0:T(8,128)S(1)}, u32[]{:S(2)}, u32[]{:S(2)}) collective-permute-start(f32[72,128]{1,0:T(8,128)S(1)} %get-tuple-element.13), channel_id=1, source_target_pairs={{0,124},{4,0},{8,4},{12,8},{16,12},{20,16},{24,20},{28,24},{32,28}... | collective-permute-start | bytes 110600 | tf_op jit(solution)/shard_map/ppermute | solution.py:592
  10.9 33.1 %order.1 = (s32[8,128]{1,0:T(8,128)S(1)}, f32[8,68,4,128]{3,2,1,0:T(4,128)}, f32[2048,128]{1,0:T(8,128)S(1)}, f32[16,128]{1,0:T(8,128)S(1)}, s32[8,128]{1,0:T(8,128)S(1)}) custom-call(s32[8,128]{1,0:T(8,128)} %bitcast.42, f32[64,8,4,128]{3,2,1,0:T(4,128)} %bitcast.35, f32[2048,128]{1,0:T(8,128)} %bitcast.36, f32[16,128]{1,0:T(8,128)} %bitcast.41, ...), custom_call_target="tpu_custom_call" | custom-call | bytes 104857600 | tf_op jit(solution)/shard_map/order/pallas_call | solution.py:165
  44.0 0.0 copy-start.10
  44.0 0.0 collective-permute-done.left
  44.0 0.0 copy-start.3
  44.0 0.0 collective-permute-done.1.right
  44.0 0.0 copy-start.5
  44.0 1.3 beside.1
  45.3 5.3 %all-to-all-start = ((f32[8,272,128]{2,1,0:T(8,128)}), f32[8,272,128]{2,1,0:T(8,128)}, u32[]{:S(2)}, u32[]{:S(2)}) async-start(f32[8,272,128]{2,1,0:T(8,128)} %bitcast.37), calls=%async_computation | async-start | bytes 2228224 | tf_op jit(solution)/shard_map/all_to_all | solution.py:600
  50.6 0.0 copy-done.10
  50.6 0.0 copy-done.3
  50.6 0.0 copy-done.5
  50.6 2.5 %heights.1.own = f32[64,1024]{1,0:T(8,128)S(1)} custom-call(f32[2048,128]{1,0:T(8,128)S(1)} %get-tuple-element.16.cur, f32[16,128]{1,0:T(8,128)S(1)} %get-tuple-element.18.depth, f32[72,128]{1,0:T(8,128)S(1)} %collective-permute-done.left, f32[72,128]{1,0:T(8,128)S(1)} %collective-permute-done.1.right, s32[8,128]{1,0:T(8,128)S(1)} %get-tuple-element.19.cells), custom_call_target="tpu_custom_call" | custom-call | flops 999999995904 | bytes 1048576 | tf_op jit(solution)/shard_map/heights/pallas_call | solution.py:289
  53.1 1.7 %collective-permute-start.3 = (f32[64,1024]{1,0:T(8,128)S(1)}, f32[64,1024]{1,0:T(8,128)S(1)}, u32[]{:S(2)}, u32[]{:S(2)}) collective-permute-start(f32[64,1024]{1,0:T(8,128)S(1)} %heights.1.own), channel_id=1, source_target_pairs={{0,124},{4,0},{8,4},{12,8},{16,12},{20,16},{24,20},{28,24},{32,28}... | collective-permute-start | bytes 786440 | tf_op jit(solution)/shard_map/ppermute | solution.py:592
  54.8 0.0 collective-permute-start.2
  54.8 6.4 %collective-permute-done.3.above = f32[64,1024]{1,0:T(8,128)S(1)} collective-permute-done((f32[64,1024]{1,0:T(8,128)S(1)}, f32[64,1024]{1,0:T(8,128)S(1)}, u32[]{:S(2)}, u32[]{:S(2)}) %collective-permute-start.3) | collective-permute-done | bytes 262176 | tf_op jit(solution)/shard_map/ppermute | solution.py:592
  61.2 4.6 %collective-permute-done.2.below = f32[64,1024]{1,0:T(8,128)S(1)} collective-permute-done((f32[64,1024]{1,0:T(8,128)S(1)}, f32[64,1024]{1,0:T(8,128)S(1)}, u32[]{:S(2)}, u32[]{:S(2)}) %collective-permute-start.2) | collective-permute-done | bytes 262176 | tf_op jit(solution)/shard_map/ppermute | solution.py:592
  65.8 0.0 all-to-all-done.received
  65.8 7.3 %pick.1 = f32[8,64,1024]{2,1,0:T(8,128)} custom-call(f32[8,272,128]{2,1,0:T(8,128)} %all-to-all-done.received, f32[64,1024]{1,0:T(8,128)S(1)} %collective-permute-done.2.below, f32[64,1024]{1,0:T(8,128)S(1)} %heights.1.own, f32[64,1024]{1,0:T(8,128)S(1)} %collective-permute-done.3.above), custom_call_target="tpu_custom_call" | custom-call | flops 999999995904 | bytes 1048576 | tf_op jit(solution)/shard_map/pick/pallas_call | solution.py:415
  73.1 0.0 copy-start
  73.1 0.0 copy-start.1
  73.1 0.0 copy-start.2
  73.1 0.0 copy-start.4
  73.1 0.0 copy-start.6
  73.1 0.0 copy-start.11
  73.1 5.7 %all-to-all-start.1 = ((f32[8,64,1024]{2,1,0:T(8,128)}), f32[8,64,1024]{2,1,0:T(8,128)S(1)}, u32[]{:S(2)}, u32[]{:S(2)}) async-start(f32[8,64,1024]{2,1,0:T(8,128)} %pick.1), calls=%async_computation.1 | async-start | bytes 4194304 | tf_op jit(solution)/shard_map/all_to_all | solution.py:600
  78.8 0.0 copy-done
  78.8 0.0 copy-done.1
  78.8 0.0 copy-done.2
  78.9 0.2 slots.1.slot_rows
  79.0 0.0 copy-done.4
  79.0 0.0 copy-done.6
  79.0 0.0 copy-done.11
  79.1 3.5 %forecast.1.state = f32[512,512]{1,0:T(8,128)S(1)} custom-call(f32[8,272,128]{2,1,0:T(8,128)} %all-to-all-done.received, f32[16,128]{1,0:T(8,128)S(1)} %copy-done.11, f32[72,128]{1,0:T(8,128)S(1)} %copy-done.4, f32[72,128]{1,0:T(8,128)S(1)} %copy-done.6), custom_call_target="tpu_custom_call" | custom-call | flops 10000000000 | bytes 1048576 | tf_op jit(solution)/shard_map/forecast/pallas_call | solution.py:344
  82.5 21.2 %all-to-all-done.1 = f32[8,64,1024]{2,1,0:T(8,128)S(1)} async-done(((f32[8,64,1024]{2,1,0:T(8,128)}), f32[8,64,1024]{2,1,0:T(8,128)S(1)}, u32[]{:S(2)}, u32[]{:S(2)}) %all-to-all-start.1) | async-done | bytes 2097184 | tf_op jit(solution)/shard_map/all_to_all | solution.py:600
  103.7 15.6 %analyse.1 = (bf16[512,512]{1,0:T(8,128)(2,1)}, bf16[512,512]{1,0:T(8,128)(2,1)}, f32[2048,128]{1,0:T(8,128)}) custom-call(f32[512,1024]{1,0:T(8,128)S(1)} %bitcast.27, f32[8,1024]{1,0:T(8,128)S(1)} %slots.1.slot_rows, f32[512,512]{1,0:T(8,128)S(1)} %forecast.1.state), custom_call_target="tpu_custom_call" | custom-call | tf_op jit(solution)/shard_map/analyse/pallas_call | solution.py:531
  119.3 0.0 copy-start.8
  119.3 0.0 copy-start.9
  119.3 5.7 %all-to-all-start.2 = ((f32[8,256,128]{2,1,0:T(8,128)}), f32[8,256,128]{2,1,0:T(8,128)S(1)}, u32[]{:S(2)}, u32[]{:S(2)}) async-start(f32[8,256,128]{2,1,0:T(8,128)} %bitcast.38), calls=%async_computation.2 | async-start | bytes 2097152 | tf_op jit(solution)/shard_map/all_to_all | solution.py:600
  125.0 0.0 copy-done.8
  125.0 0.0 copy-done.9
  125.0 0.0 copy-start.7
  125.0 1.9 %copy-done.7 = f32[3,1,1,512,512]{4,3,2,1,0:T(8,128)S(1)} copy-done((f32[3,1,1,512,512]{4,3,2,1,0:T(8,128)S(1)}, f32[3,1,1,512,512]{4,3,2,1,0:T(8,128)}, u32[]{:S(2)}) %copy-start.7) | copy-done | bytes 3145752
  126.9 3.9 %smooth.1 = f32[3,512,512]{2,1,0:T(8,128)} custom-call(bf16[512,512]{1,0:T(8,128)(2,1)S(1)} %copy-done.8, bf16[512,512]{1,0:T(8,128)(2,1)S(1)} %copy-done.9, f32[3,512,512]{2,1,0:T(8,128)S(1)} %bitcast.33), custom_call_target="tpu_custom_call" | custom-call | flops 2415919104 | bytes 6291456 | tf_op jit(solution)/shard_map/smooth/pallas_call | solution.py:557
  130.8 7.8 %all-to-all-done.2 = f32[8,256,128]{2,1,0:T(8,128)S(1)} async-done(((f32[8,256,128]{2,1,0:T(8,128)}), f32[8,256,128]{2,1,0:T(8,128)S(1)}, u32[]{:S(2)}, u32[]{:S(2)}) %all-to-all-start.2) | async-done | bytes 1048608 | tf_op jit(solution)/shard_map/all_to_all | solution.py:600
  138.6 1.0 assemble.1
Async XLA Ops:
  1.9 42.1 %collective-permute-start = (f32[72,128]{1,0:T(8,128)S(1)}, f32[72,128]{1,0:T(8,128)S(1)}, u32[]{:S(2)}, u32[]{:S(2)}) collective-permute-start(f32[72,128]{1,0:T(8,128)S(1)} %get-tuple-element.17), channel_id=1, source_target_pairs={{0,4},{4,8},{8,12},{12,16},{16,20},{20,24},{24,28},{28,32},{32,36}... | collective-permute-start | bytes 110600 | tf_op jit(solution)/shard_map/ppermute | solution.py:592
  4.4 39.6 %collective-permute-start.1 = (f32[72,128]{1,0:T(8,128)S(1)}, f32[72,128]{1,0:T(8,128)S(1)}, u32[]{:S(2)}, u32[]{:S(2)}) collective-permute-start(f32[72,128]{1,0:T(8,128)S(1)} %get-tuple-element.13), channel_id=1, source_target_pairs={{0,124},{4,0},{8,4},{12,8},{16,12},{20,16},{24,20},{28,24},{32,28}... | collective-permute-start | bytes 110600 | tf_op jit(solution)/shard_map/ppermute | solution.py:592
  44.0 6.6 %copy-start.10 = (f32[16,128]{1,0:T(8,128)}, f32[16,128]{1,0:T(8,128)S(1)}, u32[]{:S(2)}) copy-start(f32[16,128]{1,0:T(8,128)S(1)} %get-tuple-element.18.depth) | copy-start | bytes 24580
  44.0 6.6 %copy-start.3 = (f32[72,128]{1,0:T(8,128)}, f32[72,128]{1,0:T(8,128)S(1)}, u32[]{:S(2)}) copy-start(f32[72,128]{1,0:T(8,128)S(1)} %collective-permute-done.left) | copy-start | bytes 110596
  44.0 6.6 %copy-start.5 = (f32[72,128]{1,0:T(8,128)}, f32[72,128]{1,0:T(8,128)S(1)}, u32[]{:S(2)}) copy-start(f32[72,128]{1,0:T(8,128)S(1)} %collective-permute-done.1.right) | copy-start | bytes 110596
  45.3 20.5 %all-to-all-start = ((f32[8,272,128]{2,1,0:T(8,128)}), f32[8,272,128]{2,1,0:T(8,128)}, u32[]{:S(2)}, u32[]{:S(2)}) async-start(f32[8,272,128]{2,1,0:T(8,128)} %bitcast.37), calls=%async_computation | async-start | bytes 2228224 | tf_op jit(solution)/shard_map/all_to_all | solution.py:600
  53.1 8.1 %collective-permute-start.3 = (f32[64,1024]{1,0:T(8,128)S(1)}, f32[64,1024]{1,0:T(8,128)S(1)}, u32[]{:S(2)}, u32[]{:S(2)}) collective-permute-start(f32[64,1024]{1,0:T(8,128)S(1)} %heights.1.own), channel_id=1, source_target_pairs={{0,124},{4,0},{8,4},{12,8},{16,12},{20,16},{24,20},{28,24},{32,28}... | collective-permute-start | bytes 786440 | tf_op jit(solution)/shard_map/ppermute | solution.py:592
  54.8 10.9 %collective-permute-start.2 = (f32[64,1024]{1,0:T(8,128)S(1)}, f32[64,1024]{1,0:T(8,128)S(1)}, u32[]{:S(2)}, u32[]{:S(2)}) collective-permute-start(f32[64,1024]{1,0:T(8,128)S(1)} %heights.1.own), channel_id=1, source_target_pairs={{0,4},{4,8},{8,12},{12,16},{16,20},{20,24},{24,28},{28,32},{32,36}... | collective-permute-start | bytes 786440 | tf_op jit(solution)/shard_map/ppermute | solution.py:592
  73.1 5.8 %copy-start = (s32[32768]{0:T(1024)S(1)}, s32[32768]{0:T(1024)}, u32[]{:S(2)}) copy-start(s32[32768]{0:T(1024)} %param.10) | copy-start | bytes 393220
  73.1 5.8 %copy-start.1 = (f32[32768]{0:T(1024)S(1)}, f32[32768]{0:T(1024)}, u32[]{:S(2)}) copy-start(f32[32768]{0:T(1024)} %param.11) | copy-start | bytes 393220
  73.1 5.8 %copy-start.2 = (f32[32768]{0:T(1024)S(1)}, f32[32768]{0:T(1024)}, u32[]{:S(2)}) copy-start(f32[32768]{0:T(1024)} %param.12) | copy-start | bytes 393220
  73.1 5.9 %copy-start.4 = (f32[72,128]{1,0:T(8,128)S(1)}, f32[72,128]{1,0:T(8,128)}, u32[]{:S(2)}) copy-start(f32[72,128]{1,0:T(8,128)} %copy-done.3) | copy-start | bytes 110596
  73.1 5.9 %copy-start.6 = (f32[72,128]{1,0:T(8,128)S(1)}, f32[72,128]{1,0:T(8,128)}, u32[]{:S(2)}) copy-start(f32[72,128]{1,0:T(8,128)} %copy-done.5) | copy-start | bytes 110596
  73.1 5.9 %copy-start.11 = (f32[16,128]{1,0:T(8,128)S(1)}, f32[16,128]{1,0:T(8,128)}, u32[]{:S(2)}) copy-start(f32[16,128]{1,0:T(8,128)} %copy-done.10) | copy-start | bytes 24580
  73.1 30.5 %all-to-all-start.1 = ((f32[8,64,1024]{2,1,0:T(8,128)}), f32[8,64,1024]{2,1,0:T(8,128)S(1)}, u32[]{:S(2)}, u32[]{:S(2)}) async-start(f32[8,64,1024]{2,1,0:T(8,128)} %pick.1), calls=%async_computation.1 | async-start | bytes 4194304 | tf_op jit(solution)/shard_map/all_to_all | solution.py:600
  119.3 5.7 %copy-start.8 = (bf16[512,512]{1,0:T(8,128)(2,1)S(1)}, bf16[512,512]{1,0:T(8,128)(2,1)}, u32[]{:S(2)}) copy-start(bf16[512,512]{1,0:T(8,128)(2,1)} %get-tuple-element.22.gain_hi) | copy-start | bytes 1572868
  119.3 5.7 %copy-start.9 = (bf16[512,512]{1,0:T(8,128)(2,1)S(1)}, bf16[512,512]{1,0:T(8,128)(2,1)}, u32[]{:S(2)}) copy-start(bf16[512,512]{1,0:T(8,128)(2,1)} %get-tuple-element.23.gain_lo) | copy-start | bytes 1572868
  119.3 19.3 %all-to-all-start.2 = ((f32[8,256,128]{2,1,0:T(8,128)}), f32[8,256,128]{2,1,0:T(8,128)S(1)}, u32[]{:S(2)}, u32[]{:S(2)}) async-start(f32[8,256,128]{2,1,0:T(8,128)} %bitcast.38), calls=%async_computation.2 | async-start | bytes 2097152 | tf_op jit(solution)/shard_map/all_to_all | solution.py:600
  125.0 1.9 %copy-start.7 = (f32[3,1,1,512,512]{4,3,2,1,0:T(8,128)S(1)}, f32[3,1,1,512,512]{4,3,2,1,0:T(8,128)}, u32[]{:S(2)}) copy-start(f32[3,1,1,512,512]{4,3,2,1,0:T(8,128)} %param.8) | copy-start | bytes 9437188

commit v5 on v4

--- a/solution.py
+++ b/solution.py
@@ -97,22 +97,31 @@
 
 def order_kernel(
     far_list, far_parts, far_cur, far_depth, far_cells,
-    ordered, payload, cur, depth, cells, tile_list, row_list, row_place, filled, sems, sent,
+    ordered, payload, cur, depth, cells, tile_list, row_list, row_place, filled, by_part, sems, sent,
 ):
     tile = lax.axis_index("tile")
     arrivals = [
         pltpu.make_async_copy(source, target, sems.at[n])
         for n, (source, target) in enumerate(
-            ((far_list, tile_list), (far_cells.at[tile], cells), (far_depth, depth), (far_cur, cur))
+            (
+                (far_list, tile_list),
+                (far_parts, by_part),
+                (far_cells.at[tile], cells),
+                (far_depth, depth),
+                (far_cur, cur),
+            )
         )
     ]
     raw = [
-        pltpu.make_async_copy(far_parts.at[:, k], payload.at[k, pl.ds(0, ROWS)], sent.at[k])
+        pltpu.make_async_copy(by_part.at[:, k], payload.at[k, pl.ds(0, ROWS)], sent.at[k])
         for k in range(PARTS)
     ]
-    for arrival in arrivals + raw:
+    for arrival in arrivals:
         arrival.start()
     arrivals[0].wait()
+    arrivals[1].wait()
+    for copy in raw:
+        copy.start()
     listed = tile_list[...]
     rel = jnp.where(listed >= 0, (listed - (tile - 1) * OBS) & (NOBS - 1), -1)
     count = jnp.sum(jnp.where(rel >= 0, 1.0, 0.0))
@@ -156,7 +165,7 @@
     ]
     for copy in lists:
         copy.start()
-    for copy in arrivals[1:] + raw + lists:
+    for copy in arrivals[2:] + raw + lists:
         copy.wait()
     cells[...] = cells[...] - tile * CELLS
 
@@ -178,7 +187,8 @@
             pltpu.VMEM((8, SLOTS), jnp.int32),
             pltpu.VMEM((8, 3 * OBS), jnp.int32),
             pltpu.VMEM((2, 4, 128), f32),
-            pltpu.SemaphoreType.DMA((4,)),
+            pltpu.VMEM((ROWS, PARTS, 4, 128), f32),
+            pltpu.SemaphoreType.DMA((5,)),
             pltpu.SemaphoreType.DMA((2 * PARTS,)),
         ],
         cost_estimate=pl.CostEstimate(flops=0, bytes_accessed=100 * 2**20, transcendentals=0),

time: 140 us -> 112 us (0.80)
  Pallas kernels: 69.6 us -> 39.9 us
  starting transfers between devices: 27.4 us -> 29.7 us
    pallas_call x1, Pallas kernels: 33.1 us -> 2.95 us  [order(): pl.pallas_call(order_kernel, out_shape=(jax.ShapeDtypeStruct((8, 128), jn...]
    ppermute x4, starting transfers between devices: 10.8 us -> 13.1 us  [along_tiles(): lax.ppermute(x, 'tile', [(i, (i + by) % TILES) for i in range(TILES)])]
  transfers between devices with their start and end apart: 7 -> 7, of which waited for: 4 -> 4; matrix products, arithmetic and copies ran while one was open for 0% -> 0% of each run, Pallas kernels for 31% -> 12%
where the time goes in v5:
time: 112 us
  Pallas kernels  39.9 us (36%)
  waiting for transfers between devices  39.9 us (36%)
  starting transfers between devices  29.7 us (27%)
  local copies, waits for them, and re-layouts  1.94 us (2%)
    all_to_all x3, waiting for transfers between devices, exchange(): return lax.all_to_all(x, GROUP, split_axis=0, concat_axis=0, tiled=True)  28.9 us
    all_to_all x3, starting transfers between devices, exchange(): return lax.all_to_all(x, GROUP, split_axis=0, concat_axis=0, tiled=True)  16.6 us
    pallas_call x1, Pallas kernels, analyse(): pl.pallas_call(analyse_kernel, out_shape=(pltpu.HBM((MEMBERS, MEMBERS), b...  15.6 us
    ppermute x4, starting transfers between devices, along_tiles(): lax.ppermute(x, 'tile', [(i, (i + by) % TILES) for i in range(TILES)])  13.1 us
    ppermute x4, waiting for transfers between devices, along_tiles(): lax.ppermute(x, 'tile', [(i, (i + by) % TILES) for i in range(TILES)])  10.9 us
    pallas_call x1, Pallas kernels, pick(): pl.pallas_call(pick_kernel, out_shape=pltpu.HBM((PARTS, ROWS, SLOTS), f32...  7.72 us
    pallas_call x1, Pallas kernels, smooth(): pl.pallas_call(smooth_kernel, out_shape=jax.ShapeDtypeStruct((LAGS, MEMBE...  3.93 us
    pallas_call x1, Pallas kernels, forecast(): pl.pallas_call(forecast_kernel, out_shape=jax.ShapeDtypeStruct((MEMBERS,...  3.46 us
  transfers between devices with their start and end apart: 7, of which 4 were waited for; matrix products, arithmetic and copies ran while one was open for 0% of the time, Pallas kernels for 12%

profile of v5, /device:TPU:1, one launch (start us, length us, event | category | flops | bytes accessed | tf_op | source)
XLA Modules:
  0.0 112.4 jit_solution(13630694693226582027)
XLA Ops:
  0.6 1.2 %edges.1 = (f32[72,128]{1,0:T(8,128)S(1)}, f32[72,128]{1,0:T(8,128)S(1)}) custom-call(f32[64,32,128]{2,1,0:T(8,128)} %bitcast.34, f32[16,128]{1,0:T(8,128)} %bitcast.40), custom_call_target="tpu_custom_call" | custom-call | tf_op jit(solution)/shard_map/edges/pallas_call | solution.py:83
  1.9 2.5 %collective-permute-start = (f32[72,128]{1,0:T(8,128)S(1)}, f32[72,128]{1,0:T(8,128)S(1)}, u32[]{:S(2)}, u32[]{:S(2)}) collective-permute-start(f32[72,128]{1,0:T(8,128)S(1)} %get-tuple-element.17), channel_id=1, source_target_pairs={{0,4},{4,8},{8,12},{12,16},{16,20},{20,24},{24,28},{28,32},{32,36}... | collective-permute-start | bytes 110600 | tf_op jit(solution)/shard_map/ppermute | solution.py:602
  4.4 6.5 %collective-permute-start.1 = (f32[72,128]{1,0:T(8,128)S(1)}, f32[72,128]{1,0:T(8,128)S(1)}, u32[]{:S(2)}, u32[]{:S(2)}) collective-permute-start(f32[72,128]{1,0:T(8,128)S(1)} %get-tuple-element.13), channel_id=1, source_target_pairs={{0,124},{4,0},{8,4},{12,8},{16,12},{20,16},{24,20},{28,24},{32,28}... | collective-permute-start | bytes 110600 | tf_op jit(solution)/shard_map/ppermute | solution.py:602
  10.9 3.0 %order.1 = (s32[8,128]{1,0:T(8,128)S(1)}, f32[8,68,4,128]{3,2,1,0:T(4,128)}, f32[2048,128]{1,0:T(8,128)S(1)}, f32[16,128]{1,0:T(8,128)S(1)}, s32[8,128]{1,0:T(8,128)S(1)}) custom-call(s32[8,128]{1,0:T(8,128)} %bitcast.42, f32[64,8,4,128]{3,2,1,0:T(4,128)} %bitcast.35, f32[2048,128]{1,0:T(8,128)} %bitcast.36, f32[16,128]{1,0:T(8,128)} %bitcast.41, ...), custom_call_target="tpu_custom_call" | custom-call | bytes 104857600 | tf_op jit(solution)/shard_map/order/pallas_call | solution.py:174
  13.9 0.0 copy-start.10
  13.9 0.0 collective-permute-done.left
  13.9 0.0 copy-start.3
  13.9 0.0 collective-permute-done.1.right
  13.9 0.0 copy-start.5
  13.9 1.3 %beside.1 = f32[8,68,4,128]{3,2,1,0:T(4,128)} custom-call(f32[8,68,4,128]{3,2,1,0:T(4,128)} %get-tuple-element.15._, f32[2048,128]{1,0:T(8,128)S(1)} %get-tuple-element.16.cur, f32[72,128]{1,0:T(8,128)S(1)} %collective-permute-done.left, f32[72,128]{1,0:T(8,128)S(1)} %collective-permute-done.1.right), custom_call_target="tpu_custom_call", output_to_operand_aliasing={{}: (0, {})} | custom-call | flops 1000 | bytes 1048576 | tf_op jit(solution)/shard_map/beside/pallas_call | solution.py:229
  15.2 5.3 %all-to-all-start = ((f32[8,272,128]{2,1,0:T(8,128)}), f32[8,272,128]{2,1,0:T(8,128)}, u32[]{:S(2)}, u32[]{:S(2)}) async-start(f32[8,272,128]{2,1,0:T(8,128)} %bitcast.37), calls=%async_computation | async-start | bytes 2228224 | tf_op jit(solution)/shard_map/all_to_all | solution.py:610
  20.5 0.0 copy-done.10
  20.5 0.0 copy-done.3
  20.5 0.0 copy-done.5
  20.5 2.5 %heights.1.own = f32[64,1024]{1,0:T(8,128)S(1)} custom-call(f32[2048,128]{1,0:T(8,128)S(1)} %get-tuple-element.16.cur, f32[16,128]{1,0:T(8,128)S(1)} %get-tuple-element.18.depth, f32[72,128]{1,0:T(8,128)S(1)} %collective-permute-done.left, f32[72,128]{1,0:T(8,128)S(1)} %collective-permute-done.1.right, s32[8,128]{1,0:T(8,128)S(1)} %get-tuple-element.19.cells), custom_call_target="tpu_custom_call" | custom-call | flops 999999995904 | bytes 1048576 | tf_op jit(solution)/shard_map/heights/pallas_call | solution.py:299
  23.0 4.1 %collective-permute-start.3 = (f32[64,1024]{1,0:T(8,128)S(1)}, f32[64,1024]{1,0:T(8,128)S(1)}, u32[]{:S(2)}, u32[]{:S(2)}) collective-permute-start(f32[64,1024]{1,0:T(8,128)S(1)} %heights.1.own), channel_id=1, source_target_pairs={{0,124},{4,0},{8,4},{12,8},{16,12},{20,16},{24,20},{28,24},{32,28}... | collective-permute-start | bytes 786440 | tf_op jit(solution)/shard_map/ppermute | solution.py:602
  27.1 0.0 collective-permute-start.2
  27.1 5.7 %collective-permute-done.3.above = f32[64,1024]{1,0:T(8,128)S(1)} collective-permute-done((f32[64,1024]{1,0:T(8,128)S(1)}, f32[64,1024]{1,0:T(8,128)S(1)}, u32[]{:S(2)}, u32[]{:S(2)}) %collective-permute-start.3) | collective-permute-done | bytes 262176 | tf_op jit(solution)/shard_map/ppermute | solution.py:602
  32.8 5.2 %collective-permute-done.2.below = f32[64,1024]{1,0:T(8,128)S(1)} collective-permute-done((f32[64,1024]{1,0:T(8,128)S(1)}, f32[64,1024]{1,0:T(8,128)S(1)}, u32[]{:S(2)}, u32[]{:S(2)}) %collective-permute-start.2) | collective-permute-done | bytes 262176 | tf_op jit(solution)/shard_map/ppermute | solution.py:602
  38.0 0.0 all-to-all-done.received
  38.0 7.7 %pick.1 = f32[8,64,1024]{2,1,0:T(8,128)} custom-call(f32[8,272,128]{2,1,0:T(8,128)} %all-to-all-done.received, f32[64,1024]{1,0:T(8,128)S(1)} %collective-permute-done.2.below, f32[64,1024]{1,0:T(8,128)S(1)} %heights.1.own, f32[64,1024]{1,0:T(8,128)S(1)} %collective-permute-done.3.above), custom_call_target="tpu_custom_call" | custom-call | flops 999999995904 | bytes 1048576 | tf_op jit(solution)/shard_map/pick/pallas_call | solution.py:425
  45.7 0.0 copy-start
  45.7 0.0 copy-start.1
  45.7 0.0 copy-start.2
  45.8 0.0 copy-start.4
  45.8 0.0 copy-start.6
  45.8 0.0 copy-start.11
  45.8 5.7 %all-to-all-start.1 = ((f32[8,64,1024]{2,1,0:T(8,128)}), f32[8,64,1024]{2,1,0:T(8,128)S(1)}, u32[]{:S(2)}, u32[]{:S(2)}) async-start(f32[8,64,1024]{2,1,0:T(8,128)} %pick.1), calls=%async_computation.1 | async-start | bytes 4194304 | tf_op jit(solution)/shard_map/all_to_all | solution.py:610
  51.5 0.0 copy-done
  51.5 0.0 copy-done.1
  51.5 0.0 copy-done.2
  51.5 0.2 slots.1.slot_rows
  51.7 0.0 copy-done.4
  51.7 0.0 copy-done.6
  51.7 0.0 copy-done.11
  51.7 3.5 %forecast.1.state = f32[512,512]{1,0:T(8,128)S(1)} custom-call(f32[8,272,128]{2,1,0:T(8,128)} %all-to-all-done.received, f32[16,128]{1,0:T(8,128)S(1)} %copy-done.11, f32[72,128]{1,0:T(8,128)S(1)} %copy-done.4, f32[72,128]{1,0:T(8,128)S(1)} %copy-done.6), custom_call_target="tpu_custom_call" | custom-call | flops 10000000000 | bytes 1048576 | tf_op jit(solution)/shard_map/forecast/pallas_call | solution.py:354
  55.2 21.2 %all-to-all-done.1 = f32[8,64,1024]{2,1,0:T(8,128)S(1)} async-done(((f32[8,64,1024]{2,1,0:T(8,128)}), f32[8,64,1024]{2,1,0:T(8,128)S(1)}, u32[]{:S(2)}, u32[]{:S(2)}) %all-to-all-start.1) | async-done | bytes 2097184 | tf_op jit(solution)/shard_map/all_to_all | solution.py:610
  76.3 15.6 %analyse.1 = (bf16[512,512]{1,0:T(8,128)(2,1)}, bf16[512,512]{1,0:T(8,128)(2,1)}, f32[2048,128]{1,0:T(8,128)}) custom-call(f32[512,1024]{1,0:T(8,128)S(1)} %bitcast.27, f32[8,1024]{1,0:T(8,128)S(1)} %slots.1.slot_rows, f32[512,512]{1,0:T(8,128)S(1)} %forecast.1.state), custom_call_target="tpu_custom_call" | custom-call | tf_op jit(solution)/shard_map/analyse/pallas_call | solution.py:541
  91.9 0.0 copy-start.8
  91.9 0.0 copy-start.9
  91.9 5.7 %all-to-all-start.2 = ((f32[8,256,128]{2,1,0:T(8,128)}), f32[8,256,128]{2,1,0:T(8,128)S(1)}, u32[]{:S(2)}, u32[]{:S(2)}) async-start(f32[8,256,128]{2,1,0:T(8,128)} %bitcast.38), calls=%async_computation.2 | async-start | bytes 2097152 | tf_op jit(solution)/shard_map/all_to_all | solution.py:610
  97.6 0.0 copy-done.8
  97.6 0.0 copy-done.9
  97.6 0.0 copy-start.7
  97.7 1.9 %copy-done.7 = f32[3,1,1,512,512]{4,3,2,1,0:T(8,128)S(1)} copy-done((f32[3,1,1,512,512]{4,3,2,1,0:T(8,128)S(1)}, f32[3,1,1,512,512]{4,3,2,1,0:T(8,128)}, u32[]{:S(2)}) %copy-start.7) | copy-done | bytes 3145752
  99.5 3.9 %smooth.1 = f32[3,512,512]{2,1,0:T(8,128)} custom-call(bf16[512,512]{1,0:T(8,128)(2,1)S(1)} %copy-done.8, bf16[512,512]{1,0:T(8,128)(2,1)S(1)} %copy-done.9, f32[3,512,512]{2,1,0:T(8,128)S(1)} %bitcast.33), custom_call_target="tpu_custom_call" | custom-call | flops 2415919104 | bytes 6291456 | tf_op jit(solution)/shard_map/smooth/pallas_call | solution.py:567
  103.5 7.8 %all-to-all-done.2 = f32[8,256,128]{2,1,0:T(8,128)S(1)} async-done(((f32[8,256,128]{2,1,0:T(8,128)}), f32[8,256,128]{2,1,0:T(8,128)S(1)}, u32[]{:S(2)}, u32[]{:S(2)}) %all-to-all-start.2) | async-done | bytes 1048608 | tf_op jit(solution)/shard_map/all_to_all | solution.py:610
  111.2 1.0 assemble.1
Async XLA Ops:
  1.9 12.0 %collective-permute-start = (f32[72,128]{1,0:T(8,128)S(1)}, f32[72,128]{1,0:T(8,128)S(1)}, u32[]{:S(2)}, u32[]{:S(2)}) collective-permute-start(f32[72,128]{1,0:T(8,128)S(1)} %get-tuple-element.17), channel_id=1, source_target_pairs={{0,4},{4,8},{8,12},{12,16},{16,20},{20,24},{24,28},{28,32},{32,36}... | collective-permute-start | bytes 110600 | tf_op jit(solution)/shard_map/ppermute | solution.py:602
  4.4 9.5 %collective-permute-start.1 = (f32[72,128]{1,0:T(8,128)S(1)}, f32[72,128]{1,0:T(8,128)S(1)}, u32[]{:S(2)}, u32[]{:S(2)}) collective-permute-start(f32[72,128]{1,0:T(8,128)S(1)} %get-tuple-element.13), channel_id=1, source_target_pairs={{0,124},{4,0},{8,4},{12,8},{16,12},{20,16},{24,20},{28,24},{32,28}... | collective-permute-start | bytes 110600 | tf_op jit(solution)/shard_map/ppermute | solution.py:602
  13.9 6.6 %copy-start.10 = (f32[16,128]{1,0:T(8,128)}, f32[16,128]{1,0:T(8,128)S(1)}, u32[]{:S(2)}) copy-start(f32[16,128]{1,0:T(8,128)S(1)} %get-tuple-element.18.depth) | copy-start | bytes 24580
  13.9 6.6 %copy-start.3 = (f32[72,128]{1,0:T(8,128)}, f32[72,128]{1,0:T(8,128)S(1)}, u32[]{:S(2)}) copy-start(f32[72,128]{1,0:T(8,128)S(1)} %collective-permute-done.left) | copy-start | bytes 110596
  13.9 6.6 %copy-start.5 = (f32[72,128]{1,0:T(8,128)}, f32[72,128]{1,0:T(8,128)S(1)}, u32[]{:S(2)}) copy-start(f32[72,128]{1,0:T(8,128)S(1)} %collective-permute-done.1.right) | copy-start | bytes 110596
  15.2 22.8 %all-to-all-start = ((f32[8,272,128]{2,1,0:T(8,128)}), f32[8,272,128]{2,1,0:T(8,128)}, u32[]{:S(2)}, u32[]{:S(2)}) async-start(f32[8,272,128]{2,1,0:T(8,128)} %bitcast.37), calls=%async_computation | async-start | bytes 2228224 | tf_op jit(solution)/shard_map/all_to_all | solution.py:610
  23.0 9.8 %collective-permute-start.3 = (f32[64,1024]{1,0:T(8,128)S(1)}, f32[64,1024]{1,0:T(8,128)S(1)}, u32[]{:S(2)}, u32[]{:S(2)}) collective-permute-start(f32[64,1024]{1,0:T(8,128)S(1)} %heights.1.own), channel_id=1, source_target_pairs={{0,124},{4,0},{8,4},{12,8},{16,12},{20,16},{24,20},{28,24},{32,28}... | collective-permute-start | bytes 786440 | tf_op jit(solution)/shard_map/ppermute | solution.py:602
  27.1 10.9 %collective-permute-start.2 = (f32[64,1024]{1,0:T(8,128)S(1)}, f32[64,1024]{1,0:T(8,128)S(1)}, u32[]{:S(2)}, u32[]{:S(2)}) collective-permute-start(f32[64,1024]{1,0:T(8,128)S(1)} %heights.1.own), channel_id=1, source_target_pairs={{0,4},{4,8},{8,12},{12,16},{16,20},{20,24},{24,28},{28,32},{32,36}... | collective-permute-start | bytes 786440 | tf_op jit(solution)/shard_map/ppermute | solution.py:602
  45.7 5.8 %copy-start = (s32[32768]{0:T(1024)S(1)}, s32[32768]{0:T(1024)}, u32[]{:S(2)}) copy-start(s32[32768]{0:T(1024)} %param.10) | copy-start | bytes 393220
  45.7 5.8 %copy-start.1 = (f32[32768]{0:T(1024)S(1)}, f32[32768]{0:T(1024)}, u32[]{:S(2)}) copy-start(f32[32768]{0:T(1024)} %param.11) | copy-start | bytes 393220
  45.7 5.8 %copy-start.2 = (f32[32768]{0:T(1024)S(1)}, f32[32768]{0:T(1024)}, u32[]{:S(2)}) copy-start(f32[32768]{0:T(1024)} %param.12) | copy-start | bytes 393220
  45.8 5.9 %copy-start.4 = (f32[72,128]{1,0:T(8,128)S(1)}, f32[72,128]{1,0:T(8,128)}, u32[]{:S(2)}) copy-start(f32[72,128]{1,0:T(8,128)} %copy-done.3) | copy-start | bytes 110596
  45.8 5.9 %copy-start.6 = (f32[72,128]{1,0:T(8,128)S(1)}, f32[72,128]{1,0:T(8,128)}, u32[]{:S(2)}) copy-start(f32[72,128]{1,0:T(8,128)} %copy-done.5) | copy-start | bytes 110596
  45.8 5.9 %copy-start.11 = (f32[16,128]{1,0:T(8,128)S(1)}, f32[16,128]{1,0:T(8,128)}, u32[]{:S(2)}) copy-start(f32[16,128]{1,0:T(8,128)} %copy-done.10) | copy-start | bytes 24580
  45.8 30.5 %all-to-all-start.1 = ((f32[8,64,1024]{2,1,0:T(8,128)}), f32[8,64,1024]{2,1,0:T(8,128)S(1)}, u32[]{:S(2)}, u32[]{:S(2)}) async-start(f32[8,64,1024]{2,1,0:T(8,128)} %pick.1), calls=%async_computation.1 | async-start | bytes 4194304 | tf_op jit(solution)/shard_map/all_to_all | solution.py:610
  91.9 5.7 %copy-start.8 = (bf16[512,512]{1,0:T(8,128)(2,1)S(1)}, bf16[512,512]{1,0:T(8,128)(2,1)}, u32[]{:S(2)}) copy-start(bf16[512,512]{1,0:T(8,128)(2,1)} %get-tuple-element.22.gain_hi) | copy-start | bytes 1572868
  91.9 5.7 %copy-start.9 = (bf16[512,512]{1,0:T(8,128)(2,1)S(1)}, bf16[512,512]{1,0:T(8,128)(2,1)}, u32[]{:S(2)}) copy-start(bf16[512,512]{1,0:T(8,128)(2,1)} %get-tuple-element.23.gain_lo) | copy-start | bytes 1572868
  91.9 19.3 %all-to-all-start.2 = ((f32[8,256,128]{2,1,0:T(8,128)}), f32[8,256,128]{2,1,0:T(8,128)S(1)}, u32[]{:S(2)}, u32[]{:S(2)}) async-start(f32[8,256,128]{2,1,0:T(8,128)} %bitcast.38), calls=%async_computation.2 | async-start | bytes 2097152 | tf_op jit(solution)/shard_map/all_to_all | solution.py:610
  97.6 1.9 %copy-start.7 = (f32[3,1,1,512,512]{4,3,2,1,0:T(8,128)S(1)}, f32[3,1,1,512,512]{4,3,2,1,0:T(8,128)}, u32[]{:S(2)}) copy-start(f32[3,1,1,512,512]{4,3,2,1,0:T(8,128)} %param.8) | copy-start | bytes 9437188

commit v6 on v4

--- a/solution.py
+++ b/solution.py
@@ -23,7 +23,7 @@
 TILES = 32
 LOC = 512
 LAGS = 3
-DIRECT = 3
+DIRECT = 4
 f32 = jnp.float32
 bf16 = jnp.bfloat16
 VMEM = pl.BlockSpec(memory_space=pltpu.VMEM)
@@ -57,61 +57,57 @@
     return dot(ah, bh) + (dot(ah, bl) + dot(al, bh))
 
 
-def edges_kernel(cur, far_depth, to_right, to_left, ends, depth, sems):
-    copies = [
-        pltpu.make_async_copy(cur.at[:, pl.ds(at, 8), :], ends.at[n], sems.at[n])
-        for n, at in enumerate((0, 2 * CHUNKS - 8))
+def edges_kernel(far_cur, far_depth, cur, to_right, to_left, depth, sems):
+    arrivals = [
+        pltpu.make_async_copy(far_cur, cur, sems.at[0]),
+        pltpu.make_async_copy(far_depth, depth, sems.at[1]),
     ]
-    copies.append(pltpu.make_async_copy(far_depth, depth, sems.at[2]))
-    for copy in copies:
-        copy.start()
+    for arrival in arrivals:
+        arrival.start()
     low_half = lax.broadcasted_iota(jnp.int32, (ROWS, 128), 1) < ROWS
     end = CHUNKS - 1
-    copies[2].wait()
+    arrivals[1].wait()
     to_right[ROWS:, :] = jnp.broadcast_to(depth[end : end + 1, :], (8, 128))
     to_left[ROWS:, :] = jnp.broadcast_to(depth[0:1, :], (8, 128))
-    copies[1].wait()
-    h, u = ends[1, :, 6, :], ends[1, :, 7, :]
-    to_right[:ROWS, :] = jnp.where(low_half, pltpu.roll(h, ROWS, 1), u)
-    copies[0].wait()
-    h, u = ends[0, :, 0, :], ends[0, :, 1, :]
-    to_left[:ROWS, :] = jnp.where(low_half, h, pltpu.roll(u, ROWS, 1))
+    arrivals[0].wait()
+
+    def old(c, v):
+        return cur[pl.ds(2 * c + v, ROWS, stride=2 * CHUNKS), :]
+
+    to_right[:ROWS, :] = jnp.where(low_half, pltpu.roll(old(end, 0), ROWS, 1), old(end, 1))
+    to_left[:ROWS, :] = jnp.where(low_half, old(0, 0), pltpu.roll(old(0, 1), ROWS, 1))
 
 
 def edges(cur, depth):
     message = jax.ShapeDtypeStruct((ROWS + 8, 128), f32)
     return pl.pallas_call(
         edges_kernel,
-        out_shape=(message, message),
+        out_shape=(jax.ShapeDtypeStruct(cur.shape, f32), message, message),
         in_specs=[HBM, HBM],
-        out_specs=(VMEM, VMEM),
-        scratch_shapes=[
-            pltpu.VMEM((2, ROWS, 8, 128), f32),
-            pltpu.VMEM((CHUNKS, 128), f32),
-            pltpu.SemaphoreType.DMA((3,)),
-        ],
+        out_specs=(VMEM, VMEM, VMEM),
+        scratch_shapes=[pltpu.VMEM((CHUNKS, 128), f32), pltpu.SemaphoreType.DMA((2,))],
         compiler_params=params(8),
         name="edges",
     )(cur, depth)
 
 
 def order_kernel(
-    far_list, far_parts, far_cur, far_depth, far_cells,
-    ordered, payload, cur, depth, cells, tile_list, row_list, row_place, filled, sems, sent,
+    far_list, by_part, far_depth, far_cells,
+    ordered, payload, depth, cells, tile_list, row_list, row_place, filled, sems, sent,
 ):
     tile = lax.axis_index("tile")
     arrivals = [
         pltpu.make_async_copy(source, target, sems.at[n])
         for n, (source, target) in enumerate(
-            ((far_list, tile_list), (far_cells.at[tile], cells), (far_depth, depth), (far_cur, cur))
+            ((far_list, tile_list), (far_cells.at[tile], cells), (far_depth, depth))
         )
     ]
     raw = [
-        pltpu.make_async_copy(far_parts.at[:, k], payload.at[k, pl.ds(0, ROWS)], sent.at[k])
+        pltpu.make_async_copy(by_part.at[:, k], payload.at[k, pl.ds(0, ROWS)], sent.at[k])
         for k in range(PARTS)
     ]
-    for arrival in arrivals + raw:
-        arrival.start()
+    for copy in arrivals + raw:
+        copy.start()
     arrivals[0].wait()
     listed = tile_list[...]
     rel = jnp.where(listed >= 0, (listed - (tile - 1) * OBS) & (NOBS - 1), -1)
@@ -161,30 +157,29 @@
     cells[...] = cells[...] - tile * CELLS
 
 
-def order(tile_list, parts, cur, depth, cells):
+def order(tile_list, parts, depth, cells):
     return pl.pallas_call(
         order_kernel,
         out_shape=(
             jax.ShapeDtypeStruct((8, 128), jnp.int32),
             pltpu.HBM((PARTS, ROWS + 4, 4, 128), f32),
-            jax.ShapeDtypeStruct((ROWS * 2 * CHUNKS, 128), f32),
             jax.ShapeDtypeStruct((CHUNKS, 128), f32),
             jax.ShapeDtypeStruct((8, 128), jnp.int32),
         ),
-        in_specs=[HBM] * 5,
-        out_specs=(VMEM, HBM, VMEM, VMEM, VMEM),
+        in_specs=[HBM, VMEM, HBM, HBM],
+        out_specs=(VMEM, HBM, VMEM, VMEM),
         scratch_shapes=[
             pltpu.VMEM((8, 128), jnp.int32),
             pltpu.VMEM((8, SLOTS), jnp.int32),
             pltpu.VMEM((8, 3 * OBS), jnp.int32),
             pltpu.VMEM((2, 4, 128), f32),
-            pltpu.SemaphoreType.DMA((4,)),
+            pltpu.SemaphoreType.DMA((3,)),
             pltpu.SemaphoreType.DMA((2 * PARTS,)),
         ],
         cost_estimate=pl.CostEstimate(flops=0, bytes_accessed=100 * 2**20, transcendentals=0),
         compiler_params=params(12),
         name="order",
-    )(tile_list, parts, cur, depth, cells)
+    )(tile_list, parts, depth, cells)
 
 
 def chunk_with_halo(cur, left, right, c, v):
@@ -353,21 +348,10 @@
     )(received, depth, left, right)
 
 
-def pick_kernel(
-    received, below, own, above, out, source, held, floats, lists, bounds, sems, list_sems
-):
-    arrivals = [
-        pltpu.make_async_copy(
-            received.at[k, pl.ds(4 * ROWS, 8), :], floats.at[k], list_sems.at[k]
-        )
-        for k in range(PARTS)
-    ]
-    for arrival in arrivals:
-        arrival.start()
-    for arrival in arrivals:
-        arrival.wait()
-    lists[...] = floats[...].astype(jnp.int32)
-    to_scalars = pltpu.make_async_copy(lists, bounds, list_sems.at[PARTS])
+def pick_kernel(received, below, own, above, out, source, held, lists, bounds, sems, list_sem):
+    for k in range(PARTS):
+        lists[k] = received[k, 4 * ROWS : 4 * ROWS + 8, :].astype(jnp.int32)
+    to_scalars = pltpu.make_async_copy(lists, bounds, list_sem)
     to_scalars.start()
     for n, part in enumerate((below, own, above)):
         for c in range(8):
@@ -415,16 +399,15 @@
     return pl.pallas_call(
         pick_kernel,
         out_shape=pltpu.HBM((PARTS, ROWS, SLOTS), f32),
-        in_specs=[pl.BlockSpec(memory_space=pl.ANY)] + [VMEM] * 3,
+        in_specs=[VMEM] * 4,
         out_specs=HBM,
         scratch_shapes=[
             pltpu.VMEM((24 + DIRECT, ROWS, 128), f32),
             pltpu.VMEM((PARTS, ROWS, SLOTS), f32),
-            pltpu.VMEM((PARTS, 8, 128), f32),
             pltpu.VMEM((PARTS, 8, 128), jnp.int32),
             pltpu.SMEM((PARTS, 8, 128), jnp.int32),
             pltpu.SemaphoreType.DMA((PARTS,)),
-            pltpu.SemaphoreType.DMA((PARTS + 1,)),
+            pltpu.SemaphoreType.DMA,
         ],
         compiler_params=params(16),
         cost_estimate=cost(10**12),
@@ -475,42 +458,80 @@
     )(rel, values, errors, cells)
 
 
-def analyse_kernel(predicted, slot_rows, state, gain_hi, gain_lo, analysis, held, result, sems):
+def analyse_kernel(
+    predicted, slot_rows, state, gain_hi, gain_lo, analysis,
+    left, right, z_left, z_right, y_right, slots_left, slots_right, held, result, sems,
+):
+    n = MEMBERS
+
+    def put_left(ref, x, rows=slice(None)):
+        high, low = halves(x)
+        k = x.shape[1]
+        ref[rows, :k] = high
+        ref[rows, k : 2 * k] = high
+        ref[rows, 2 * k :] = low
+
+    def put_right(ref, x):
+        high, low = halves(x)
+        ref[:n] = high
+        ref[n : 2 * n] = low
+        ref[2 * n :] = high
+
+    def times(a, b):
+        return dot(a[...], b[...])
+
     y = predicted[...]
     weight = slot_rows[0:1, :]
     mean = jnp.sum(y, axis=0, keepdims=True) * (1.0 / MEMBERS)
     root_weight = jnp.sqrt(weight)
     spread = (y - mean) * root_weight
     departure = (slot_rows[1:2, :] - mean) * root_weight
-    sh, sl = halves(spread)
-    dh, dl = halves(jnp.broadcast_to(departure, (16, SLOTS)))
-    rows_i = lax.broadcasted_iota(jnp.int32, (MEMBERS, MEMBERS), 0)
-    cols_i = lax.broadcasted_iota(jnp.int32, (MEMBERS, MEMBERS), 1)
-    eye = jnp.where(rows_i == cols_i, 1.0, 0.0)
-    a = dot_nt(sh, sh) + (dot_nt(sh, sl) + dot_nt(sl, sh)) + (MEMBERS - 1.0) * eye
-    innovation = (dot_nt(dh, sh) + (dot_nt(dh, sl) + dot_nt(dl, sh)))[0:1, :]
+    put_left(slots_left, spread, slice(0, n))
+    put_left(slots_left, jnp.broadcast_to(departure, (16, SLOTS)), slice(n, n + 16))
+    high, low = halves(spread)
+    slots_right[:, :SLOTS] = high
+    slots_right[:, SLOTS : 2 * SLOTS] = low
+    slots_right[:, 2 * SLOTS :] = high
+    on_diagonal = lax.broadcasted_iota(jnp.int32, (n, n), 0) == lax.broadcasted_iota(
+        jnp.int32, (n, n), 1
+    )
+
+    def plus(x, d):
+        return jnp.where(on_diagonal, x + d, x)
+
+    products = dot_nt(slots_left[...], slots_right[...])
+    a = plus(products[:n], MEMBERS - 1.0)
+    innovation = products[n : n + 1]
     bound = jnp.max(jnp.sum(jnp.abs(a), axis=0, keepdims=True), axis=1, keepdims=True)
     approx = a / bound
 
     def two_steps(m):
-        mp = halves(m)
-        m2 = product(mp, mp)
-        q = 1.6875 * eye - 0.5625 * m + 0.0625 * m2
-        return 2.25 * eye - 2.4375 * m + product(halves(m2), halves(q))
-
-    r = halves(two_steps(approx))
-    z = r
-    w = halves(product(halves(approx), r))
-    r = halves(two_steps(product(z, w)))
-    z, w = halves(product(r, z)), halves(product(w, r))
-    r = halves(two_steps(product(z, w)))
-    root = product(r, z) * lax.rsqrt(bound)
+        put_left(left, m)
+        put_right(right, m)
+        m2 = times(left, right)
+        put_left(left, m2)
+        put_right(right, plus(0.0625 * m2 - 0.5625 * m, 1.6875))
+        return plus(times(left, right) - 2.4375 * m, 2.25)
+
+    r = two_steps(approx)
+    put_left(left, r)
+    put_right(z_right, r)
+    put_right(y_right, approx)
+    put_right(y_right, times(left, y_right))
+    r = two_steps(times(left, y_right))
+    put_left(left, r)
+    z = times(left, z_right)
+    put_right(y_right, times(left, y_right))
+    put_right(z_right, z)
+    put_left(z_left, z)
+    put_left(left, two_steps(times(z_left, y_right)))
+    root = times(left, z_right) * lax.rsqrt(bound)
     once = jnp.sum(root * innovation, axis=1, keepdims=True)
     mean_weight = jnp.sum(root * once, axis=0, keepdims=True)
     moved = math.sqrt(MEMBERS - 1) * root + mean_weight
     gain = moved + (1.0 - jnp.sum(moved, axis=1, keepdims=True)) * (1.0 / MEMBERS)
-    gain = halves(gain)
-    held[0], held[1] = gain
+    put_left(left, gain)
+    held[0], held[1] = halves(gain)
     copies = [
         pltpu.make_async_copy(held.at[0], gain_hi, sems.at[0]),
         pltpu.make_async_copy(held.at[1], gain_lo, sems.at[1]),
@@ -518,7 +539,8 @@
     ]
     copies[0].start()
     copies[1].start()
-    analysed = product(gain, halves(state[...]))
+    put_right(right, state[...])
+    analysed = times(left, right)
     for row in range(4):
         at = (row % 2) * CELLS_TILE + (row // 2) * 128
         result[pl.ds(row, MEMBERS, stride=4), :] = analysed[:, at : at + 128]
@@ -538,11 +560,18 @@
         in_specs=[VMEM, VMEM, VMEM],
         out_specs=(HBM, HBM, HBM),
         scratch_shapes=[
+            pltpu.VMEM((MEMBERS, 3 * MEMBERS), bf16),
+            pltpu.VMEM((3 * MEMBERS, MEMBERS), bf16),
+            pltpu.VMEM((MEMBERS, 3 * MEMBERS), bf16),
+            pltpu.VMEM((3 * MEMBERS, MEMBERS), bf16),
+            pltpu.VMEM((3 * MEMBERS, MEMBERS), bf16),
+            pltpu.VMEM((MEMBERS + 16, 3 * SLOTS), bf16),
+            pltpu.VMEM((MEMBERS, 3 * SLOTS), bf16),
             pltpu.VMEM((2, MEMBERS, MEMBERS), bf16),
             pltpu.VMEM((MEMBERS * 4, 128), f32),
             pltpu.SemaphoreType.DMA((3,)),
         ],
-        compiler_params=params(32),
+        compiler_params=params(40),
         name="analyse",
     )(predicted, slot_rows, state)
 
@@ -605,14 +634,13 @@
 ):
     cur = current_state.reshape(ROWS, 2, CHUNKS, 128).transpose(0, 2, 1, 3)
     depth = water_depth.reshape(CHUNKS, 128)
-    to_right, to_left = edges(far(cur.reshape(ROWS, 2 * CHUNKS, 128)), far(depth))
+    cur, to_right, to_left = edges(far(cur.reshape(ROWS * 2 * CHUNKS, 128)), far(depth))
     left = along_tiles(to_right, 1)
     right = along_tiles(to_left, -1)
     to_left, listed = lax.optimization_barrier((to_left, tile_obs[0, 0].reshape(8, 128)))
-    ordered, payload, cur, depth, cells = order(
+    ordered, payload, depth, cells = order(
         far(listed),
-        far(cur.reshape(ROWS, PARTS, 4, 128)),
-        far(cur.reshape(ROWS * 2 * CHUNKS, 128)),
+        cur.reshape(ROWS, PARTS, 4, 128),
         far(depth),
         far(obs_cells.reshape(TILES, 8, 128)),
     )

time: 140 us -> 112 us (0.80)
  Pallas kernels: 69.6 us -> 38.4 us
  starting transfers between devices: 27.4 us -> 30.3 us
    pallas_call x1, Pallas kernels: 33.1 us -> 2.38 us  [order(): pl.pallas_call(order_kernel, out_shape=(jax.ShapeDtypeStruct((8, 128), jn...]
    ppermute x4, starting transfers between devices: 10.8 us -> 13.7 us  [along_tiles(): lax.ppermute(x, 'tile', [(i, (i + by) % TILES) for i in range(TILES)])]
  transfers between devices with their start and end apart: 7 -> 7, of which waited for: 4 -> 4; matrix products, arithmetic and copies ran while one was open for 0% -> 0% of each run, Pallas kernels for 31% -> 11%
where the time goes in v6:
time: 112 us
  waiting for transfers between devices  39.9 us (36%)
  Pallas kernels  38.4 us (34%)
  starting transfers between devices  30.3 us (27%)
  local copies, waits for them, and re-layouts  1.94 us (2%)
    all_to_all x3, waiting for transfers between devices, exchange(): return lax.all_to_all(x, GROUP, split_axis=0, concat_axis=0, tiled=True)  28.9 us
    all_to_all x3, starting transfers between devices, exchange(): return lax.all_to_all(x, GROUP, split_axis=0, concat_axis=0, tiled=True)  16.7 us
    pallas_call x1, Pallas kernels, analyse(): pl.pallas_call(analyse_kernel, out_shape=(pltpu.HBM((MEMBERS, MEMBERS), b...  15 us
    ppermute x4, starting transfers between devices, along_tiles(): lax.ppermute(x, 'tile', [(i, (i + by) % TILES) for i in range(TILES)])  13.7 us
    ppermute x4, waiting for transfers between devices, along_tiles(): lax.ppermute(x, 'tile', [(i, (i + by) % TILES) for i in range(TILES)])  10.9 us
    pallas_call x1, Pallas kernels, pick(): pl.pallas_call(pick_kernel, out_shape=pltpu.HBM((PARTS, ROWS, SLOTS), f32...  7.32 us
    pallas_call x1, Pallas kernels, smooth(): pl.pallas_call(smooth_kernel, out_shape=jax.ShapeDtypeStruct((LAGS, MEMBE...  3.93 us
    pallas_call x1, Pallas kernels, forecast(): pl.pallas_call(forecast_kernel, out_shape=jax.ShapeDtypeStruct((MEMBERS,...  3.46 us
  transfers between devices with their start and end apart: 7, of which 4 were waited for; matrix products, arithmetic and copies ran while one was open for 0% of the time, Pallas kernels for 11%

profile of v6, /device:TPU:1, one launch (start us, length us, event | category | flops | bytes accessed | tf_op | source)
XLA Modules:
  0.0 111.5 jit_solution(15230885865225163570)
XLA Ops:
  0.6 1.4 %edges.1 = (f32[2048,128]{1,0:T(8,128)S(1)}, f32[72,128]{1,0:T(8,128)S(1)}, f32[72,128]{1,0:T(8,128)S(1)}) custom-call(f32[2048,128]{1,0:T(8,128)} %bitcast.33, f32[16,128]{1,0:T(8,128)} %bitcast.36), custom_call_target="tpu_custom_call" | custom-call | tf_op jit(solution)/shard_map/edges/pallas_call | solution.py:83
  2.0 2.5 %collective-permute-start = (f32[72,128]{1,0:T(8,128)S(1)}, f32[72,128]{1,0:T(8,128)S(1)}, u32[]{:S(2)}, u32[]{:S(2)}) collective-permute-start(f32[72,128]{1,0:T(8,128)S(1)} %get-tuple-element.17), channel_id=1, source_target_pairs={{0,4},{4,8},{8,12},{12,16},{16,20},{20,24},{24,28},{28,32},{32,36}... | collective-permute-start | bytes 110600 | tf_op jit(solution)/shard_map/ppermute | solution.py:621
  4.5 6.5 %collective-permute-start.1 = (f32[72,128]{1,0:T(8,128)S(1)}, f32[72,128]{1,0:T(8,128)S(1)}, u32[]{:S(2)}, u32[]{:S(2)}) collective-permute-start(f32[72,128]{1,0:T(8,128)S(1)} %get-tuple-element.13), channel_id=1, source_target_pairs={{0,124},{4,0},{8,4},{12,8},{16,12},{20,16},{24,20},{28,24},{32,28}... | collective-permute-start | bytes 110600 | tf_op jit(solution)/shard_map/ppermute | solution.py:621
  11.0 2.4 %order.1 = (s32[8,128]{1,0:T(8,128)S(1)}, f32[8,68,4,128]{3,2,1,0:T(4,128)}, f32[16,128]{1,0:T(8,128)S(1)}, s32[8,128]{1,0:T(8,128)S(1)}) custom-call(s32[8,128]{1,0:T(8,128)} %bitcast.38, f32[64,8,4,128]{3,2,1,0:T(4,128)S(1)} %bitcast.25, f32[16,128]{1,0:T(8,128)} %bitcast.37, s32[32,8,128]{2,1,0:T(8,128)} %bitcast.27), custom_call_target="tpu_custom_call" | custom-call | bytes 104857600 | tf_op jit(solution)/shard_map/order/pallas_call | solution.py:161
  13.4 0.0 copy-start.10
  13.4 0.0 collective-permute-done.left
  13.4 0.0 copy-start.3
  13.4 0.0 collective-permute-done.1.right
  13.5 0.0 copy-start.5
  13.5 1.3 %beside.1 = f32[8,68,4,128]{3,2,1,0:T(4,128)} custom-call(f32[8,68,4,128]{3,2,1,0:T(4,128)} %get-tuple-element.16._, f32[2048,128]{1,0:T(8,128)S(1)} %get-tuple-element.15.cur, f32[72,128]{1,0:T(8,128)S(1)} %collective-permute-done.left, f32[72,128]{1,0:T(8,128)S(1)} %collective-permute-done.1.right), custom_call_target="tpu_custom_call", output_to_operand_aliasing={{}: (0, {})} | custom-call | flops 1000 | bytes 1048576 | tf_op jit(solution)/shard_map/beside/pallas_call | solution.py:214
  14.7 5.3 %all-to-all-start = ((f32[8,272,128]{2,1,0:T(8,128)}), f32[8,272,128]{2,1,0:T(8,128)}, u32[]{:S(2)}, u32[]{:S(2)}) async-start(f32[8,272,128]{2,1,0:T(8,128)} %bitcast.32), calls=%async_computation | async-start | bytes 2228224 | tf_op jit(solution)/shard_map/all_to_all | solution.py:629
  20.0 0.0 copy-done.10
  20.0 0.0 copy-done.3
  20.0 0.0 copy-done.5
  20.0 2.5 %heights.1.own = f32[64,1024]{1,0:T(8,128)S(1)} custom-call(f32[2048,128]{1,0:T(8,128)S(1)} %get-tuple-element.15.cur, f32[16,128]{1,0:T(8,128)S(1)} %get-tuple-element.18.depth, f32[72,128]{1,0:T(8,128)S(1)} %collective-permute-done.left, f32[72,128]{1,0:T(8,128)S(1)} %collective-permute-done.1.right, s32[8,128]{1,0:T(8,128)S(1)} %get-tuple-element.19.cells), custom_call_target="tpu_custom_call" | custom-call | flops 999999995904 | bytes 1048576 | tf_op jit(solution)/shard_map/heights/pallas_call | solution.py:284
  22.5 4.6 %collective-permute-start.3 = (f32[64,1024]{1,0:T(8,128)S(1)}, f32[64,1024]{1,0:T(8,128)S(1)}, u32[]{:S(2)}, u32[]{:S(2)}) collective-permute-start(f32[64,1024]{1,0:T(8,128)S(1)} %heights.1.own), channel_id=1, source_target_pairs={{0,124},{4,0},{8,4},{12,8},{16,12},{20,16},{24,20},{28,24},{32,28}... | collective-permute-start | bytes 786440 | tf_op jit(solution)/shard_map/ppermute | solution.py:621
  27.2 0.0 collective-permute-start.2
  27.2 5.7 %collective-permute-done.3.above = f32[64,1024]{1,0:T(8,128)S(1)} collective-permute-done((f32[64,1024]{1,0:T(8,128)S(1)}, f32[64,1024]{1,0:T(8,128)S(1)}, u32[]{:S(2)}, u32[]{:S(2)}) %collective-permute-start.3) | collective-permute-done | bytes 262176 | tf_op jit(solution)/shard_map/ppermute | solution.py:621
  32.9 5.2 %collective-permute-done.2.below = f32[64,1024]{1,0:T(8,128)S(1)} collective-permute-done((f32[64,1024]{1,0:T(8,128)S(1)}, f32[64,1024]{1,0:T(8,128)S(1)}, u32[]{:S(2)}, u32[]{:S(2)}) %collective-permute-start.2) | collective-permute-done | bytes 262176 | tf_op jit(solution)/shard_map/ppermute | solution.py:621
  38.1 0.0 all-to-all-done.received
  38.1 7.3 %pick.1 = f32[8,64,1024]{2,1,0:T(8,128)} custom-call(f32[8,272,128]{2,1,0:T(8,128)} %all-to-all-done.received, f32[64,1024]{1,0:T(8,128)S(1)} %collective-permute-done.2.below, f32[64,1024]{1,0:T(8,128)S(1)} %heights.1.own, f32[64,1024]{1,0:T(8,128)S(1)} %collective-permute-done.3.above), custom_call_target="tpu_custom_call" | custom-call | flops 999999995904 | bytes 1048576 | tf_op jit(solution)/shard_map/pick/pallas_call | solution.py:399
  45.4 0.0 copy-start
  45.4 0.0 copy-start.1
  45.5 0.0 copy-start.2
  45.5 0.0 copy-start.4
  45.5 0.0 copy-start.6
  45.5 0.0 copy-start.11
  45.5 5.7 %all-to-all-start.1 = ((f32[8,64,1024]{2,1,0:T(8,128)}), f32[8,64,1024]{2,1,0:T(8,128)S(1)}, u32[]{:S(2)}, u32[]{:S(2)}) async-start(f32[8,64,1024]{2,1,0:T(8,128)} %pick.1), calls=%async_computation.1 | async-start | bytes 4194304 | tf_op jit(solution)/shard_map/all_to_all | solution.py:629
  51.2 0.0 copy-done
  51.2 0.0 copy-done.1
  51.2 0.0 copy-done.2
  51.2 0.2 slots.1.slot_rows
  51.4 0.0 copy-done.4
  51.4 0.0 copy-done.6
  51.4 0.0 copy-done.11
  51.4 3.5 %forecast.1.state = f32[512,512]{1,0:T(8,128)S(1)} custom-call(f32[8,272,128]{2,1,0:T(8,128)} %all-to-all-done.received, f32[16,128]{1,0:T(8,128)S(1)} %copy-done.11, f32[72,128]{1,0:T(8,128)S(1)} %copy-done.4, f32[72,128]{1,0:T(8,128)S(1)} %copy-done.6), custom_call_target="tpu_custom_call" | custom-call | flops 10000000000 | bytes 1048576 | tf_op jit(solution)/shard_map/forecast/pallas_call | solution.py:339
  54.9 21.1 %all-to-all-done.1 = f32[8,64,1024]{2,1,0:T(8,128)S(1)} async-done(((f32[8,64,1024]{2,1,0:T(8,128)}), f32[8,64,1024]{2,1,0:T(8,128)S(1)}, u32[]{:S(2)}, u32[]{:S(2)}) %all-to-all-start.1) | async-done | bytes 2097184 | tf_op jit(solution)/shard_map/all_to_all | solution.py:629
  76.0 15.0 %analyse.1 = (bf16[512,512]{1,0:T(8,128)(2,1)}, bf16[512,512]{1,0:T(8,128)(2,1)}, f32[2048,128]{1,0:T(8,128)}) custom-call(f32[512,1024]{1,0:T(8,128)S(1)} %bitcast.24, f32[8,1024]{1,0:T(8,128)S(1)} %slots.1.slot_rows, f32[512,512]{1,0:T(8,128)S(1)} %forecast.1.state), custom_call_target="tpu_custom_call" | custom-call | tf_op jit(solution)/shard_map/analyse/pallas_call | solution.py:553
  91.0 0.0 copy-start.8
  91.0 0.0 copy-start.9
  91.0 5.7 %all-to-all-start.2 = ((f32[8,256,128]{2,1,0:T(8,128)}), f32[8,256,128]{2,1,0:T(8,128)S(1)}, u32[]{:S(2)}, u32[]{:S(2)}) async-start(f32[8,256,128]{2,1,0:T(8,128)} %bitcast.34), calls=%async_computation.2 | async-start | bytes 2097152 | tf_op jit(solution)/shard_map/all_to_all | solution.py:629
  96.7 0.0 copy-done.8
  96.7 0.0 copy-done.9
  96.7 0.0 copy-start.7
  96.7 1.9 %copy-done.7 = f32[3,1,1,512,512]{4,3,2,1,0:T(8,128)S(1)} copy-done((f32[3,1,1,512,512]{4,3,2,1,0:T(8,128)S(1)}, f32[3,1,1,512,512]{4,3,2,1,0:T(8,128)}, u32[]{:S(2)}) %copy-start.7) | copy-done | bytes 3145752
  98.6 3.9 %smooth.1 = f32[3,512,512]{2,1,0:T(8,128)} custom-call(bf16[512,512]{1,0:T(8,128)(2,1)S(1)} %copy-done.8, bf16[512,512]{1,0:T(8,128)(2,1)S(1)} %copy-done.9, f32[3,512,512]{2,1,0:T(8,128)S(1)} %bitcast.31), custom_call_target="tpu_custom_call" | custom-call | flops 2415919104 | bytes 6291456 | tf_op jit(solution)/shard_map/smooth/pallas_call | solution.py:586
  102.6 7.8 %all-to-all-done.2 = f32[8,256,128]{2,1,0:T(8,128)S(1)} async-done(((f32[8,256,128]{2,1,0:T(8,128)}), f32[8,256,128]{2,1,0:T(8,128)S(1)}, u32[]{:S(2)}, u32[]{:S(2)}) %all-to-all-start.2) | async-done | bytes 1048608 | tf_op jit(solution)/shard_map/all_to_all | solution.py:629
  110.3 1.0 assemble.1
Async XLA Ops:
  2.0 11.4 %collective-permute-start = (f32[72,128]{1,0:T(8,128)S(1)}, f32[72,128]{1,0:T(8,128)S(1)}, u32[]{:S(2)}, u32[]{:S(2)}) collective-permute-start(f32[72,128]{1,0:T(8,128)S(1)} %get-tuple-element.17), channel_id=1, source_target_pairs={{0,4},{4,8},{8,12},{12,16},{16,20},{20,24},{24,28},{28,32},{32,36}... | collective-permute-start | bytes 110600 | tf_op jit(solution)/shard_map/ppermute | solution.py:621
  4.5 8.9 %collective-permute-start.1 = (f32[72,128]{1,0:T(8,128)S(1)}, f32[72,128]{1,0:T(8,128)S(1)}, u32[]{:S(2)}, u32[]{:S(2)}) collective-permute-start(f32[72,128]{1,0:T(8,128)S(1)} %get-tuple-element.13), channel_id=1, source_target_pairs={{0,124},{4,0},{8,4},{12,8},{16,12},{20,16},{24,20},{28,24},{32,28}... | collective-permute-start | bytes 110600 | tf_op jit(solution)/shard_map/ppermute | solution.py:621
  13.4 6.6 %copy-start.10 = (f32[16,128]{1,0:T(8,128)}, f32[16,128]{1,0:T(8,128)S(1)}, u32[]{:S(2)}) copy-start(f32[16,128]{1,0:T(8,128)S(1)} %get-tuple-element.18.depth) | copy-start | bytes 24580
  13.4 6.6 %copy-start.3 = (f32[72,128]{1,0:T(8,128)}, f32[72,128]{1,0:T(8,128)S(1)}, u32[]{:S(2)}) copy-start(f32[72,128]{1,0:T(8,128)S(1)} %collective-permute-done.left) | copy-start | bytes 110596
  13.5 6.6 %copy-start.5 = (f32[72,128]{1,0:T(8,128)}, f32[72,128]{1,0:T(8,128)S(1)}, u32[]{:S(2)}) copy-start(f32[72,128]{1,0:T(8,128)S(1)} %collective-permute-done.1.right) | copy-start | bytes 110596
  14.7 23.4 %all-to-all-start = ((f32[8,272,128]{2,1,0:T(8,128)}), f32[8,272,128]{2,1,0:T(8,128)}, u32[]{:S(2)}, u32[]{:S(2)}) async-start(f32[8,272,128]{2,1,0:T(8,128)} %bitcast.32), calls=%async_computation | async-start | bytes 2228224 | tf_op jit(solution)/shard_map/all_to_all | solution.py:629
  22.5 10.4 %collective-permute-start.3 = (f32[64,1024]{1,0:T(8,128)S(1)}, f32[64,1024]{1,0:T(8,128)S(1)}, u32[]{:S(2)}, u32[]{:S(2)}) collective-permute-start(f32[64,1024]{1,0:T(8,128)S(1)} %heights.1.own), channel_id=1, source_target_pairs={{0,124},{4,0},{8,4},{12,8},{16,12},{20,16},{24,20},{28,24},{32,28}... | collective-permute-start | bytes 786440 | tf_op jit(solution)/shard_map/ppermute | solution.py:621
  27.2 10.9 %collective-permute-start.2 = (f32[64,1024]{1,0:T(8,128)S(1)}, f32[64,1024]{1,0:T(8,128)S(1)}, u32[]{:S(2)}, u32[]{:S(2)}) collective-permute-start(f32[64,1024]{1,0:T(8,128)S(1)} %heights.1.own), channel_id=1, source_target_pairs={{0,4},{4,8},{8,12},{12,16},{16,20},{20,24},{24,28},{28,32},{32,36}... | collective-permute-start | bytes 786440 | tf_op jit(solution)/shard_map/ppermute | solution.py:621
  45.4 5.8 %copy-start = (s32[32768]{0:T(1024)S(1)}, s32[32768]{0:T(1024)}, u32[]{:S(2)}) copy-start(s32[32768]{0:T(1024)} %param.10) | copy-start | bytes 393220
  45.4 5.8 %copy-start.1 = (f32[32768]{0:T(1024)S(1)}, f32[32768]{0:T(1024)}, u32[]{:S(2)}) copy-start(f32[32768]{0:T(1024)} %param.11) | copy-start | bytes 393220
  45.5 5.8 %copy-start.2 = (f32[32768]{0:T(1024)S(1)}, f32[32768]{0:T(1024)}, u32[]{:S(2)}) copy-start(f32[32768]{0:T(1024)} %param.12) | copy-start | bytes 393220
  45.5 5.9 %copy-start.4 = (f32[72,128]{1,0:T(8,128)S(1)}, f32[72,128]{1,0:T(8,128)}, u32[]{:S(2)}) copy-start(f32[72,128]{1,0:T(8,128)} %copy-done.3) | copy-start | bytes 110596
  45.5 5.9 %copy-start.6 = (f32[72,128]{1,0:T(8,128)S(1)}, f32[72,128]{1,0:T(8,128)}, u32[]{:S(2)}) copy-start(f32[72,128]{1,0:T(8,128)} %copy-done.5) | copy-start | bytes 110596
  45.5 5.9 %copy-start.11 = (f32[16,128]{1,0:T(8,128)S(1)}, f32[16,128]{1,0:T(8,128)}, u32[]{:S(2)}) copy-start(f32[16,128]{1,0:T(8,128)} %copy-done.10) | copy-start | bytes 24580
  45.5 30.5 %all-to-all-start.1 = ((f32[8,64,1024]{2,1,0:T(8,128)}), f32[8,64,1024]{2,1,0:T(8,128)S(1)}, u32[]{:S(2)}, u32[]{:S(2)}) async-start(f32[8,64,1024]{2,1,0:T(8,128)} %pick.1), calls=%async_computation.1 | async-start | bytes 4194304 | tf_op jit(solution)/shard_map/all_to_all | solution.py:629
  91.0 5.7 %copy-start.8 = (bf16[512,512]{1,0:T(8,128)(2,1)S(1)}, bf16[512,512]{1,0:T(8,128)(2,1)}, u32[]{:S(2)}) copy-start(bf16[512,512]{1,0:T(8,128)(2,1)} %get-tuple-element.22.gain_hi) | copy-start | bytes 1572868
  91.0 5.7 %copy-start.9 = (bf16[512,512]{1,0:T(8,128)(2,1)S(1)}, bf16[512,512]{1,0:T(8,128)(2,1)}, u32[]{:S(2)}) copy-start(bf16[512,512]{1,0:T(8,128)(2,1)} %get-tuple-element.23.gain_lo) | copy-start | bytes 1572868
  91.0 19.3 %all-to-all-start.2 = ((f32[8,256,128]{2,1,0:T(8,128)}), f32[8,256,128]{2,1,0:T(8,128)S(1)}, u32[]{:S(2)}, u32[]{:S(2)}) async-start(f32[8,256,128]{2,1,0:T(8,128)} %bitcast.34), calls=%async_computation.2 | async-start | bytes 2097152 | tf_op jit(solution)/shard_map/all_to_all | solution.py:629
  96.7 1.9 %copy-start.7 = (f32[3,1,1,512,512]{4,3,2,1,0:T(8,128)S(1)}, f32[3,1,1,512,512]{4,3,2,1,0:T(8,128)}, u32[]{:S(2)}) copy-start(f32[3,1,1,512,512]{4,3,2,1,0:T(8,128)} %param.8) | copy-start | bytes 9437188

commit v7 on v6

--- a/solution.py
+++ b/solution.py
@@ -23,7 +23,7 @@
 TILES = 32
 LOC = 512
 LAGS = 3
-DIRECT = 4
+DIRECT = 3
 f32 = jnp.float32
 bf16 = jnp.bfloat16
 VMEM = pl.BlockSpec(memory_space=pltpu.VMEM)
@@ -332,13 +332,16 @@
         h = height_step(h, u, 1)
         u = speed_step(h, u, 1, 3)
         for i, x in enumerate((h[1], h[2], u[1], u[2])):
-            state[b * ROWS : (b + 1) * ROWS, i * 128 : (i + 1) * 128] = x
+            high, low = halves(x)
+            for place, part_of in enumerate((high, low, high)):
+                at = place * MEMBERS + b * ROWS
+                state[at : at + ROWS, i * 128 : (i + 1) * 128] = part_of
 
 
 def forecast(received, depth, left, right):
     return pl.pallas_call(
         forecast_kernel,
-        out_shape=jax.ShapeDtypeStruct((MEMBERS, STATE), f32),
+        out_shape=jax.ShapeDtypeStruct((3 * MEMBERS, STATE), bf16),
         in_specs=[VMEM] * 4,
         out_specs=VMEM,
         scratch_shapes=[pltpu.VMEM((128, 128), f32), pltpu.VMEM((24, 128), f32)],
@@ -348,7 +351,7 @@
     )(received, depth, left, right)
 
 
-def pick_kernel(received, below, own, above, out, source, held, lists, bounds, sems, list_sem):
+def pick_kernel(received, above, own, below, out, source, held, lists, bounds, sems, list_sem):
     for k in range(PARTS):
         lists[k] = received[k, 4 * ROWS : 4 * ROWS + 8, :].astype(jnp.int32)
     to_scalars = pltpu.make_async_copy(lists, bounds, list_sem)
@@ -395,7 +398,7 @@
         send(k).wait()
 
 
-def pick(received, below, own, above):
+def pick(received, above, own, below):
     return pl.pallas_call(
         pick_kernel,
         out_shape=pltpu.HBM((PARTS, ROWS, SLOTS), f32),
@@ -412,7 +415,7 @@
         compiler_params=params(16),
         cost_estimate=cost(10**12),
         name="pick",
-    )(received, below, own, above)
+    )(received, above, own, below)
 
 
 def slots_kernel(rel, values, errors, cells, out):
@@ -539,8 +542,7 @@
     ]
     copies[0].start()
     copies[1].start()
-    put_right(right, state[...])
-    analysed = times(left, right)
+    analysed = times(left, state)
     for row in range(4):
         at = (row % 2) * CELLS_TILE + (row // 2) * 128
         result[pl.ds(row, MEMBERS, stride=4), :] = analysed[:, at : at + 128]
@@ -649,7 +651,7 @@
     own = heights(cur, depth, left, right, cells)
     below = along_tiles(own, 1)
     above = along_tiles(own, -1)
-    picked = pick(received, below, own, above)
+    picked = pick(received, above, own, below)
     predicted = exchange(picked).reshape(MEMBERS, SLOTS)
     state = forecast(received, depth, left, right)
     slot_rows = slots(

time: 112 us -> 110 us (0.982)
  waiting for transfers between devices: 39.9 us -> 34.7 us
  local copies, waits for them, and re-layouts: 1.94 us -> 4.53 us
    ppermute x4, waiting for transfers between devices: 10.9 us -> 6.47 us  [along_tiles(): lax.ppermute(x, 'tile', [(i, (i + by) % TILES) for i in range(TILES)])]
    unnamed x24 -> x28, local copies, waits for them, and re-layouts: 1.94 us -> 4.53 us
where the time goes in v7:
time: 110 us
  Pallas kernels  39.4 us (36%)
  waiting for transfers between devices  34.7 us (32%)
  starting transfers between devices  30.6 us (28%)
  local copies, waits for them, and re-layouts  4.53 us (4%)
    all_to_all x3, waiting for transfers between devices, exchange(): return lax.all_to_all(x, GROUP, split_axis=0, concat_axis=0, tiled=True)  28.2 us
    all_to_all x3, starting transfers between devices, exchange(): return lax.all_to_all(x, GROUP, split_axis=0, concat_axis=0, tiled=True)  16.7 us
    pallas_call x1, Pallas kernels, analyse(): pl.pallas_call(analyse_kernel, out_shape=(pltpu.HBM((MEMBERS, MEMBERS), b...  15 us
    ppermute x4, starting transfers between devices, along_tiles(): lax.ppermute(x, 'tile', [(i, (i + by) % TILES) for i in range(TILES)])  13.9 us
    pallas_call x1, Pallas kernels, pick(): pl.pallas_call(pick_kernel, out_shape=pltpu.HBM((PARTS, ROWS, SLOTS), f32...  8.23 us
    ppermute x4, waiting for transfers between devices, along_tiles(): lax.ppermute(x, 'tile', [(i, (i + by) % TILES) for i in range(TILES)])  6.47 us
    unnamed x28, local copies, waits for them, and re-layouts  4.53 us
    pallas_call x1, Pallas kernels, smooth(): pl.pallas_call(smooth_kernel, out_shape=jax.ShapeDtypeStruct((LAGS, MEMBE...  3.93 us
  transfers between devices with their start and end apart: 7, of which 4 were waited for; matrix products, arithmetic and copies ran while one was open for 0% of the time, Pallas kernels for 11%

profile of v7, /device:TPU:1, one launch (start us, length us, event | category | flops | bytes accessed | tf_op | source)
XLA Modules:
  0.0 110.2 jit_solution(5136037607378312696)
XLA Ops:
  0.6 1.4 %edges.1 = (f32[2048,128]{1,0:T(8,128)S(1)}, f32[72,128]{1,0:T(8,128)S(1)}, f32[72,128]{1,0:T(8,128)S(1)}) custom-call(f32[2048,128]{1,0:T(8,128)} %bitcast.33, f32[16,128]{1,0:T(8,128)} %bitcast.36), custom_call_target="tpu_custom_call" | custom-call | tf_op jit(solution)/shard_map/edges/pallas_call | solution.py:83
  2.0 2.5 %collective-permute-start = (f32[72,128]{1,0:T(8,128)S(1)}, f32[72,128]{1,0:T(8,128)S(1)}, u32[]{:S(2)}, u32[]{:S(2)}) collective-permute-start(f32[72,128]{1,0:T(8,128)S(1)} %get-tuple-element.17), channel_id=1, source_target_pairs={{0,4},{4,8},{8,12},{12,16},{16,20},{20,24},{24,28},{28,32},{32,36}... | collective-permute-start | bytes 110600 | tf_op jit(solution)/shard_map/ppermute | solution.py:623
  4.5 6.5 %collective-permute-start.1 = (f32[72,128]{1,0:T(8,128)S(1)}, f32[72,128]{1,0:T(8,128)S(1)}, u32[]{:S(2)}, u32[]{:S(2)}) collective-permute-start(f32[72,128]{1,0:T(8,128)S(1)} %get-tuple-element.13), channel_id=1, source_target_pairs={{0,124},{4,0},{8,4},{12,8},{16,12},{20,16},{24,20},{28,24},{32,28}... | collective-permute-start | bytes 110600 | tf_op jit(solution)/shard_map/ppermute | solution.py:623
  11.0 2.4 %order.1 = (s32[8,128]{1,0:T(8,128)S(1)}, f32[8,68,4,128]{3,2,1,0:T(4,128)}, f32[16,128]{1,0:T(8,128)S(1)}, s32[8,128]{1,0:T(8,128)S(1)}) custom-call(s32[8,128]{1,0:T(8,128)} %bitcast.38, f32[64,8,4,128]{3,2,1,0:T(4,128)S(1)} %bitcast.25, f32[16,128]{1,0:T(8,128)} %bitcast.37, s32[32,8,128]{2,1,0:T(8,128)} %bitcast.27), custom_call_target="tpu_custom_call" | custom-call | bytes 104857600 | tf_op jit(solution)/shard_map/order/pallas_call | solution.py:161
  13.4 0.0 copy-start.12
  13.4 0.0 collective-permute-done.left
  13.4 0.0 copy-start.5
  13.4 0.0 collective-permute-done.1.right
  13.5 0.0 copy-start.7
  13.5 1.3 %beside.1 = f32[8,68,4,128]{3,2,1,0:T(4,128)} custom-call(f32[8,68,4,128]{3,2,1,0:T(4,128)} %get-tuple-element.16._, f32[2048,128]{1,0:T(8,128)S(1)} %get-tuple-element.15.cur, f32[72,128]{1,0:T(8,128)S(1)} %collective-permute-done.left, f32[72,128]{1,0:T(8,128)S(1)} %collective-permute-done.1.right), custom_call_target="tpu_custom_call", output_to_operand_aliasing={{}: (0, {})} | custom-call | flops 1000 | bytes 1048576 | tf_op jit(solution)/shard_map/beside/pallas_call | solution.py:214
  14.7 5.3 %all-to-all-start = ((f32[8,272,128]{2,1,0:T(8,128)}), f32[8,272,128]{2,1,0:T(8,128)}, u32[]{:S(2)}, u32[]{:S(2)}) async-start(f32[8,272,128]{2,1,0:T(8,128)} %bitcast.32), calls=%async_computation | async-start | bytes 2228224 | tf_op jit(solution)/shard_map/all_to_all | solution.py:631
  20.0 0.0 copy-done.12
  20.0 0.0 copy-done.5
  20.0 0.0 copy-done.7
  20.0 2.6 %heights.1.own = f32[64,1024]{1,0:T(8,128)S(1)} custom-call(f32[2048,128]{1,0:T(8,128)S(1)} %get-tuple-element.15.cur, f32[16,128]{1,0:T(8,128)S(1)} %get-tuple-element.18.depth, f32[72,128]{1,0:T(8,128)S(1)} %collective-permute-done.left, f32[72,128]{1,0:T(8,128)S(1)} %collective-permute-done.1.right, s32[8,128]{1,0:T(8,128)S(1)} %get-tuple-element.19.cells), custom_call_target="tpu_custom_call" | custom-call | flops 999999995904 | bytes 1048576 | tf_op jit(solution)/shard_map/heights/pallas_call | solution.py:284
  22.6 0.1 collective-permute-start.3
  22.7 4.8 %collective-permute-start.2 = (f32[64,1024]{1,0:T(8,128)S(1)}, f32[64,1024]{1,0:T(8,128)S(1)}, u32[]{:S(2)}, u32[]{:S(2)}) collective-permute-start(f32[64,1024]{1,0:T(8,128)S(1)} %heights.1.own), channel_id=1, source_target_pairs={{0,124},{4,0},{8,4},{12,8},{16,12},{20,16},{24,20},{28,24},{32,28}... | collective-permute-start | bytes 786440 | tf_op jit(solution)/shard_map/ppermute | solution.py:623
  27.5 6.5 %collective-permute-done.3.below = f32[64,1024]{1,0:T(8,128)S(1)} collective-permute-done((f32[64,1024]{1,0:T(8,128)S(1)}, f32[64,1024]{1,0:T(8,128)S(1)}, u32[]{:S(2)}, u32[]{:S(2)}) %collective-permute-start.3) | collective-permute-done | bytes 262176 | tf_op jit(solution)/shard_map/ppermute | solution.py:623
  34.0 0.0 collective-permute-done.2.above
  34.0 0.4 all-to-all-done.received
  34.4 8.2 %pick.1 = f32[8,64,1024]{2,1,0:T(8,128)} custom-call(f32[8,272,128]{2,1,0:T(8,128)} %all-to-all-done.received, f32[64,1024]{1,0:T(8,128)S(1)} %collective-permute-done.2.above, f32[64,1024]{1,0:T(8,128)S(1)} %heights.1.own, f32[64,1024]{1,0:T(8,128)S(1)} %collective-permute-done.3.below), custom_call_target="tpu_custom_call" | custom-call | flops 999999995904 | bytes 1048576 | tf_op jit(solution)/shard_map/pick/pallas_call | solution.py:402
  42.6 0.0 copy-start.2
  42.7 0.0 copy-start.3
  42.7 0.0 copy-start.4
  42.7 0.0 copy-start.6
  42.7 0.0 copy-start.8
  42.7 0.0 copy-start.13
  42.7 5.7 %all-to-all-start.1 = ((f32[8,64,1024]{2,1,0:T(8,128)}), f32[8,64,1024]{2,1,0:T(8,128)S(1)}, u32[]{:S(2)}, u32[]{:S(2)}) async-start(f32[8,64,1024]{2,1,0:T(8,128)} %pick.1), calls=%async_computation.1 | async-start | bytes 4194304 | tf_op jit(solution)/shard_map/all_to_all | solution.py:631
  48.5 0.0 copy-done.2
  48.5 0.0 copy-done.3
  48.5 0.0 copy-done.4
  48.5 0.2 slots.1.slot_rows
  48.6 0.0 copy-done.6
  48.6 0.0 copy-done.8
  48.7 0.0 copy-done.13
  48.7 3.5 %forecast.1.state = bf16[1536,512]{1,0:T(8,128)(2,1)S(1)} custom-call(f32[8,272,128]{2,1,0:T(8,128)} %all-to-all-done.received, f32[16,128]{1,0:T(8,128)S(1)} %copy-done.13, f32[72,128]{1,0:T(8,128)S(1)} %copy-done.6, f32[72,128]{1,0:T(8,128)S(1)} %copy-done.8), custom_call_target="tpu_custom_call" | custom-call | flops 10000000000 | bytes 1048576 | tf_op jit(solution)/shard_map/forecast/pallas_call | solution.py:342
  52.2 0.0 copy-start
  52.2 1.2 %copy-done = bf16[1536,512]{1,0:T(8,128)(2,1)} copy-done((bf16[1536,512]{1,0:T(8,128)(2,1)}, bf16[1536,512]{1,0:T(8,128)(2,1)S(1)}, u32[]{:S(2)}) %copy-start) | copy-done | bytes 1572888
  53.3 20.0 %all-to-all-done.1 = f32[8,64,1024]{2,1,0:T(8,128)S(1)} async-done(((f32[8,64,1024]{2,1,0:T(8,128)}), f32[8,64,1024]{2,1,0:T(8,128)S(1)}, u32[]{:S(2)}, u32[]{:S(2)}) %all-to-all-start.1) | async-done | bytes 2097184 | tf_op jit(solution)/shard_map/all_to_all | solution.py:631
  73.3 0.0 copy-start.1
  73.3 1.4 %copy-done.1 = bf16[1536,512]{1,0:T(8,128)(2,1)S(1)} copy-done((bf16[1536,512]{1,0:T(8,128)(2,1)S(1)}, bf16[1536,512]{1,0:T(8,128)(2,1)}, u32[]{:S(2)}) %copy-start.1) | copy-done | bytes 1572888
  74.7 15.0 %analyse.1 = (bf16[512,512]{1,0:T(8,128)(2,1)}, bf16[512,512]{1,0:T(8,128)(2,1)}, f32[2048,128]{1,0:T(8,128)}) custom-call(f32[512,1024]{1,0:T(8,128)S(1)} %bitcast.24, f32[8,1024]{1,0:T(8,128)S(1)} %slots.1.slot_rows, bf16[1536,512]{1,0:T(8,128)(2,1)S(1)} %copy-done.1), custom_call_target="tpu_custom_call" | custom-call | tf_op jit(solution)/shard_map/analyse/pallas_call | solution.py:555
  89.7 0.0 copy-start.10
  89.7 0.0 copy-start.11
  89.7 5.7 %all-to-all-start.2 = ((f32[8,256,128]{2,1,0:T(8,128)}), f32[8,256,128]{2,1,0:T(8,128)S(1)}, u32[]{:S(2)}, u32[]{:S(2)}) async-start(f32[8,256,128]{2,1,0:T(8,128)} %bitcast.34), calls=%async_computation.2 | async-start | bytes 2097152 | tf_op jit(solution)/shard_map/all_to_all | solution.py:631
  95.4 0.0 copy-done.10
  95.4 0.0 copy-done.11
  95.4 0.0 copy-start.9
  95.4 1.9 %copy-done.9 = f32[3,1,1,512,512]{4,3,2,1,0:T(8,128)S(1)} copy-done((f32[3,1,1,512,512]{4,3,2,1,0:T(8,128)S(1)}, f32[3,1,1,512,512]{4,3,2,1,0:T(8,128)}, u32[]{:S(2)}) %copy-start.9) | copy-done | bytes 3145752
  97.3 3.9 %smooth.1 = f32[3,512,512]{2,1,0:T(8,128)} custom-call(bf16[512,512]{1,0:T(8,128)(2,1)S(1)} %copy-done.10, bf16[512,512]{1,0:T(8,128)(2,1)S(1)} %copy-done.11, f32[3,512,512]{2,1,0:T(8,128)S(1)} %bitcast.31), custom_call_target="tpu_custom_call" | custom-call | flops 2415919104 | bytes 6291456 | tf_op jit(solution)/shard_map/smooth/pallas_call | solution.py:588
  101.2 7.8 %all-to-all-done.2 = f32[8,256,128]{2,1,0:T(8,128)S(1)} async-done(((f32[8,256,128]{2,1,0:T(8,128)}), f32[8,256,128]{2,1,0:T(8,128)S(1)}, u32[]{:S(2)}, u32[]{:S(2)}) %all-to-all-start.2) | async-done | bytes 1048608 | tf_op jit(solution)/shard_map/all_to_all | solution.py:631
  109.0 1.0 assemble.1
Async XLA Ops:
  2.0 11.4 %collective-permute-start = (f32[72,128]{1,0:T(8,128)S(1)}, f32[72,128]{1,0:T(8,128)S(1)}, u32[]{:S(2)}, u32[]{:S(2)}) collective-permute-start(f32[72,128]{1,0:T(8,128)S(1)} %get-tuple-element.17), channel_id=1, source_target_pairs={{0,4},{4,8},{8,12},{12,16},{16,20},{20,24},{24,28},{28,32},{32,36}... | collective-permute-start | bytes 110600 | tf_op jit(solution)/shard_map/ppermute | solution.py:623
  4.5 8.9 %collective-permute-start.1 = (f32[72,128]{1,0:T(8,128)S(1)}, f32[72,128]{1,0:T(8,128)S(1)}, u32[]{:S(2)}, u32[]{:S(2)}) collective-permute-start(f32[72,128]{1,0:T(8,128)S(1)} %get-tuple-element.13), channel_id=1, source_target_pairs={{0,124},{4,0},{8,4},{12,8},{16,12},{20,16},{24,20},{28,24},{32,28}... | collective-permute-start | bytes 110600 | tf_op jit(solution)/shard_map/ppermute | solution.py:623
  13.4 6.6 %copy-start.12 = (f32[16,128]{1,0:T(8,128)}, f32[16,128]{1,0:T(8,128)S(1)}, u32[]{:S(2)}) copy-start(f32[16,128]{1,0:T(8,128)S(1)} %get-tuple-element.18.depth) | copy-start | bytes 24580
  13.4 6.6 %copy-start.5 = (f32[72,128]{1,0:T(8,128)}, f32[72,128]{1,0:T(8,128)S(1)}, u32[]{:S(2)}) copy-start(f32[72,128]{1,0:T(8,128)S(1)} %collective-permute-done.left) | copy-start | bytes 110596
  13.5 6.6 %copy-start.7 = (f32[72,128]{1,0:T(8,128)}, f32[72,128]{1,0:T(8,128)S(1)}, u32[]{:S(2)}) copy-start(f32[72,128]{1,0:T(8,128)S(1)} %collective-permute-done.1.right) | copy-start | bytes 110596
  14.7 19.7 %all-to-all-start = ((f32[8,272,128]{2,1,0:T(8,128)}), f32[8,272,128]{2,1,0:T(8,128)}, u32[]{:S(2)}, u32[]{:S(2)}) async-start(f32[8,272,128]{2,1,0:T(8,128)} %bitcast.32), calls=%async_computation | async-start | bytes 2228224 | tf_op jit(solution)/shard_map/all_to_all | solution.py:631
  22.6 11.3 %collective-permute-start.3 = (f32[64,1024]{1,0:T(8,128)S(1)}, f32[64,1024]{1,0:T(8,128)S(1)}, u32[]{:S(2)}, u32[]{:S(2)}) collective-permute-start(f32[64,1024]{1,0:T(8,128)S(1)} %heights.1.own), channel_id=1, source_target_pairs={{0,4},{4,8},{8,12},{12,16},{16,20},{20,24},{24,28},{28,32},{32,36}... | collective-permute-start | bytes 786440 | tf_op jit(solution)/shard_map/ppermute | solution.py:623
  22.7 11.2 %collective-permute-start.2 = (f32[64,1024]{1,0:T(8,128)S(1)}, f32[64,1024]{1,0:T(8,128)S(1)}, u32[]{:S(2)}, u32[]{:S(2)}) collective-permute-start(f32[64,1024]{1,0:T(8,128)S(1)} %heights.1.own), channel_id=1, source_target_pairs={{0,124},{4,0},{8,4},{12,8},{16,12},{20,16},{24,20},{28,24},{32,28}... | collective-permute-start | bytes 786440 | tf_op jit(solution)/shard_map/ppermute | solution.py:623
  42.6 5.8 %copy-start.2 = (s32[32768]{0:T(1024)S(1)}, s32[32768]{0:T(1024)}, u32[]{:S(2)}) copy-start(s32[32768]{0:T(1024)} %param.10) | copy-start | bytes 393220
  42.7 5.8 %copy-start.3 = (f32[32768]{0:T(1024)S(1)}, f32[32768]{0:T(1024)}, u32[]{:S(2)}) copy-start(f32[32768]{0:T(1024)} %param.11) | copy-start | bytes 393220
  42.7 5.8 %copy-start.4 = (f32[32768]{0:T(1024)S(1)}, f32[32768]{0:T(1024)}, u32[]{:S(2)}) copy-start(f32[32768]{0:T(1024)} %param.12) | copy-start | bytes 393220
  42.7 6.0 %copy-start.6 = (f32[72,128]{1,0:T(8,128)S(1)}, f32[72,128]{1,0:T(8,128)}, u32[]{:S(2)}) copy-start(f32[72,128]{1,0:T(8,128)} %copy-done.5) | copy-start | bytes 110596
  42.7 6.0 %copy-start.8 = (f32[72,128]{1,0:T(8,128)S(1)}, f32[72,128]{1,0:T(8,128)}, u32[]{:S(2)}) copy-start(f32[72,128]{1,0:T(8,128)} %copy-done.7) | copy-start | bytes 110596
  42.7 6.0 %copy-start.13 = (f32[16,128]{1,0:T(8,128)S(1)}, f32[16,128]{1,0:T(8,128)}, u32[]{:S(2)}) copy-start(f32[16,128]{1,0:T(8,128)} %copy-done.12) | copy-start | bytes 24580
  42.7 30.6 %all-to-all-start.1 = ((f32[8,64,1024]{2,1,0:T(8,128)}), f32[8,64,1024]{2,1,0:T(8,128)S(1)}, u32[]{:S(2)}, u32[]{:S(2)}) async-start(f32[8,64,1024]{2,1,0:T(8,128)} %pick.1), calls=%async_computation.1 | async-start | bytes 4194304 | tf_op jit(solution)/shard_map/all_to_all | solution.py:631
  52.2 1.2 %copy-start = (bf16[1536,512]{1,0:T(8,128)(2,1)}, bf16[1536,512]{1,0:T(8,128)(2,1)S(1)}, u32[]{:S(2)}) copy-start(bf16[1536,512]{1,0:T(8,128)(2,1)S(1)} %forecast.1.state) | copy-start | bytes 4718596
  73.3 1.4 %copy-start.1 = (bf16[1536,512]{1,0:T(8,128)(2,1)S(1)}, bf16[1536,512]{1,0:T(8,128)(2,1)}, u32[]{:S(2)}) copy-start(bf16[1536,512]{1,0:T(8,128)(2,1)} %copy-done) | copy-start | bytes 4718596
  89.7 5.7 %copy-start.10 = (bf16[512,512]{1,0:T(8,128)(2,1)S(1)}, bf16[512,512]{1,0:T(8,128)(2,1)}, u32[]{:S(2)}) copy-start(bf16[512,512]{1,0:T(8,128)(2,1)} %get-tuple-element.22.gain_hi) | copy-start | bytes 1572868
  89.7 5.7 %copy-start.11 = (bf16[512,512]{1,0:T(8,128)(2,1)S(1)}, bf16[512,512]{1,0:T(8,128)(2,1)}, u32[]{:S(2)}) copy-start(bf16[512,512]{1,0:T(8,128)(2,1)} %get-tuple-element.23.gain_lo) | copy-start | bytes 1572868
  89.7 19.3 %all-to-all-start.2 = ((f32[8,256,128]{2,1,0:T(8,128)}), f32[8,256,128]{2,1,0:T(8,128)S(1)}, u32[]{:S(2)}, u32[]{:S(2)}) async-start(f32[8,256,128]{2,1,0:T(8,128)} %bitcast.34), calls=%async_computation.2 | async-start | bytes 2097152 | tf_op jit(solution)/shard_map/all_to_all | solution.py:631
  95.4 1.9 %copy-start.9 = (f32[3,1,1,512,512]{4,3,2,1,0:T(8,128)S(1)}, f32[3,1,1,512,512]{4,3,2,1,0:T(8,128)}, u32[]{:S(2)}) copy-start(f32[3,1,1,512,512]{4,3,2,1,0:T(8,128)} %param.8) | copy-start | bytes 9437188

commit v8 on v7

--- a/solution.py
+++ b/solution.py
@@ -332,16 +332,13 @@
         h = height_step(h, u, 1)
         u = speed_step(h, u, 1, 3)
         for i, x in enumerate((h[1], h[2], u[1], u[2])):
-            high, low = halves(x)
-            for place, part_of in enumerate((high, low, high)):
-                at = place * MEMBERS + b * ROWS
-                state[at : at + ROWS, i * 128 : (i + 1) * 128] = part_of
+            state[b * ROWS : (b + 1) * ROWS, i * 128 : (i + 1) * 128] = x
 
 
 def forecast(received, depth, left, right):
     return pl.pallas_call(
         forecast_kernel,
-        out_shape=jax.ShapeDtypeStruct((3 * MEMBERS, STATE), bf16),
+        out_shape=jax.ShapeDtypeStruct((MEMBERS, STATE), f32),
         in_specs=[VMEM] * 4,
         out_specs=VMEM,
         scratch_shapes=[pltpu.VMEM((128, 128), f32), pltpu.VMEM((24, 128), f32)],
@@ -382,14 +379,21 @@
                 held[k, g * 8 : g * 8 + 8, j * 128 : (j + 1) * 128] = found[g]
         for j, lane, chunk, low, high in blocks:
 
-            def more(c, carry):
-                here = chunk == c
-                for g in range(ROWS // 8):
-                    at = (k, slice(g * 8, g * 8 + 8), slice(j * 128, (j + 1) * 128))
-                    held[at] = jnp.where(here, take(c, g, lane), held[at])
+            def more(i, carry):
+                c = low + DIRECT * i
+                at = [
+                    (k, slice(g * 8, g * 8 + 8), slice(j * 128, (j + 1) * 128))
+                    for g in range(ROWS // 8)
+                ]
+                found = [held[place] for place in at]
+                for d in range(DIRECT):
+                    here = chunk == c + d
+                    found = [jnp.where(here, take(c + d, g, lane), f) for g, f in enumerate(found)]
+                for place, f in zip(at, found):
+                    held[place] = f
                 return carry
 
-            lax.fori_loop(low + DIRECT, high + 1, more, 0)
+            lax.fori_loop(1, (high - low) // DIRECT + 1, more, 0)
         send(k).start()
         return carry
 
@@ -542,7 +546,8 @@
     ]
     copies[0].start()
     copies[1].start()
-    analysed = times(left, state)
+    put_right(right, state[...])
+    analysed = times(left, right)
     for row in range(4):
         at = (row % 2) * CELLS_TILE + (row // 2) * 128
         result[pl.ds(row, MEMBERS, stride=4), :] = analysed[:, at : at + 128]

time: 110 us -> 109 us (level)
  local copies, waits for them, and re-layouts: 4.53 us -> 1.94 us
  waiting for transfers between devices: 34.7 us -> 36 us
    unnamed x28 -> x24, local copies, waits for them, and re-layouts: 4.53 us -> 1.94 us
    all_to_all x3, waiting for transfers between devices: 28.2 us -> 29.5 us  [exchange(): return lax.all_to_all(x, GROUP, split_axis=0, concat_axis=0, tiled=True)]
where the time goes in v8:
time: 109 us
  Pallas kernels  39 us (36%)
  waiting for transfers between devices  36 us (33%)
  starting transfers between devices  30.6 us (28%)
  local copies, waits for them, and re-layouts  1.94 us (2%)
    all_to_all x3, waiting for transfers between devices, exchange(): return lax.all_to_all(x, GROUP, split_axis=0, concat_axis=0, tiled=True)  29.5 us
    all_to_all x3, starting transfers between devices, exchange(): return lax.all_to_all(x, GROUP, split_axis=0, concat_axis=0, tiled=True)  16.7 us
    pallas_call x1, Pallas kernels, analyse(): pl.pallas_call(analyse_kernel, out_shape=(pltpu.HBM((MEMBERS, MEMBERS), b...  15 us
    ppermute x4, starting transfers between devices, along_tiles(): lax.ppermute(x, 'tile', [(i, (i + by) % TILES) for i in range(TILES)])  13.9 us
    pallas_call x1, Pallas kernels, pick(): pl.pallas_call(pick_kernel, out_shape=pltpu.HBM((PARTS, ROWS, SLOTS), f32...  7.95 us
    ppermute x4, waiting for transfers between devices, along_tiles(): lax.ppermute(x, 'tile', [(i, (i + by) % TILES) for i in range(TILES)])  6.47 us
    pallas_call x1, Pallas kernels, smooth(): pl.pallas_call(smooth_kernel, out_shape=jax.ShapeDtypeStruct((LAGS, MEMBE...  3.93 us
    pallas_call x1, Pallas kernels, forecast(): pl.pallas_call(forecast_kernel, out_shape=jax.ShapeDtypeStruct((MEMBERS,...  3.46 us
  transfers between devices with their start and end apart: 7, of which 4 were waited for; matrix products, arithmetic and copies ran while one was open for 0% of the time, Pallas kernels for 11%

profile of v8, /device:TPU:1, one launch (start us, length us, event | category | flops | bytes accessed | tf_op | source)
XLA Modules:
  0.0 108.5 jit_solution(9993141691209153530)
XLA Ops:
  0.6 1.4 %edges.1 = (f32[2048,128]{1,0:T(8,128)S(1)}, f32[72,128]{1,0:T(8,128)S(1)}, f32[72,128]{1,0:T(8,128)S(1)}) custom-call(f32[2048,128]{1,0:T(8,128)} %bitcast.33, f32[16,128]{1,0:T(8,128)} %bitcast.36), custom_call_target="tpu_custom_call" | custom-call | tf_op jit(solution)/shard_map/edges/pallas_call | solution.py:83
  2.0 2.5 %collective-permute-start = (f32[72,128]{1,0:T(8,128)S(1)}, f32[72,128]{1,0:T(8,128)S(1)}, u32[]{:S(2)}, u32[]{:S(2)}) collective-permute-start(f32[72,128]{1,0:T(8,128)S(1)} %get-tuple-element.17), channel_id=1, source_target_pairs={{0,4},{4,8},{8,12},{12,16},{16,20},{20,24},{24,28},{28,32},{32,36}... | collective-permute-start | bytes 110600 | tf_op jit(solution)/shard_map/ppermute | solution.py:628
  4.5 6.5 %collective-permute-start.1 = (f32[72,128]{1,0:T(8,128)S(1)}, f32[72,128]{1,0:T(8,128)S(1)}, u32[]{:S(2)}, u32[]{:S(2)}) collective-permute-start(f32[72,128]{1,0:T(8,128)S(1)} %get-tuple-element.13), channel_id=1, source_target_pairs={{0,124},{4,0},{8,4},{12,8},{16,12},{20,16},{24,20},{28,24},{32,28}... | collective-permute-start | bytes 110600 | tf_op jit(solution)/shard_map/ppermute | solution.py:628
  11.0 2.4 %order.1 = (s32[8,128]{1,0:T(8,128)S(1)}, f32[8,68,4,128]{3,2,1,0:T(4,128)}, f32[16,128]{1,0:T(8,128)S(1)}, s32[8,128]{1,0:T(8,128)S(1)}) custom-call(s32[8,128]{1,0:T(8,128)} %bitcast.38, f32[64,8,4,128]{3,2,1,0:T(4,128)S(1)} %bitcast.25, f32[16,128]{1,0:T(8,128)} %bitcast.37, s32[32,8,128]{2,1,0:T(8,128)} %bitcast.27), custom_call_target="tpu_custom_call" | custom-call | bytes 104857600 | tf_op jit(solution)/shard_map/order/pallas_call | solution.py:161
  13.4 0.0 copy-start.10
  13.4 0.0 collective-permute-done.left
  13.4 0.0 copy-start.3
  13.4 0.0 collective-permute-done.1.right
  13.5 0.0 copy-start.5
  13.5 1.3 %beside.1 = f32[8,68,4,128]{3,2,1,0:T(4,128)} custom-call(f32[8,68,4,128]{3,2,1,0:T(4,128)} %get-tuple-element.16._, f32[2048,128]{1,0:T(8,128)S(1)} %get-tuple-element.15.cur, f32[72,128]{1,0:T(8,128)S(1)} %collective-permute-done.left, f32[72,128]{1,0:T(8,128)S(1)} %collective-permute-done.1.right), custom_call_target="tpu_custom_call", output_to_operand_aliasing={{}: (0, {})} | custom-call | flops 1000 | bytes 1048576 | tf_op jit(solution)/shard_map/beside/pallas_call | solution.py:214
  14.7 5.3 %all-to-all-start = ((f32[8,272,128]{2,1,0:T(8,128)}), f32[8,272,128]{2,1,0:T(8,128)}, u32[]{:S(2)}, u32[]{:S(2)}) async-start(f32[8,272,128]{2,1,0:T(8,128)} %bitcast.32), calls=%async_computation | async-start | bytes 2228224 | tf_op jit(solution)/shard_map/all_to_all | solution.py:636
  20.0 0.0 copy-done.10
  20.0 0.0 copy-done.3
  20.0 0.0 copy-done.5
  20.0 2.5 %heights.1.own = f32[64,1024]{1,0:T(8,128)S(1)} custom-call(f32[2048,128]{1,0:T(8,128)S(1)} %get-tuple-element.15.cur, f32[16,128]{1,0:T(8,128)S(1)} %get-tuple-element.18.depth, f32[72,128]{1,0:T(8,128)S(1)} %collective-permute-done.left, f32[72,128]{1,0:T(8,128)S(1)} %collective-permute-done.1.right, s32[8,128]{1,0:T(8,128)S(1)} %get-tuple-element.19.cells), custom_call_target="tpu_custom_call" | custom-call | flops 999999995904 | bytes 1048576 | tf_op jit(solution)/shard_map/heights/pallas_call | solution.py:284
  22.5 0.1 collective-permute-start.3
  22.6 4.8 %collective-permute-start.2 = (f32[64,1024]{1,0:T(8,128)S(1)}, f32[64,1024]{1,0:T(8,128)S(1)}, u32[]{:S(2)}, u32[]{:S(2)}) collective-permute-start(f32[64,1024]{1,0:T(8,128)S(1)} %heights.1.own), channel_id=1, source_target_pairs={{0,124},{4,0},{8,4},{12,8},{16,12},{20,16},{24,20},{28,24},{32,28}... | collective-permute-start | bytes 786440 | tf_op jit(solution)/shard_map/ppermute | solution.py:628
  27.4 6.5 %collective-permute-done.3.below = f32[64,1024]{1,0:T(8,128)S(1)} collective-permute-done((f32[64,1024]{1,0:T(8,128)S(1)}, f32[64,1024]{1,0:T(8,128)S(1)}, u32[]{:S(2)}, u32[]{:S(2)}) %collective-permute-start.3) | collective-permute-done | bytes 262176 | tf_op jit(solution)/shard_map/ppermute | solution.py:628
  33.9 0.0 collective-permute-done.2.above
  33.9 0.5 all-to-all-done.received
  34.4 8.0 %pick.1 = f32[8,64,1024]{2,1,0:T(8,128)} custom-call(f32[8,272,128]{2,1,0:T(8,128)} %all-to-all-done.received, f32[64,1024]{1,0:T(8,128)S(1)} %collective-permute-done.2.above, f32[64,1024]{1,0:T(8,128)S(1)} %heights.1.own, f32[64,1024]{1,0:T(8,128)S(1)} %collective-permute-done.3.below), custom_call_target="tpu_custom_call" | custom-call | flops 999999995904 | bytes 1048576 | tf_op jit(solution)/shard_map/pick/pallas_call | solution.py:406
  42.4 0.0 copy-start
  42.4 0.0 copy-start.1
  42.4 0.0 copy-start.2
  42.4 0.0 copy-start.4
  42.4 0.0 copy-start.6
  42.4 0.0 copy-start.11
  42.4 5.7 %all-to-all-start.1 = ((f32[8,64,1024]{2,1,0:T(8,128)}), f32[8,64,1024]{2,1,0:T(8,128)S(1)}, u32[]{:S(2)}, u32[]{:S(2)}) async-start(f32[8,64,1024]{2,1,0:T(8,128)} %pick.1), calls=%async_computation.1 | async-start | bytes 4194304 | tf_op jit(solution)/shard_map/all_to_all | solution.py:636
  48.2 0.0 copy-done
  48.2 0.0 copy-done.1
  48.2 0.0 copy-done.2
  48.2 0.2 slots.1.slot_rows
  48.4 0.0 copy-done.4
  48.4 0.0 copy-done.6
  48.4 0.0 copy-done.11
  48.4 3.5 %forecast.1.state = f32[512,512]{1,0:T(8,128)S(1)} custom-call(f32[8,272,128]{2,1,0:T(8,128)} %all-to-all-done.received, f32[16,128]{1,0:T(8,128)S(1)} %copy-done.11, f32[72,128]{1,0:T(8,128)S(1)} %copy-done.4, f32[72,128]{1,0:T(8,128)S(1)} %copy-done.6), custom_call_target="tpu_custom_call" | custom-call | flops 10000000000 | bytes 1048576 | tf_op jit(solution)/shard_map/forecast/pallas_call | solution.py:339
  51.9 21.2 %all-to-all-done.1 = f32[8,64,1024]{2,1,0:T(8,128)S(1)} async-done(((f32[8,64,1024]{2,1,0:T(8,128)}), f32[8,64,1024]{2,1,0:T(8,128)S(1)}, u32[]{:S(2)}, u32[]{:S(2)}) %all-to-all-start.1) | async-done | bytes 2097184 | tf_op jit(solution)/shard_map/all_to_all | solution.py:636
  73.0 15.0 %analyse.1 = (bf16[512,512]{1,0:T(8,128)(2,1)}, bf16[512,512]{1,0:T(8,128)(2,1)}, f32[2048,128]{1,0:T(8,128)}) custom-call(f32[512,1024]{1,0:T(8,128)S(1)} %bitcast.24, f32[8,1024]{1,0:T(8,128)S(1)} %slots.1.slot_rows, f32[512,512]{1,0:T(8,128)S(1)} %forecast.1.state), custom_call_target="tpu_custom_call" | custom-call | tf_op jit(solution)/shard_map/analyse/pallas_call | solution.py:560
  88.0 0.0 copy-start.8
  88.0 0.0 copy-start.9
  88.0 5.7 %all-to-all-start.2 = ((f32[8,256,128]{2,1,0:T(8,128)}), f32[8,256,128]{2,1,0:T(8,128)S(1)}, u32[]{:S(2)}, u32[]{:S(2)}) async-start(f32[8,256,128]{2,1,0:T(8,128)} %bitcast.34), calls=%async_computation.2 | async-start | bytes 2097152 | tf_op jit(solution)/shard_map/all_to_all | solution.py:636
  93.7 0.0 copy-done.8
  93.7 0.0 copy-done.9
  93.7 0.0 copy-start.7
  93.8 1.9 %copy-done.7 = f32[3,1,1,512,512]{4,3,2,1,0:T(8,128)S(1)} copy-done((f32[3,1,1,512,512]{4,3,2,1,0:T(8,128)S(1)}, f32[3,1,1,512,512]{4,3,2,1,0:T(8,128)}, u32[]{:S(2)}) %copy-start.7) | copy-done | bytes 3145752
  95.6 3.9 %smooth.1 = f32[3,512,512]{2,1,0:T(8,128)} custom-call(bf16[512,512]{1,0:T(8,128)(2,1)S(1)} %copy-done.8, bf16[512,512]{1,0:T(8,128)(2,1)S(1)} %copy-done.9, f32[3,512,512]{2,1,0:T(8,128)S(1)} %bitcast.31), custom_call_target="tpu_custom_call" | custom-call | flops 2415919104 | bytes 6291456 | tf_op jit(solution)/shard_map/smooth/pallas_call | solution.py:593
  99.6 7.8 %all-to-all-done.2 = f32[8,256,128]{2,1,0:T(8,128)S(1)} async-done(((f32[8,256,128]{2,1,0:T(8,128)}), f32[8,256,128]{2,1,0:T(8,128)S(1)}, u32[]{:S(2)}, u32[]{:S(2)}) %all-to-all-start.2) | async-done | bytes 1048608 | tf_op jit(solution)/shard_map/all_to_all | solution.py:636
  107.3 1.0 assemble.1
Async XLA Ops:
  2.0 11.4 %collective-permute-start = (f32[72,128]{1,0:T(8,128)S(1)}, f32[72,128]{1,0:T(8,128)S(1)}, u32[]{:S(2)}, u32[]{:S(2)}) collective-permute-start(f32[72,128]{1,0:T(8,128)S(1)} %get-tuple-element.17), channel_id=1, source_target_pairs={{0,4},{4,8},{8,12},{12,16},{16,20},{20,24},{24,28},{28,32},{32,36}... | collective-permute-start | bytes 110600 | tf_op jit(solution)/shard_map/ppermute | solution.py:628
  4.5 8.9 %collective-permute-start.1 = (f32[72,128]{1,0:T(8,128)S(1)}, f32[72,128]{1,0:T(8,128)S(1)}, u32[]{:S(2)}, u32[]{:S(2)}) collective-permute-start(f32[72,128]{1,0:T(8,128)S(1)} %get-tuple-element.13), channel_id=1, source_target_pairs={{0,124},{4,0},{8,4},{12,8},{16,12},{20,16},{24,20},{28,24},{32,28}... | collective-permute-start | bytes 110600 | tf_op jit(solution)/shard_map/ppermute | solution.py:628
  13.4 6.6 %copy-start.10 = (f32[16,128]{1,0:T(8,128)}, f32[16,128]{1,0:T(8,128)S(1)}, u32[]{:S(2)}) copy-start(f32[16,128]{1,0:T(8,128)S(1)} %get-tuple-element.18.depth) | copy-start | bytes 24580
  13.4 6.6 %copy-start.3 = (f32[72,128]{1,0:T(8,128)}, f32[72,128]{1,0:T(8,128)S(1)}, u32[]{:S(2)}) copy-start(f32[72,128]{1,0:T(8,128)S(1)} %collective-permute-done.left) | copy-start | bytes 110596
  13.5 6.6 %copy-start.5 = (f32[72,128]{1,0:T(8,128)}, f32[72,128]{1,0:T(8,128)S(1)}, u32[]{:S(2)}) copy-start(f32[72,128]{1,0:T(8,128)S(1)} %collective-permute-done.1.right) | copy-start | bytes 110596
  14.7 19.7 %all-to-all-start = ((f32[8,272,128]{2,1,0:T(8,128)}), f32[8,272,128]{2,1,0:T(8,128)}, u32[]{:S(2)}, u32[]{:S(2)}) async-start(f32[8,272,128]{2,1,0:T(8,128)} %bitcast.32), calls=%async_computation | async-start | bytes 2228224 | tf_op jit(solution)/shard_map/all_to_all | solution.py:636
  22.5 11.3 %collective-permute-start.3 = (f32[64,1024]{1,0:T(8,128)S(1)}, f32[64,1024]{1,0:T(8,128)S(1)}, u32[]{:S(2)}, u32[]{:S(2)}) collective-permute-start(f32[64,1024]{1,0:T(8,128)S(1)} %heights.1.own), channel_id=1, source_target_pairs={{0,4},{4,8},{8,12},{12,16},{16,20},{20,24},{24,28},{28,32},{32,36}... | collective-permute-start | bytes 786440 | tf_op jit(solution)/shard_map/ppermute | solution.py:628
  22.6 11.2 %collective-permute-start.2 = (f32[64,1024]{1,0:T(8,128)S(1)}, f32[64,1024]{1,0:T(8,128)S(1)}, u32[]{:S(2)}, u32[]{:S(2)}) collective-permute-start(f32[64,1024]{1,0:T(8,128)S(1)} %heights.1.own), channel_id=1, source_target_pairs={{0,124},{4,0},{8,4},{12,8},{16,12},{20,16},{24,20},{28,24},{32,28}... | collective-permute-start | bytes 786440 | tf_op jit(solution)/shard_map/ppermute | solution.py:628
  42.4 5.8 %copy-start = (s32[32768]{0:T(1024)S(1)}, s32[32768]{0:T(1024)}, u32[]{:S(2)}) copy-start(s32[32768]{0:T(1024)} %param.10) | copy-start | bytes 393220
  42.4 5.8 %copy-start.1 = (f32[32768]{0:T(1024)S(1)}, f32[32768]{0:T(1024)}, u32[]{:S(2)}) copy-start(f32[32768]{0:T(1024)} %param.11) | copy-start | bytes 393220
  42.4 5.8 %copy-start.2 = (f32[32768]{0:T(1024)S(1)}, f32[32768]{0:T(1024)}, u32[]{:S(2)}) copy-start(f32[32768]{0:T(1024)} %param.12) | copy-start | bytes 393220
  42.4 6.0 %copy-start.4 = (f32[72,128]{1,0:T(8,128)S(1)}, f32[72,128]{1,0:T(8,128)}, u32[]{:S(2)}) copy-start(f32[72,128]{1,0:T(8,128)} %copy-done.3) | copy-start | bytes 110596
  42.4 6.0 %copy-start.6 = (f32[72,128]{1,0:T(8,128)S(1)}, f32[72,128]{1,0:T(8,128)}, u32[]{:S(2)}) copy-start(f32[72,128]{1,0:T(8,128)} %copy-done.5) | copy-start | bytes 110596
  42.4 6.0 %copy-start.11 = (f32[16,128]{1,0:T(8,128)S(1)}, f32[16,128]{1,0:T(8,128)}, u32[]{:S(2)}) copy-start(f32[16,128]{1,0:T(8,128)} %copy-done.10) | copy-start | bytes 24580
  42.4 30.6 %all-to-all-start.1 = ((f32[8,64,1024]{2,1,0:T(8,128)}), f32[8,64,1024]{2,1,0:T(8,128)S(1)}, u32[]{:S(2)}, u32[]{:S(2)}) async-start(f32[8,64,1024]{2,1,0:T(8,128)} %pick.1), calls=%async_computation.1 | async-start | bytes 4194304 | tf_op jit(solution)/shard_map/all_to_all | solution.py:636
  88.0 5.7 %copy-start.8 = (bf16[512,512]{1,0:T(8,128)(2,1)S(1)}, bf16[512,512]{1,0:T(8,128)(2,1)}, u32[]{:S(2)}) copy-start(bf16[512,512]{1,0:T(8,128)(2,1)} %get-tuple-element.22.gain_hi) | copy-start | bytes 1572868
  88.0 5.7 %copy-start.9 = (bf16[512,512]{1,0:T(8,128)(2,1)S(1)}, bf16[512,512]{1,0:T(8,128)(2,1)}, u32[]{:S(2)}) copy-start(bf16[512,512]{1,0:T(8,128)(2,1)} %get-tuple-element.23.gain_lo) | copy-start | bytes 1572868
  88.0 19.3 %all-to-all-start.2 = ((f32[8,256,128]{2,1,0:T(8,128)}), f32[8,256,128]{2,1,0:T(8,128)S(1)}, u32[]{:S(2)}, u32[]{:S(2)}) async-start(f32[8,256,128]{2,1,0:T(8,128)} %bitcast.34), calls=%async_computation.2 | async-start | bytes 2097152 | tf_op jit(solution)/shard_map/all_to_all | solution.py:636
  93.7 1.9 %copy-start.7 = (f32[3,1,1,512,512]{4,3,2,1,0:T(8,128)S(1)}, f32[3,1,1,512,512]{4,3,2,1,0:T(8,128)}, u32[]{:S(2)}) copy-start(f32[3,1,1,512,512]{4,3,2,1,0:T(8,128)} %param.8) | copy-start | bytes 9437188

commit v9 on v8

--- a/solution.py
+++ b/solution.py
@@ -24,6 +24,8 @@
 LOC = 512
 LAGS = 3
 DIRECT = 3
+OUTER = (0, PARTS - 1)
+INNER = range(1, PARTS - 1)
 f32 = jnp.float32
 bf16 = jnp.bfloat16
 VMEM = pl.BlockSpec(memory_space=pltpu.VMEM)
@@ -92,8 +94,8 @@
 
 
 def order_kernel(
-    far_list, by_part, far_depth, far_cells,
-    ordered, payload, depth, cells, tile_list, row_list, row_place, filled, sems, sent,
+    far_list, by_part, cur, far_depth, far_cells,
+    ordered, payload, depth, cells, tile_list, row_list, row_place, filled, rows, sems, sent,
 ):
     tile = lax.axis_index("tile")
     arrivals = [
@@ -108,6 +110,7 @@
     ]
     for copy in arrivals + raw:
         copy.start()
+    beside = [put_beside(k, cur, None, None, payload, rows, sent.at[2 * PARTS + k]) for k in INNER]
     arrivals[0].wait()
     listed = tile_list[...]
     rel = jnp.where(listed >= 0, (listed - (tile - 1) * OBS) & (NOBS - 1), -1)
@@ -152,12 +155,12 @@
     ]
     for copy in lists:
         copy.start()
-    for copy in arrivals[1:] + raw + lists:
+    for copy in arrivals[1:] + raw + lists + beside:
         copy.wait()
     cells[...] = cells[...] - tile * CELLS
 
 
-def order(tile_list, parts, depth, cells):
+def order(tile_list, parts, cur, depth, cells):
     return pl.pallas_call(
         order_kernel,
         out_shape=(
@@ -166,20 +169,21 @@
             jax.ShapeDtypeStruct((CHUNKS, 128), f32),
             jax.ShapeDtypeStruct((8, 128), jnp.int32),
         ),
-        in_specs=[HBM, VMEM, HBM, HBM],
+        in_specs=[HBM, VMEM, VMEM, HBM, HBM],
         out_specs=(VMEM, HBM, VMEM, VMEM),
         scratch_shapes=[
             pltpu.VMEM((8, 128), jnp.int32),
             pltpu.VMEM((8, SLOTS), jnp.int32),
             pltpu.VMEM((8, 3 * OBS), jnp.int32),
             pltpu.VMEM((2, 4, 128), f32),
+            pltpu.VMEM((PARTS, 2, 4, 128), f32),
             pltpu.SemaphoreType.DMA((3,)),
-            pltpu.SemaphoreType.DMA((2 * PARTS,)),
+            pltpu.SemaphoreType.DMA((3 * PARTS,)),
         ],
         cost_estimate=pl.CostEstimate(flops=0, bytes_accessed=100 * 2**20, transcendentals=0),
         compiler_params=params(12),
         name="order",
-    )(tile_list, parts, depth, cells)
+    )(tile_list, parts, cur, depth, cells)
 
 
 def chunk_with_halo(cur, left, right, c, v):
@@ -192,21 +196,20 @@
     return cur[pl.ds(2 * c + v, ROWS, stride=2 * CHUNKS), :]
 
 
-def beside_kernel(_, cur, left, right, payload, rows, sems):
+def put_beside(k, cur, left, right, payload, rows, sem):
     def turned(c):
         pair = [chunk_with_halo(cur, left, right, c, v) for v in range(2)]
         return jnp.concatenate(pair, axis=0).T
 
-    upper = lax.broadcasted_iota(jnp.int32, (8, 128), 0) < 4
-    copies = []
-    for k in range(PARTS):
-        chosen = jnp.where(upper, turned(2 * k + 2)[:8], turned(2 * k - 1)[120:])
-        rows[k, 0], rows[k, 1] = chosen[:4], chosen[4:]
-        copies.append(
-            pltpu.make_async_copy(rows.at[k], payload.at[k, pl.ds(ROWS + 2, 2)], sems.at[k])
-        )
-        copies[k].start()
-    for copy in copies:
+    rows[k, 0] = turned(2 * k + 2)[:4]
+    rows[k, 1] = turned(2 * k - 1)[124:]
+    copy = pltpu.make_async_copy(rows.at[k], payload.at[k, pl.ds(ROWS + 2, 2)], sem)
+    copy.start()
+    return copy
+
+
+def beside_kernel(_, cur, left, right, payload, rows, sems):
+    for copy in [put_beside(k, cur, left, right, payload, rows, sems.at[k]) for k in OUTER]:
         copy.wait()
 
 
@@ -348,7 +351,7 @@
     )(received, depth, left, right)
 
 
-def pick_kernel(received, above, own, below, out, source, held, lists, bounds, sems, list_sem):
+def pick_kernel(received, below, own, above, out, source, held, lists, bounds, sems, list_sem):
     for k in range(PARTS):
         lists[k] = received[k, 4 * ROWS : 4 * ROWS + 8, :].astype(jnp.int32)
     to_scalars = pltpu.make_async_copy(lists, bounds, list_sem)
@@ -402,7 +405,7 @@
         send(k).wait()
 
 
-def pick(received, above, own, below):
+def pick(received, below, own, above):
     return pl.pallas_call(
         pick_kernel,
         out_shape=pltpu.HBM((PARTS, ROWS, SLOTS), f32),
@@ -419,7 +422,7 @@
         compiler_params=params(16),
         cost_estimate=cost(10**12),
         name="pick",
-    )(received, above, own, below)
+    )(received, below, own, above)
 
 
 def slots_kernel(rel, values, errors, cells, out):
@@ -648,6 +651,7 @@
     ordered, payload, depth, cells = order(
         far(listed),
         cur.reshape(ROWS, PARTS, 4, 128),
+        cur,
         far(depth),
         far(obs_cells.reshape(TILES, 8, 128)),
     )
@@ -656,7 +660,7 @@
     own = heights(cur, depth, left, right, cells)
     below = along_tiles(own, 1)
     above = along_tiles(own, -1)
-    picked = pick(received, above, own, below)
+    picked = pick(received, below, own, above)
     predicted = exchange(picked).reshape(MEMBERS, SLOTS)
     state = forecast(received, depth, left, right)
     slot_rows = slots(

time: 109 us -> 113 us (1.037)
  waiting for transfers between devices: 36 us -> 39.1 us
    ppermute x4, waiting for transfers between devices: 6.47 us -> 9.64 us  [along_tiles(): lax.ppermute(x, 'tile', [(i, (i + by) % TILES) for i in range(TILES)])]
    all_to_all x3, starting transfers between devices: 16.7 us -> 17.8 us  [exchange(): return lax.all_to_all(x, GROUP, split_axis=0, concat_axis=0, tiled=True)]
  transfers between devices with their start and end apart: 7 -> 7, of which waited for: 4 -> 5; matrix products, arithmetic and copies ran while one was open for 0% -> 0% of each run, Pallas kernels for 11% -> 12%
where the time goes in v9:
time: 113 us; the launch traced here: 112 us
  waiting for transfers between devices  39.1 us (35%)
  Pallas kernels  38.5 us (34%)
  starting transfers between devices  31.6 us (28%)
  local copies, waits for them, and re-layouts  1.94 us (2%)
    all_to_all x3, waiting for transfers between devices, exchange(): return lax.all_to_all(x, GROUP, split_axis=0, concat_axis=0, tiled=True)  29.5 us
    all_to_all x3, starting transfers between devices, exchange(): return lax.all_to_all(x, GROUP, split_axis=0, concat_axis=0, tiled=True)  17.8 us
    pallas_call x1, Pallas kernels, analyse(): pl.pallas_call(analyse_kernel, out_shape=(pltpu.HBM((MEMBERS, MEMBERS), b...  15 us
    ppermute x4, starting transfers between devices, along_tiles(): lax.ppermute(x, 'tile', [(i, (i + by) % TILES) for i in range(TILES)])  13.8 us
    ppermute x4, waiting for transfers between devices, along_tiles(): lax.ppermute(x, 'tile', [(i, (i + by) % TILES) for i in range(TILES)])  9.64 us
    pallas_call x1, Pallas kernels, pick(): pl.pallas_call(pick_kernel, out_shape=pltpu.HBM((PARTS, ROWS, SLOTS), f32...  7.32 us
    pallas_call x1, Pallas kernels, smooth(): pl.pallas_call(smooth_kernel, out_shape=jax.ShapeDtypeStruct((LAGS, MEMBE...  3.93 us
    pallas_call x1, Pallas kernels, forecast(): pl.pallas_call(forecast_kernel, out_shape=jax.ShapeDtypeStruct((MEMBERS,...  3.46 us
  transfers between devices with their start and end apart: 7, of which 5 were waited for; matrix products, arithmetic and copies ran while one was open for 0% of the time, Pallas kernels for 12%

profile of v9, /device:TPU:1, one launch (start us, length us, event | category | flops | bytes accessed | tf_op | source)
XLA Modules:
  0.0 112.2 jit_solution(17186808136356723700)
XLA Ops:
  0.6 1.4 %edges.1 = (f32[2048,128]{1,0:T(8,128)S(1)}, f32[72,128]{1,0:T(8,128)S(1)}, f32[72,128]{1,0:T(8,128)S(1)}) custom-call(f32[2048,128]{1,0:T(8,128)} %bitcast.33, f32[16,128]{1,0:T(8,128)} %bitcast.36), custom_call_target="tpu_custom_call" | custom-call | tf_op jit(solution)/shard_map/edges/pallas_call | solution.py:85
  2.0 8.9 %collective-permute-start.1 = (f32[72,128]{1,0:T(8,128)S(1)}, f32[72,128]{1,0:T(8,128)S(1)}, u32[]{:S(2)}, u32[]{:S(2)}) collective-permute-start(f32[72,128]{1,0:T(8,128)S(1)} %get-tuple-element.13), channel_id=1, source_target_pairs={{0,124},{4,0},{8,4},{12,8},{16,12},{20,16},{24,20},{28,24},{32,28}... | collective-permute-start | bytes 110600 | tf_op jit(solution)/shard_map/ppermute | solution.py:631
  10.9 0.0 collective-permute-start
  10.9 2.9 %order.1 = (s32[8,128]{1,0:T(8,128)S(1)}, f32[8,68,4,128]{3,2,1,0:T(4,128)}, f32[16,128]{1,0:T(8,128)S(1)}, s32[8,128]{1,0:T(8,128)S(1)}) custom-call(s32[8,128]{1,0:T(8,128)} %bitcast.38, f32[64,8,4,128]{3,2,1,0:T(4,128)S(1)} %bitcast.24, f32[2048,128]{1,0:T(8,128)S(1)} %get-tuple-element.15.cur, f32[16,128]{1,0:T(8,128)} %bitcast.37, s32[32,8,128]{2,1,0:T(8,128)} %bitcast.27), custom_call_target="tpu_custom_call" | custom-call | bytes 104857600 | tf_op jit(solution)/shard_map/order/pallas_call | solution.py:164
  13.9 0.0 copy-start.10
  13.9 0.0 collective-permute-done.1.right
  13.9 0.0 copy-start.3
  13.9 3.2 %collective-permute-done.left = f32[72,128]{1,0:T(8,128)S(1)} collective-permute-done((f32[72,128]{1,0:T(8,128)S(1)}, f32[72,128]{1,0:T(8,128)S(1)}, u32[]{:S(2)}, u32[]{:S(2)}) %collective-permute-start) | collective-permute-done | bytes 36896 | tf_op jit(solution)/shard_map/ppermute | solution.py:631
  17.1 0.0 copy-start.5
  17.1 0.9 beside.1
  17.9 6.4 %all-to-all-start = ((f32[8,272,128]{2,1,0:T(8,128)}), f32[8,272,128]{2,1,0:T(8,128)}, u32[]{:S(2)}, u32[]{:S(2)}) async-start(f32[8,272,128]{2,1,0:T(8,128)} %bitcast.32), calls=%async_computation | async-start | bytes 2228224 | tf_op jit(solution)/shard_map/all_to_all | solution.py:639
  24.3 0.0 copy-done.10
  24.4 0.0 copy-done.3
  24.4 0.0 copy-done.5
  24.4 2.5 %heights.1.own = f32[64,1024]{1,0:T(8,128)S(1)} custom-call(f32[2048,128]{1,0:T(8,128)S(1)} %get-tuple-element.15.cur, f32[16,128]{1,0:T(8,128)S(1)} %get-tuple-element.18.depth, f32[72,128]{1,0:T(8,128)S(1)} %collective-permute-done.left, f32[72,128]{1,0:T(8,128)S(1)} %collective-permute-done.1.right, s32[8,128]{1,0:T(8,128)S(1)} %get-tuple-element.19.cells), custom_call_target="tpu_custom_call" | custom-call | flops 999999995904 | bytes 1048576 | tf_op jit(solution)/shard_map/heights/pallas_call | solution.py:287
  26.9 0.1 collective-permute-start.2
  27.0 4.8 %collective-permute-start.3 = (f32[64,1024]{1,0:T(8,128)S(1)}, f32[64,1024]{1,0:T(8,128)S(1)}, u32[]{:S(2)}, u32[]{:S(2)}) collective-permute-start(f32[64,1024]{1,0:T(8,128)S(1)} %heights.1.own), channel_id=1, source_target_pairs={{0,124},{4,0},{8,4},{12,8},{16,12},{20,16},{24,20},{28,24},{32,28}... | collective-permute-start | bytes 786440 | tf_op jit(solution)/shard_map/ppermute | solution.py:631
  31.7 6.5 %collective-permute-done.2.below = f32[64,1024]{1,0:T(8,128)S(1)} collective-permute-done((f32[64,1024]{1,0:T(8,128)S(1)}, f32[64,1024]{1,0:T(8,128)S(1)}, u32[]{:S(2)}, u32[]{:S(2)}) %collective-permute-start.2) | collective-permute-done | bytes 262176 | tf_op jit(solution)/shard_map/ppermute | solution.py:631
  38.2 0.0 collective-permute-done.3.above
  38.2 0.5 all-to-all-done.received
  38.8 7.3 %pick.1 = f32[8,64,1024]{2,1,0:T(8,128)} custom-call(f32[8,272,128]{2,1,0:T(8,128)} %all-to-all-done.received, f32[64,1024]{1,0:T(8,128)S(1)} %collective-permute-done.2.below, f32[64,1024]{1,0:T(8,128)S(1)} %heights.1.own, f32[64,1024]{1,0:T(8,128)S(1)} %collective-permute-done.3.above), custom_call_target="tpu_custom_call" | custom-call | flops 999999995904 | bytes 1048576 | tf_op jit(solution)/shard_map/pick/pallas_call | solution.py:409
  46.1 0.0 copy-start
  46.1 0.0 copy-start.1
  46.1 0.0 copy-start.2
  46.1 0.0 copy-start.4
  46.1 0.0 copy-start.6
  46.1 0.0 copy-start.11
  46.1 5.7 %all-to-all-start.1 = ((f32[8,64,1024]{2,1,0:T(8,128)}), f32[8,64,1024]{2,1,0:T(8,128)S(1)}, u32[]{:S(2)}, u32[]{:S(2)}) async-start(f32[8,64,1024]{2,1,0:T(8,128)} %pick.1), calls=%async_computation.1 | async-start | bytes 4194304 | tf_op jit(solution)/shard_map/all_to_all | solution.py:639
  51.9 0.0 copy-done
  51.9 0.0 copy-done.1
  51.9 0.0 copy-done.2
  51.9 0.2 slots.1.slot_rows
  52.1 0.0 copy-done.4
  52.1 0.0 copy-done.6
  52.1 0.0 copy-done.11
  52.1 3.5 %forecast.1.state = f32[512,512]{1,0:T(8,128)S(1)} custom-call(f32[8,272,128]{2,1,0:T(8,128)} %all-to-all-done.received, f32[16,128]{1,0:T(8,128)S(1)} %copy-done.11, f32[72,128]{1,0:T(8,128)S(1)} %copy-done.6, f32[72,128]{1,0:T(8,128)S(1)} %copy-done.4), custom_call_target="tpu_custom_call" | custom-call | flops 10000000000 | bytes 1048576 | tf_op jit(solution)/shard_map/forecast/pallas_call | solution.py:342
  55.6 21.2 %all-to-all-done.1 = f32[8,64,1024]{2,1,0:T(8,128)S(1)} async-done(((f32[8,64,1024]{2,1,0:T(8,128)}), f32[8,64,1024]{2,1,0:T(8,128)S(1)}, u32[]{:S(2)}, u32[]{:S(2)}) %all-to-all-start.1) | async-done | bytes 2097184 | tf_op jit(solution)/shard_map/all_to_all | solution.py:639
  76.7 15.0 %analyse.1 = (bf16[512,512]{1,0:T(8,128)(2,1)}, bf16[512,512]{1,0:T(8,128)(2,1)}, f32[2048,128]{1,0:T(8,128)}) custom-call(f32[512,1024]{1,0:T(8,128)S(1)} %bitcast.25, f32[8,1024]{1,0:T(8,128)S(1)} %slots.1.slot_rows, f32[512,512]{1,0:T(8,128)S(1)} %forecast.1.state), custom_call_target="tpu_custom_call" | custom-call | tf_op jit(solution)/shard_map/analyse/pallas_call | solution.py:563
  91.7 0.0 copy-start.8
  91.7 0.0 copy-start.9
  91.7 5.7 %all-to-all-start.2 = ((f32[8,256,128]{2,1,0:T(8,128)}), f32[8,256,128]{2,1,0:T(8,128)S(1)}, u32[]{:S(2)}, u32[]{:S(2)}) async-start(f32[8,256,128]{2,1,0:T(8,128)} %bitcast.34), calls=%async_computation.2 | async-start | bytes 2097152 | tf_op jit(solution)/shard_map/all_to_all | solution.py:639
  97.4 0.0 copy-done.8
  97.4 0.0 copy-done.9
  97.4 0.0 copy-start.7
  97.5 1.9 %copy-done.7 = f32[3,1,1,512,512]{4,3,2,1,0:T(8,128)S(1)} copy-done((f32[3,1,1,512,512]{4,3,2,1,0:T(8,128)S(1)}, f32[3,1,1,512,512]{4,3,2,1,0:T(8,128)}, u32[]{:S(2)}) %copy-start.7) | copy-done | bytes 3145752
  99.3 3.9 %smooth.1 = f32[3,512,512]{2,1,0:T(8,128)} custom-call(bf16[512,512]{1,0:T(8,128)(2,1)S(1)} %copy-done.8, bf16[512,512]{1,0:T(8,128)(2,1)S(1)} %copy-done.9, f32[3,512,512]{2,1,0:T(8,128)S(1)} %bitcast.31), custom_call_target="tpu_custom_call" | custom-call | flops 2415919104 | bytes 6291456 | tf_op jit(solution)/shard_map/smooth/pallas_call | solution.py:596
  103.3 7.8 %all-to-all-done.2 = f32[8,256,128]{2,1,0:T(8,128)S(1)} async-done(((f32[8,256,128]{2,1,0:T(8,128)}), f32[8,256,128]{2,1,0:T(8,128)S(1)}, u32[]{:S(2)}, u32[]{:S(2)}) %all-to-all-start.2) | async-done | bytes 1048608 | tf_op jit(solution)/shard_map/all_to_all | solution.py:639
  111.0 1.0 assemble.1
Async XLA Ops:
  2.0 11.9 %collective-permute-start.1 = (f32[72,128]{1,0:T(8,128)S(1)}, f32[72,128]{1,0:T(8,128)S(1)}, u32[]{:S(2)}, u32[]{:S(2)}) collective-permute-start(f32[72,128]{1,0:T(8,128)S(1)} %get-tuple-element.13), channel_id=1, source_target_pairs={{0,124},{4,0},{8,4},{12,8},{16,12},{20,16},{24,20},{28,24},{32,28}... | collective-permute-start | bytes 110600 | tf_op jit(solution)/shard_map/ppermute | solution.py:631
  10.9 6.1 %collective-permute-start = (f32[72,128]{1,0:T(8,128)S(1)}, f32[72,128]{1,0:T(8,128)S(1)}, u32[]{:S(2)}, u32[]{:S(2)}) collective-permute-start(f32[72,128]{1,0:T(8,128)S(1)} %get-tuple-element.17), channel_id=1, source_target_pairs={{0,4},{4,8},{8,12},{12,16},{16,20},{20,24},{24,28},{28,32},{32,36}... | collective-permute-start | bytes 110600 | tf_op jit(solution)/shard_map/ppermute | solution.py:631
  13.9 10.5 %copy-start.10 = (f32[16,128]{1,0:T(8,128)}, f32[16,128]{1,0:T(8,128)S(1)}, u32[]{:S(2)}) copy-start(f32[16,128]{1,0:T(8,128)S(1)} %get-tuple-element.18.depth) | copy-start | bytes 24580
  13.9 10.5 %copy-start.3 = (f32[72,128]{1,0:T(8,128)}, f32[72,128]{1,0:T(8,128)S(1)}, u32[]{:S(2)}) copy-start(f32[72,128]{1,0:T(8,128)S(1)} %collective-permute-done.1.right) | copy-start | bytes 110596
  17.1 7.3 %copy-start.5 = (f32[72,128]{1,0:T(8,128)}, f32[72,128]{1,0:T(8,128)S(1)}, u32[]{:S(2)}) copy-start(f32[72,128]{1,0:T(8,128)S(1)} %collective-permute-done.left) | copy-start | bytes 110596
  17.9 20.8 %all-to-all-start = ((f32[8,272,128]{2,1,0:T(8,128)}), f32[8,272,128]{2,1,0:T(8,128)}, u32[]{:S(2)}, u32[]{:S(2)}) async-start(f32[8,272,128]{2,1,0:T(8,128)} %bitcast.32), calls=%async_computation | async-start | bytes 2228224 | tf_op jit(solution)/shard_map/all_to_all | solution.py:639
  26.9 11.3 %collective-permute-start.2 = (f32[64,1024]{1,0:T(8,128)S(1)}, f32[64,1024]{1,0:T(8,128)S(1)}, u32[]{:S(2)}, u32[]{:S(2)}) collective-permute-start(f32[64,1024]{1,0:T(8,128)S(1)} %heights.1.own), channel_id=1, source_target_pairs={{0,4},{4,8},{8,12},{12,16},{16,20},{20,24},{24,28},{28,32},{32,36}... | collective-permute-start | bytes 786440 | tf_op jit(solution)/shard_map/ppermute | solution.py:631
  27.0 11.2 %collective-permute-start.3 = (f32[64,1024]{1,0:T(8,128)S(1)}, f32[64,1024]{1,0:T(8,128)S(1)}, u32[]{:S(2)}, u32[]{:S(2)}) collective-permute-start(f32[64,1024]{1,0:T(8,128)S(1)} %heights.1.own), channel_id=1, source_target_pairs={{0,124},{4,0},{8,4},{12,8},{16,12},{20,16},{24,20},{28,24},{32,28}... | collective-permute-start | bytes 786440 | tf_op jit(solution)/shard_map/ppermute | solution.py:631
  46.1 5.8 %copy-start = (s32[32768]{0:T(1024)S(1)}, s32[32768]{0:T(1024)}, u32[]{:S(2)}) copy-start(s32[32768]{0:T(1024)} %param.10) | copy-start | bytes 393220
  46.1 5.8 %copy-start.1 = (f32[32768]{0:T(1024)S(1)}, f32[32768]{0:T(1024)}, u32[]{:S(2)}) copy-start(f32[32768]{0:T(1024)} %param.11) | copy-start | bytes 393220
  46.1 5.8 %copy-start.2 = (f32[32768]{0:T(1024)S(1)}, f32[32768]{0:T(1024)}, u32[]{:S(2)}) copy-start(f32[32768]{0:T(1024)} %param.12) | copy-start | bytes 393220
  46.1 6.0 %copy-start.4 = (f32[72,128]{1,0:T(8,128)S(1)}, f32[72,128]{1,0:T(8,128)}, u32[]{:S(2)}) copy-start(f32[72,128]{1,0:T(8,128)} %copy-done.3) | copy-start | bytes 110596
  46.1 6.0 %copy-start.6 = (f32[72,128]{1,0:T(8,128)S(1)}, f32[72,128]{1,0:T(8,128)}, u32[]{:S(2)}) copy-start(f32[72,128]{1,0:T(8,128)} %copy-done.5) | copy-start | bytes 110596
  46.1 6.0 %copy-start.11 = (f32[16,128]{1,0:T(8,128)S(1)}, f32[16,128]{1,0:T(8,128)}, u32[]{:S(2)}) copy-start(f32[16,128]{1,0:T(8,128)} %copy-done.10) | copy-start | bytes 24580
  46.1 30.6 %all-to-all-start.1 = ((f32[8,64,1024]{2,1,0:T(8,128)}), f32[8,64,1024]{2,1,0:T(8,128)S(1)}, u32[]{:S(2)}, u32[]{:S(2)}) async-start(f32[8,64,1024]{2,1,0:T(8,128)} %pick.1), calls=%async_computation.1 | async-start | bytes 4194304 | tf_op jit(solution)/shard_map/all_to_all | solution.py:639
  91.7 5.7 %copy-start.8 = (bf16[512,512]{1,0:T(8,128)(2,1)S(1)}, bf16[512,512]{1,0:T(8,128)(2,1)}, u32[]{:S(2)}) copy-start(bf16[512,512]{1,0:T(8,128)(2,1)} %get-tuple-element.22.gain_hi) | copy-start | bytes 1572868
  91.7 5.7 %copy-start.9 = (bf16[512,512]{1,0:T(8,128)(2,1)S(1)}, bf16[512,512]{1,0:T(8,128)(2,1)}, u32[]{:S(2)}) copy-start(bf16[512,512]{1,0:T(8,128)(2,1)} %get-tuple-element.23.gain_lo) | copy-start | bytes 1572868
  91.7 19.3 %all-to-all-start.2 = ((f32[8,256,128]{2,1,0:T(8,128)}), f32[8,256,128]{2,1,0:T(8,128)S(1)}, u32[]{:S(2)}, u32[]{:S(2)}) async-start(f32[8,256,128]{2,1,0:T(8,128)} %bitcast.34), calls=%async_computation.2 | async-start | bytes 2097152 | tf_op jit(solution)/shard_map/all_to_all | solution.py:639
  97.4 1.9 %copy-start.7 = (f32[3,1,1,512,512]{4,3,2,1,0:T(8,128)S(1)}, f32[3,1,1,512,512]{4,3,2,1,0:T(8,128)}, u32[]{:S(2)}) copy-start(f32[3,1,1,512,512]{4,3,2,1,0:T(8,128)} %param.8) | copy-start | bytes 9437188
